TPU v7x, 512 devices: a whole 4x8x8 slice. The times are simulated.
512 devices in a mesh: wide: 64 (over y, z_lo, x), narrow: 8 (over z_hi, core).
Axes of the slice: x: 4, y: 8, z: 8 (z_hi: 4, z_lo: 2; z = z_hi * 2 + z_lo), core: 2. Of those that a mesh axis runs over, the one named last changes fastest.
Arguments:
- pressure: float32 [128, 2048, 128], P('narrow', 'wide'), may hold values from -6 to 6
- saturation: float32 [128, 2048, 128], P('narrow', 'wide'), may hold values from 0.1 to 0.9
- source: float32 [128, 2048, 128], P('narrow', 'wide'), may hold values from -6 to 6
- permeability: float32 [3, 128, 2048, 128], P(None, 'narrow', 'wide'), may hold values from 0.1 to 10
- pore_volume: float32 [128, 2048, 128], P('narrow', 'wide'), may hold values from 0.5 to 2
- basis: bfloat16 [128, 2048, 4, 128], P('narrow', 'wide'), may hold values from 0 to 1
- support: int32 [128, 2048, 4], P('narrow', 'wide'), may hold values from 0 to 8, all different within a row
- coarse_matrix: float32 [9, 128, 2048], P(None, 'narrow', 'wide'), may hold values from -44.8 to 768, as said below
Outputs:
- new_pressure: float32 [128, 2048, 128], P('narrow', 'wide')
- new_saturation: float32 [128, 2048, 128], P('narrow', 'wide')
Inputs may be any that keep to these rules, and one draw needn't show every extreme that they name: `support`: the 4 codes of one column are distinct. `coarse_matrix`: entries at codes other than 4 are negative; the entry at code 4 exceeds the sum of magnitudes of the other eight of its block.
All inputs are finite; a program needn't handle non-finite values.
Results may differ from a plain program's by a relative error of at most 0.0003.
Values sent between devices are 32-bit elements; how exact they have to be, the bound alone decides.
No kernel may reach another device: no remote copies, remote signals or barrier semaphores. Data moves between devices by JAX's collectives and lax.ppermute only.
A program may use at most 64 MiB of HBM per device.

v0:
```python
import jax
import jax.numpy as jnp
from jax import lax
from jax.sharding import PartitionSpec as P

SWEEPS = 3


OFFSETS = [(o // 3 - 1, o % 3 - 1) for o in range(9)]
DIRECTIONS = [(1, 0, 0, 0), (-1, 0, 0, 0), (0, 1, 0, 1), (0, -1, 0, 1), (0, 0, 1, 2), (0, 0, -1, 2)]
OMEGA = 0.6667
DT = 0.01


def padded_2(array, sides, width):
    for axis, dim in sides:
        devices, length = (lax.axis_size(axis), array.shape[dim])
        up = [(i, (i + 1) % devices) for i in range(devices - 1)]
        down = [(j, i) for i, j in up]
        last = lax.slice_in_dim(array, length - width, length, axis=dim)
        leading = lax.slice_in_dim(array, 0, width, axis=dim)
        before = lax.ppermute(last, axis, up)
        after = lax.ppermute(leading, axis, down)
        array = jnp.concatenate([before, array, after], axis=dim)
    return array


def neighbour(padded, step_x, step_y, step_z, count_x, count_y):
    depth = padded.shape[2] - 2
    return padded[
        1 + step_x : 1 + step_x + count_x,
        1 + step_y : 1 + step_y + count_y,
        1 + step_z : 1 + step_z + depth,
    ]


def face_fluxes(pres_pad, perm_pads, count_x, count_y):
    centre = neighbour(pres_pad, 0, 0, 0, count_x, count_y)
    result = []
    for step_x, step_y, step_z, comp in DIRECTIONS:
        k_here = neighbour(perm_pads[comp], 0, 0, 0, count_x, count_y)
        k_there = neighbour(perm_pads[comp], step_x, step_y, step_z, count_x, count_y)
        trans = 2.0 * k_here * k_there / (k_here + k_there)
        result.append(
            trans * (centre - neighbour(pres_pad, step_x, step_y, step_z, count_x, count_y))
        )
    return result


def fraction(sat):
    return sat * sat / (sat * sat + 0.5 * (1.0 - sat) * (1.0 - sat))


def outflow(fluxes, sat_pad, count_x, count_y):
    centre = neighbour(sat_pad, 0, 0, 0, count_x, count_y)
    total = jnp.zeros_like(centre)
    for flux, (step_x, step_y, step_z, comp) in zip(fluxes, DIRECTIONS):
        other = neighbour(sat_pad, step_x, step_y, step_z, count_x, count_y)
        upwind = jnp.where(flux > 0, centre, other)
        total = total + flux * fraction(upwind)
    return total


def restrict_pieces(basis, support, residual):
    pieces = []
    for k in range(basis.shape[2]):
        pieces.append(jnp.sum(basis[:, :, k, :].astype(jnp.float32) * residual, axis=-1))
    binned = []
    for o in range(9):
        acc = jnp.zeros(residual.shape[:2], jnp.float32)
        for k in range(basis.shape[2]):
            acc = acc + jnp.where(support[:, :, k] == o, pieces[k], 0.0)
        binned.append(acc)
    return jnp.stack(binned)


def collect_pieces(binned_pad, count_x, count_y):
    total = jnp.zeros((count_x, count_y), jnp.float32)
    for o, (dx, dy) in enumerate(OFFSETS):
        total = total + binned_pad[o, 1 - dx : 1 - dx + count_x, 1 - dy : 1 - dy + count_y]
    return total


def apply_coarse(coarse_matrix, coarse_pad, count_x, count_y):
    total = jnp.zeros((count_x, count_y), jnp.float32)
    for o, (dx, dy) in enumerate(OFFSETS):
        total = (
            total
            + coarse_matrix[o] * coarse_pad[1 + dx : 1 + dx + count_x, 1 + dy : 1 + dy + count_y]
        )
    return total


def prolong(basis, support, coarse_pad, count_x, count_y):
    moved = [coarse_pad[1 + dx : 1 + dx + count_x, 1 + dy : 1 + dy + count_y] for dx, dy in OFFSETS]
    total = jnp.zeros(basis.shape[:2] + basis.shape[3:], jnp.float32)
    for k in range(basis.shape[2]):
        picked = jnp.zeros((count_x, count_y), jnp.float32)
        for o in range(9):
            picked = picked + jnp.where(support[:, :, k] == o, moved[o], 0.0)
        total = total + basis[:, :, k, :].astype(jnp.float32) * picked[:, :, None]
    return total


def coarse_padded(coarse):
    return padded_2(coarse, (("wide", 1), ("narrow", 0)), 1)


def pad_depth(field):
    return jnp.pad(field, ((0, 0), (0, 0), (1, 1)))


def on_device(
    pressure, saturation, source, permeability, pore_volume, basis, support, coarse_matrix
):
    count_x, count_y = (pressure.shape[0], pressure.shape[1])
    pres_pad, kx_pad, ky_pad, sat_pad = (
        padded_2(pressure, (("wide", 1), ("narrow", 0)), 1),
        padded_2(permeability[0], (("wide", 1), ("narrow", 0)), 1),
        padded_2(permeability[1], (("wide", 1), ("narrow", 0)), 1),
        padded_2(saturation, (("wide", 1), ("narrow", 0)), 1),
    )
    perm_pads = [pad_depth(kx_pad), pad_depth(ky_pad), jnp.pad(permeability[2], 1)]
    fluxes = face_fluxes(pad_depth(pres_pad), perm_pads, count_x, count_y)
    residual = source - sum(fluxes)
    binned = restrict_pieces(basis, support, residual)
    binned_pad = padded_2(binned, (("wide", 2), ("narrow", 1)), 1)
    coarse_residual = collect_pieces(binned_pad, count_x, count_y)
    diag = coarse_matrix[4]
    coarse = OMEGA * coarse_residual / diag
    for sweep in range(SWEEPS - 1):
        coarse = (
            coarse
            + OMEGA
            * (
                coarse_residual
                - apply_coarse(coarse_matrix, coarse_padded(coarse), count_x, count_y)
            )
            / diag
        )
    new_pressure = pressure + prolong(basis, support, coarse_padded(coarse), count_x, count_y)
    new_pad = padded_2(new_pressure, (("wide", 1), ("narrow", 0)), 1)
    new_fluxes = face_fluxes(pad_depth(new_pad), perm_pads, count_x, count_y)
    total = outflow(new_fluxes, pad_depth(sat_pad), count_x, count_y)
    new_saturation = saturation - DT * total / pore_volume
    return (new_pressure, new_saturation)


def solution(mesh):
    return jax.shard_map(
        on_device,
        mesh=mesh,
        in_specs=(
            P("narrow", "wide", None),
            P("narrow", "wide", None),
            P("narrow", "wide", None),
            P(None, "narrow", "wide", None),
            P("narrow", "wide", None),
            P("narrow", "wide", None, None),
            P("narrow", "wide", None),
            P(None, "narrow", "wide"),
        ),
        out_specs=(P("narrow", "wide", None), P("narrow", "wide", None)),
        check_vma=False,
    )
```

profile of v0, /device:TPU:161, one launch (start us, length us, event | category | flops | bytes accessed | tf_op | source)
XLA Modules:
  0.0 171.0 jit_solution(3860027851676128776)
XLA Ops:
  0.6 1.2 slice_bitcast_fusion.2
  1.9 3.1 %collective-permute-start = (f32[16,1,128]{2,1,0:T(1,128)S(1)}, f32[16,1,128]{2,1,0:T(1,128)S(1)}, u32[]{:S(2)}, u32[]{:S(2)}) collective-permute-start(f32[16,1,128]{2,1,0:T(1,128)S(1)} %get-tuple-element.72), channel_id=1, source_target_pairs={{0,8},{8,16},{16,24},{24,32},{32,40},{40,48},{48,56},{56,64},{64,7... | collective-permute-start | bytes 24584 | tf_op jit(solution)/shard_map/ppermute | solution.py:22
  5.0 6.4 %collective-permute-start.1 = (f32[16,1,128]{2,1,0:T(1,128)S(1)}, f32[16,1,128]{2,1,0:T(1,128)S(1)}, u32[]{:S(2)}, u32[]{:S(2)}) collective-permute-start(f32[16,1,128]{2,1,0:T(1,128)S(1)} %get-tuple-element.73), channel_id=1, source_target_pairs={{8,0},{16,8},{24,16},{32,24},{40,32},{48,40},{56,48},{64,56},{72,6... | collective-permute-start | bytes 24584 | tf_op jit(solution)/shard_map/ppermute | solution.py:23
  11.5 1.9 %collective-permute-start.3 = (f32[16,1,128]{2,1,0:T(1,128)S(1)}, f32[16,1,128]{2,1,0:T(1,128)S(1)}, u32[]{:S(2)}, u32[]{:S(2)}) collective-permute-start(f32[16,1,128]{2,1,0:T(1,128)S(1)} %get-tuple-element.76), channel_id=1, source_target_pairs={{0,8},{8,16},{16,24},{24,32},{32,40},{40,48},{48,56},{56,64},{64,7... | collective-permute-start | bytes 24584 | tf_op jit(solution)/shard_map/ppermute | solution.py:22
  13.4 7.6 %collective-permute-start.4 = (f32[16,1,128]{2,1,0:T(1,128)S(1)}, f32[16,1,128]{2,1,0:T(1,128)S(1)}, u32[]{:S(2)}, u32[]{:S(2)}) collective-permute-start(f32[16,1,128]{2,1,0:T(1,128)S(1)} %get-tuple-element.77), channel_id=1, source_target_pairs={{8,0},{16,8},{24,16},{32,24},{40,32},{48,40},{56,48},{64,56},{72,6... | collective-permute-start | bytes 24584 | tf_op jit(solution)/shard_map/ppermute | solution.py:23
  21.0 1.9 %collective-permute-start.8 = (f32[16,1,128]{2,1,0:T(1,128)S(1)}, f32[16,1,128]{2,1,0:T(1,128)S(1)}, u32[]{:S(2)}, u32[]{:S(2)}) collective-permute-start(f32[16,1,128]{2,1,0:T(1,128)S(1)} %get-tuple-element.75), channel_id=1, source_target_pairs={{8,0},{16,8},{24,16},{32,24},{40,32},{48,40},{56,48},{64,56},{72,6... | collective-permute-start | bytes 24584 | tf_op jit(solution)/shard_map/ppermute | solution.py:23
  22.9 1.1 fusion.128
  24.2 3.4 %collective-permute-start.9 = (f32[16,1,128]{2,1,0:T(1,128)S(1)}, f32[16,1,128]{2,1,0:T(1,128)S(1)}, u32[]{:S(2)}, u32[]{:S(2)}) collective-permute-start(f32[16,1,128]{2,1,0:T(1,128)S(1)} %get-tuple-element.74), channel_id=1, source_target_pairs={{0,8},{8,16},{16,24},{24,32},{32,40},{40,48},{48,56},{56,64},{64,7... | collective-permute-start | bytes 24584 | tf_op jit(solution)/shard_map/ppermute | solution.py:22
  27.6 4.3 %collective-permute-start.5 = (f32[1,34,128]{2,1,0:T(8,128)S(1)}, f32[1,34,128]{2,1,0:T(8,128)S(1)}, u32[]{:S(2)}, u32[]{:S(2)}) collective-permute-start(f32[1,34,128]{2,1,0:T(8,128)S(1)} %get-tuple-element.67), channel_id=1, source_target_pairs={{1,0},{2,1},{3,2},{4,3},{5,4},{6,5},{7,6},{9,8},{10,9},{11,10},{12... | collective-permute-start | bytes 52232 | tf_op jit(solution)/shard_map/ppermute | solution.py:23
  31.8 6.9 %collective-permute-start.7 = (f32[1,34,128]{2,1,0:T(8,128)S(1)}, f32[1,34,128]{2,1,0:T(8,128)S(1)}, u32[]{:S(2)}, u32[]{:S(2)}) collective-permute-start(f32[1,34,128]{2,1,0:T(8,128)S(1)} %get-tuple-element.66), channel_id=1, source_target_pairs={{0,1},{1,2},{2,3},{3,4},{4,5},{5,6},{6,7},{8,9},{9,10},{10,11},{11... | collective-permute-start | bytes 52232 | tf_op jit(solution)/shard_map/ppermute | solution.py:22
  38.8 1.9 %collective-permute-start.2 = (f32[1,34,128]{2,1,0:T(8,128)S(1)}, f32[1,34,128]{2,1,0:T(8,128)S(1)}, u32[]{:S(2)}, u32[]{:S(2)}) collective-permute-start(f32[1,34,128]{2,1,0:T(8,128)S(1)} %get-tuple-element.65), channel_id=1, source_target_pairs={{1,0},{2,1},{3,2},{4,3},{5,4},{6,5},{7,6},{9,8},{10,9},{11,10},{12... | collective-permute-start | bytes 52232 | tf_op jit(solution)/shard_map/ppermute | solution.py:23
  40.7 5.9 %collective-permute-start.6 = (f32[1,34,128]{2,1,0:T(8,128)S(1)}, f32[1,34,128]{2,1,0:T(8,128)S(1)}, u32[]{:S(2)}, u32[]{:S(2)}) collective-permute-start(f32[1,34,128]{2,1,0:T(8,128)S(1)} %get-tuple-element.64), channel_id=1, source_target_pairs={{0,1},{1,2},{2,3},{3,4},{4,5},{5,6},{6,7},{8,9},{9,10},{10,11},{11... | collective-permute-start | bytes 52232 | tf_op jit(solution)/shard_map/ppermute | solution.py:22
  46.6 0.3 select_maximum_fusion.8
  47.0 0.5 collective-permute-done.6
  47.5 0.9 fusion.1
  48.6 0.1 fusion.134
  48.7 1.9 %collective-permute-start.10 = (f32[9,16,1]{2,1,0:T(8,128)S(1)}, f32[9,16,1]{2,1,0:T(8,128)S(1)}, u32[]{:S(2)}, u32[]{:S(2)}) collective-permute-start(f32[9,16,1]{2,1,0:T(8,128)S(1)} %get-tuple-element.80), channel_id=1, source_target_pairs={{0,8},{8,16},{16,24},{24,32},{32,40},{40,48},{48,56},{56,64},{64,7... | collective-permute-start | bytes 1736 | tf_op jit(solution)/shard_map/ppermute | solution.py:22
  50.7 7.7 %collective-permute-start.11 = (f32[9,16,1]{2,1,0:T(8,128)S(1)}, f32[9,16,1]{2,1,0:T(8,128)S(1)}, u32[]{:S(2)}, u32[]{:S(2)}) collective-permute-start(f32[9,16,1]{2,1,0:T(8,128)S(1)} %get-tuple-element.81), channel_id=1, source_target_pairs={{8,0},{16,8},{24,16},{32,24},{40,32},{48,40},{56,48},{64,56},{72,6... | collective-permute-start | bytes 1736 | tf_op jit(solution)/shard_map/ppermute | solution.py:23
  58.4 1.4 collective-permute-done.11
  59.8 0.1 pad_maximum_fusion.63
  59.9 1.9 %collective-permute-start.12 = (f32[9,1,34]{2,1,0:T(1,128)S(1)}, f32[9,1,34]{2,1,0:T(1,128)S(1)}, u32[]{:S(2)}, u32[]{:S(2)}) collective-permute-start(f32[9,1,34]{2,1,0:T(1,128)S(1)} %get-tuple-element.78), channel_id=1, source_target_pairs={{1,0},{2,1},{3,2},{4,3},{5,4},{6,5},{7,6},{9,8},{10,9},{11,10},{12... | collective-permute-start | bytes 3680 | tf_op jit(solution)/shard_map/ppermute | solution.py:23
  61.8 7.5 %collective-permute-start.13 = (f32[9,1,34]{2,1,0:T(1,128)S(1)}, f32[9,1,34]{2,1,0:T(1,128)S(1)}, u32[]{:S(2)}, u32[]{:S(2)}) collective-permute-start(f32[9,1,34]{2,1,0:T(1,128)S(1)} %get-tuple-element.79), channel_id=1, source_target_pairs={{0,1},{1,2},{2,3},{3,4},{4,5},{5,6},{6,7},{8,9},{9,10},{10,11},{11... | collective-permute-start | bytes 3680 | tf_op jit(solution)/shard_map/ppermute | solution.py:22
  69.3 0.7 collective-permute-done.13
  70.0 0.1 bitcast_divide_fusion
  70.2 1.9 %collective-permute-start.14 = (f32[16,1]{1,0:T(8,128)S(1)}, f32[16,1]{1,0:T(8,128)S(1)}, u32[]{:S(2)}, u32[]{:S(2)}) collective-permute-start(f32[16,1]{1,0:T(8,128)S(1)} %get-tuple-element.102), channel_id=1, source_target_pairs={{0,8},{8,16},{16,24},{24,32},{32,40},{40,48},{48,56},{56,64},{64,7... | collective-permute-start | bytes 200 | tf_op jit(solution)/shard_map/ppermute | solution.py:22
  72.1 8.3 %collective-permute-start.15 = (f32[16,1]{1,0:T(8,128)S(1)}, f32[16,1]{1,0:T(8,128)S(1)}, u32[]{:S(2)}, u32[]{:S(2)}) collective-permute-start(f32[16,1]{1,0:T(8,128)S(1)} %get-tuple-element.103), channel_id=1, source_target_pairs={{8,0},{16,8},{24,16},{32,24},{40,32},{48,40},{56,48},{64,56},{72,6... | collective-permute-start | bytes 200 | tf_op jit(solution)/shard_map/ppermute | solution.py:23
  80.4 0.8 collective-permute-done.15
  81.3 7.1 %collective-permute-start.16 = (f32[1,34]{1,0:T(1,128)S(1)}, f32[1,34]{1,0:T(1,128)S(1)}, u32[]{:S(2)}, u32[]{:S(2)}) collective-permute-start(f32[1,34]{1,0:T(1,128)S(1)} %get-tuple-element.96), channel_id=1, source_target_pairs={{0,1},{1,2},{2,3},{3,4},{4,5},{5,6},{6,7},{8,9},{9,10},{10,11},{11... | collective-permute-start | bytes 416 | tf_op jit(solution)/shard_map/ppermute | solution.py:22
  88.4 1.9 %collective-permute-start.17 = (f32[1,34]{1,0:T(1,128)S(1)}, f32[1,34]{1,0:T(1,128)S(1)}, u32[]{:S(2)}, u32[]{:S(2)}) collective-permute-start(f32[1,34]{1,0:T(1,128)S(1)} %get-tuple-element.97), channel_id=1, source_target_pairs={{1,0},{2,1},{3,2},{4,3},{5,4},{6,5},{7,6},{9,8},{10,9},{11,10},{12... | collective-permute-start | bytes 416 | tf_op jit(solution)/shard_map/ppermute | solution.py:23
  90.4 5.0 %collective-permute-done.17 = f32[1,34]{1,0:T(1,128)S(1)} collective-permute-done((f32[1,34]{1,0:T(1,128)S(1)}, f32[1,34]{1,0:T(1,128)S(1)}, u32[]{:S(2)}, u32[]{:S(2)}) %collective-permute-start.17) | collective-permute-done | bytes 168 | tf_op jit(solution)/shard_map/ppermute | solution.py:23
  95.4 0.1 maximum_maximum_fusion
  95.5 0.1 fusion.80
  95.6 1.9 %collective-permute-start.18 = (f32[16,1]{1,0:T(8,128)S(1)}, f32[16,1]{1,0:T(8,128)S(1)}, u32[]{:S(2)}, u32[]{:S(2)}) collective-permute-start(f32[16,1]{1,0:T(8,128)S(1)} %get-tuple-element.100), channel_id=1, source_target_pairs={{0,8},{8,16},{16,24},{24,32},{32,40},{40,48},{48,56},{56,64},{64,7... | collective-permute-start | bytes 200 | tf_op jit(solution)/shard_map/ppermute | solution.py:22
  97.5 8.1 %collective-permute-start.19 = (f32[16,1]{1,0:T(8,128)S(1)}, f32[16,1]{1,0:T(8,128)S(1)}, u32[]{:S(2)}, u32[]{:S(2)}) collective-permute-start(f32[16,1]{1,0:T(8,128)S(1)} %get-tuple-element.101), channel_id=1, source_target_pairs={{8,0},{16,8},{24,16},{32,24},{40,32},{48,40},{56,48},{64,56},{72,6... | collective-permute-start | bytes 200 | tf_op jit(solution)/shard_map/ppermute | solution.py:23
  105.7 0.8 collective-permute-done.19
  106.5 0.1 pad_maximum_fusion.69
  106.5 2.8 %collective-permute-start.20 = (f32[1,34]{1,0:T(1,128)S(1)}, f32[1,34]{1,0:T(1,128)S(1)}, u32[]{:S(2)}, u32[]{:S(2)}) collective-permute-start(f32[1,34]{1,0:T(1,128)S(1)} %get-tuple-element.92), channel_id=1, source_target_pairs={{0,1},{1,2},{2,3},{3,4},{4,5},{5,6},{6,7},{8,9},{9,10},{10,11},{11... | collective-permute-start | bytes 416 | tf_op jit(solution)/shard_map/ppermute | solution.py:22
  109.4 1.9 %collective-permute-start.21 = (f32[1,34]{1,0:T(1,128)S(1)}, f32[1,34]{1,0:T(1,128)S(1)}, u32[]{:S(2)}, u32[]{:S(2)}) collective-permute-start(f32[1,34]{1,0:T(1,128)S(1)} %get-tuple-element.93), channel_id=1, source_target_pairs={{1,0},{2,1},{3,2},{4,3},{5,4},{6,5},{7,6},{9,8},{10,9},{11,10},{12... | collective-permute-start | bytes 416 | tf_op jit(solution)/shard_map/ppermute | solution.py:23
  111.3 1.9 %collective-permute-start.29 = (f32[16,1,128]{2,1,0:T(1,128)S(1)}, f32[16,1,128]{2,1,0:T(1,128)S(1)}, u32[]{:S(2)}, u32[]{:S(2)}) collective-permute-start(f32[16,1,128]{2,1,0:T(1,128)S(1)} %get-tuple-element.70), channel_id=1, source_target_pairs={{0,8},{8,16},{16,24},{24,32},{32,40},{40,48},{48,56},{56,64},{64,7... | collective-permute-start | bytes 24584 | tf_op jit(solution)/shard_map/ppermute | solution.py:22
  113.2 3.1 %collective-permute-done.21 = f32[1,34]{1,0:T(1,128)S(1)} collective-permute-done((f32[1,34]{1,0:T(1,128)S(1)}, f32[1,34]{1,0:T(1,128)S(1)}, u32[]{:S(2)}, u32[]{:S(2)}) %collective-permute-start.21) | collective-permute-done | bytes 168 | tf_op jit(solution)/shard_map/ppermute | solution.py:23
  116.3 0.1 maximum_maximum_fusion.1
  116.4 0.1 fusion.66
  116.6 1.9 %collective-permute-start.22 = (f32[16,1]{1,0:T(8,128)S(1)}, f32[16,1]{1,0:T(8,128)S(1)}, u32[]{:S(2)}, u32[]{:S(2)}) collective-permute-start(f32[16,1]{1,0:T(8,128)S(1)} %get-tuple-element.98), channel_id=1, source_target_pairs={{0,8},{8,16},{16,24},{24,32},{32,40},{40,48},{48,56},{56,64},{64,7... | collective-permute-start | bytes 200 | tf_op jit(solution)/shard_map/ppermute | solution.py:22
  118.5 8.1 %collective-permute-start.23 = (f32[16,1]{1,0:T(8,128)S(1)}, f32[16,1]{1,0:T(8,128)S(1)}, u32[]{:S(2)}, u32[]{:S(2)}) collective-permute-start(f32[16,1]{1,0:T(8,128)S(1)} %get-tuple-element.99), channel_id=1, source_target_pairs={{8,0},{16,8},{24,16},{32,24},{40,32},{48,40},{56,48},{64,56},{72,6... | collective-permute-start | bytes 200 | tf_op jit(solution)/shard_map/ppermute | solution.py:23
  126.7 0.8 collective-permute-done.23
  127.5 3.5 %collective-permute-start.24 = (f32[1,34]{1,0:T(1,128)S(1)}, f32[1,34]{1,0:T(1,128)S(1)}, u32[]{:S(2)}, u32[]{:S(2)}) collective-permute-start(f32[1,34]{1,0:T(1,128)S(1)} %get-tuple-element.88), channel_id=1, source_target_pairs={{0,1},{1,2},{2,3},{3,4},{4,5},{5,6},{6,7},{8,9},{9,10},{10,11},{11... | collective-permute-start | bytes 416 | tf_op jit(solution)/shard_map/ppermute | solution.py:22
  131.0 1.9 %collective-permute-start.25 = (f32[1,34]{1,0:T(1,128)S(1)}, f32[1,34]{1,0:T(1,128)S(1)}, u32[]{:S(2)}, u32[]{:S(2)}) collective-permute-start(f32[1,34]{1,0:T(1,128)S(1)} %get-tuple-element.89), channel_id=1, source_target_pairs={{1,0},{2,1},{3,2},{4,3},{5,4},{6,5},{7,6},{9,8},{10,9},{11,10},{12... | collective-permute-start | bytes 416 | tf_op jit(solution)/shard_map/ppermute | solution.py:23
  132.9 8.1 %collective-permute-start.30 = (f32[16,1,128]{2,1,0:T(1,128)S(1)}, f32[16,1,128]{2,1,0:T(1,128)S(1)}, u32[]{:S(2)}, u32[]{:S(2)}) collective-permute-start(f32[16,1,128]{2,1,0:T(1,128)S(1)} %get-tuple-element.71), channel_id=1, source_target_pairs={{8,0},{16,8},{24,16},{32,24},{40,32},{48,40},{56,48},{64,56},{72,6... | collective-permute-start | bytes 24584 | tf_op jit(solution)/shard_map/ppermute | solution.py:23
  141.1 0.1 maximum_maximum_fusion.2
  141.2 0.1 select_add_fusion.3
  141.3 0.1 select_add_fusion.2
  141.4 0.1 select_add_fusion.1
  141.5 0.1 select_add_fusion
  141.6 0.3 fusion.5
  141.9 1.9 %collective-permute-start.26 = (f32[16,1,128]{2,1,0:T(1,128)S(1)}, f32[16,1,128]{2,1,0:T(1,128)S(1)}, u32[]{:S(2)}, u32[]{:S(2)}) collective-permute-start(f32[16,1,128]{2,1,0:T(1,128)S(1)} %get-tuple-element.68), channel_id=1, source_target_pairs={{0,8},{8,16},{16,24},{24,32},{32,40},{40,48},{48,56},{56,64},{64,7... | collective-permute-start | bytes 24584 | tf_op jit(solution)/shard_map/ppermute | solution.py:22
  143.9 7.6 %collective-permute-start.27 = (f32[16,1,128]{2,1,0:T(1,128)S(1)}, f32[16,1,128]{2,1,0:T(1,128)S(1)}, u32[]{:S(2)}, u32[]{:S(2)}) collective-permute-start(f32[16,1,128]{2,1,0:T(1,128)S(1)} %get-tuple-element.69), channel_id=1, source_target_pairs={{8,0},{16,8},{24,16},{32,24},{40,32},{48,40},{56,48},{64,56},{72,6... | collective-permute-start | bytes 24584 | tf_op jit(solution)/shard_map/ppermute | solution.py:23
  151.5 1.9 %collective-permute-start.31 = (f32[1,34,128]{2,1,0:T(8,128)S(1)}, f32[1,34,128]{2,1,0:T(8,128)S(1)}, u32[]{:S(2)}, u32[]{:S(2)}) collective-permute-start(f32[1,34,128]{2,1,0:T(8,128)S(1)} %get-tuple-element.63), channel_id=1, source_target_pairs={{1,0},{2,1},{3,2},{4,3},{5,4},{6,5},{7,6},{9,8},{10,9},{11,10},{12... | collective-permute-start | bytes 52232 | tf_op jit(solution)/shard_map/ppermute | solution.py:23
  153.4 6.6 %collective-permute-start.33 = (f32[1,34,128]{2,1,0:T(8,128)S(1)}, f32[1,34,128]{2,1,0:T(8,128)S(1)}, u32[]{:S(2)}, u32[]{:S(2)}) collective-permute-start(f32[1,34,128]{2,1,0:T(8,128)S(1)} %get-tuple-element.62), channel_id=1, source_target_pairs={{0,1},{1,2},{2,3},{3,4},{4,5},{5,6},{6,7},{8,9},{9,10},{10,11},{11... | collective-permute-start | bytes 52232 | tf_op jit(solution)/shard_map/ppermute | solution.py:22
  160.1 1.9 %collective-permute-start.28 = (f32[1,34,128]{2,1,0:T(8,128)S(1)}, f32[1,34,128]{2,1,0:T(8,128)S(1)}, u32[]{:S(2)}, u32[]{:S(2)}) collective-permute-start(f32[1,34,128]{2,1,0:T(8,128)S(1)} %get-tuple-element.61), channel_id=1, source_target_pairs={{1,0},{2,1},{3,2},{4,3},{5,4},{6,5},{7,6},{9,8},{10,9},{11,10},{12... | collective-permute-start | bytes 52232 | tf_op jit(solution)/shard_map/ppermute | solution.py:23
  162.0 5.8 %collective-permute-start.32 = (f32[1,34,128]{2,1,0:T(8,128)S(1)}, f32[1,34,128]{2,1,0:T(8,128)S(1)}, u32[]{:S(2)}, u32[]{:S(2)}) collective-permute-start(f32[1,34,128]{2,1,0:T(8,128)S(1)} %get-tuple-element.60), channel_id=1, source_target_pairs={{0,1},{1,2},{2,3},{3,4},{4,5},{5,6},{6,7},{8,9},{9,10},{10,11},{11... | collective-permute-start | bytes 52232 | tf_op jit(solution)/shard_map/ppermute | solution.py:22
  167.8 0.3 select_maximum_fusion
  168.1 0.5 collective-permute-done.32
  168.6 0.3 select_maximum_fusion.4
  169.1 1.9 %divide_subtract_fusion = f32[16,32,128]{2,1,0:T(8,128)} fusion(f32[16,32,128]{2,1,0:T(8,128)S(1)} %copy-done.2, f32[16,32,128]{2,1,0:T(8,128)S(1)} %copy-done.6, f32[18,34,130]{2,1,0:T(8,128)S(1)} %select_maximum_fusion, f32[16,1,128]{2,1,0:T(1,128)S(1)} %collective-permute-done.29, f32[16,1,128]{2,1,0:T(1,128)S(1)} %collective-permute-done.30, ...), kind=kLoop, calls=%fused_computation.136 | loop fusion | flops 7798784 | bytes 3053568 | tf_op jit(solution)/shard_map/sub | solution.py:145
  (65 shorter events, 0.8 us)
Async XLA Ops:
  0.6 10.8 %copy-start = (f32[16,32,128]{2,1,0:T(8,128)S(1)}, f32[16,32,128]{2,1,0:T(8,128)}, u32[]{:S(2)}) copy-start(f32[16,32,128]{2,1,0:T(8,128)} %param.8) | copy-start | bytes 786436
  0.6 22.3 %copy-start.3 = (bf16[16,32,4,128]{3,2,1,0:T(4,128)(2,1)S(1)}, bf16[16,32,4,128]{3,2,1,0:T(4,128)(2,1)}, u32[]{:S(2)}) copy-start(bf16[16,32,4,128]{3,2,1,0:T(4,128)(2,1)} %param.13) | copy-start | bytes 1572868
  1.9 29.9 %collective-permute-start = (f32[16,1,128]{2,1,0:T(1,128)S(1)}, f32[16,1,128]{2,1,0:T(1,128)S(1)}, u32[]{:S(2)}, u32[]{:S(2)}) collective-permute-start(f32[16,1,128]{2,1,0:T(1,128)S(1)} %get-tuple-element.72), channel_id=1, source_target_pairs={{0,8},{8,16},{16,24},{24,32},{32,40},{40,48},{48,56},{56,64},{64,7... | collective-permute-start | bytes 24584 | tf_op jit(solution)/shard_map/ppermute | solution.py:22
  5.0 33.7 %collective-permute-start.1 = (f32[16,1,128]{2,1,0:T(1,128)S(1)}, f32[16,1,128]{2,1,0:T(1,128)S(1)}, u32[]{:S(2)}, u32[]{:S(2)}) collective-permute-start(f32[16,1,128]{2,1,0:T(1,128)S(1)} %get-tuple-element.73), channel_id=1, source_target_pairs={{8,0},{16,8},{24,16},{32,24},{40,32},{48,40},{56,48},{64,56},{72,6... | collective-permute-start | bytes 24584 | tf_op jit(solution)/shard_map/ppermute | solution.py:23
  11.5 12.7 %collective-permute-start.3 = (f32[16,1,128]{2,1,0:T(1,128)S(1)}, f32[16,1,128]{2,1,0:T(1,128)S(1)}, u32[]{:S(2)}, u32[]{:S(2)}) collective-permute-start(f32[16,1,128]{2,1,0:T(1,128)S(1)} %get-tuple-element.76), channel_id=1, source_target_pairs={{0,8},{8,16},{16,24},{24,32},{32,40},{40,48},{48,56},{56,64},{64,7... | collective-permute-start | bytes 24584 | tf_op jit(solution)/shard_map/ppermute | solution.py:22
  13.4 14.1 %collective-permute-start.4 = (f32[16,1,128]{2,1,0:T(1,128)S(1)}, f32[16,1,128]{2,1,0:T(1,128)S(1)}, u32[]{:S(2)}, u32[]{:S(2)}) collective-permute-start(f32[16,1,128]{2,1,0:T(1,128)S(1)} %get-tuple-element.77), channel_id=1, source_target_pairs={{8,0},{16,8},{24,16},{32,24},{40,32},{48,40},{56,48},{64,56},{72,6... | collective-permute-start | bytes 24584 | tf_op jit(solution)/shard_map/ppermute | solution.py:23
  21.0 3.1 %copy-start.7 = (s32[16,32,4]{1,2,0:T(4,128)S(1)}, s32[16,32,4]{1,2,0:T(4,128)}, u32[]{:S(2)}) copy-start(s32[16,32,4]{1,2,0:T(4,128)} %param.14) | copy-start | bytes 24580
  21.0 26.0 %collective-permute-start.8 = (f32[16,1,128]{2,1,0:T(1,128)S(1)}, f32[16,1,128]{2,1,0:T(1,128)S(1)}, u32[]{:S(2)}, u32[]{:S(2)}) collective-permute-start(f32[16,1,128]{2,1,0:T(1,128)S(1)} %get-tuple-element.75), channel_id=1, source_target_pairs={{8,0},{16,8},{24,16},{32,24},{40,32},{48,40},{56,48},{64,56},{72,6... | collective-permute-start | bytes 24584 | tf_op jit(solution)/shard_map/ppermute | solution.py:23
  24.2 22.8 %collective-permute-start.9 = (f32[16,1,128]{2,1,0:T(1,128)S(1)}, f32[16,1,128]{2,1,0:T(1,128)S(1)}, u32[]{:S(2)}, u32[]{:S(2)}) collective-permute-start(f32[16,1,128]{2,1,0:T(1,128)S(1)} %get-tuple-element.74), channel_id=1, source_target_pairs={{0,8},{8,16},{16,24},{24,32},{32,40},{40,48},{48,56},{56,64},{64,7... | collective-permute-start | bytes 24584 | tf_op jit(solution)/shard_map/ppermute | solution.py:22
  27.6 13.2 %collective-permute-start.5 = (f32[1,34,128]{2,1,0:T(8,128)S(1)}, f32[1,34,128]{2,1,0:T(8,128)S(1)}, u32[]{:S(2)}, u32[]{:S(2)}) collective-permute-start(f32[1,34,128]{2,1,0:T(8,128)S(1)} %get-tuple-element.67), channel_id=1, source_target_pairs={{1,0},{2,1},{3,2},{4,3},{5,4},{6,5},{7,6},{9,8},{10,9},{11,10},{12... | collective-permute-start | bytes 52232 | tf_op jit(solution)/shard_map/ppermute | solution.py:23
  31.8 14.8 %collective-permute-start.7 = (f32[1,34,128]{2,1,0:T(8,128)S(1)}, f32[1,34,128]{2,1,0:T(8,128)S(1)}, u32[]{:S(2)}, u32[]{:S(2)}) collective-permute-start(f32[1,34,128]{2,1,0:T(8,128)S(1)} %get-tuple-element.66), channel_id=1, source_target_pairs={{0,1},{1,2},{2,3},{3,4},{4,5},{5,6},{6,7},{8,9},{9,10},{10,11},{11... | collective-permute-start | bytes 52232 | tf_op jit(solution)/shard_map/ppermute | solution.py:22
  38.8 8.2 %collective-permute-start.2 = (f32[1,34,128]{2,1,0:T(8,128)S(1)}, f32[1,34,128]{2,1,0:T(8,128)S(1)}, u32[]{:S(2)}, u32[]{:S(2)}) collective-permute-start(f32[1,34,128]{2,1,0:T(8,128)S(1)} %get-tuple-element.65), channel_id=1, source_target_pairs={{1,0},{2,1},{3,2},{4,3},{5,4},{6,5},{7,6},{9,8},{10,9},{11,10},{12... | collective-permute-start | bytes 52232 | tf_op jit(solution)/shard_map/ppermute | solution.py:23
  40.7 6.8 %copy-start.5 = (f32[16,32,128]{2,1,0:T(8,128)S(1)}, f32[16,32,128]{2,1,0:T(8,128)}, u32[]{:S(2)}) copy-start(f32[16,32,128]{2,1,0:T(8,128)} %param.10) | copy-start | bytes 786436
  40.7 6.8 %collective-permute-start.6 = (f32[1,34,128]{2,1,0:T(8,128)S(1)}, f32[1,34,128]{2,1,0:T(8,128)S(1)}, u32[]{:S(2)}, u32[]{:S(2)}) collective-permute-start(f32[1,34,128]{2,1,0:T(8,128)S(1)} %get-tuple-element.64), channel_id=1, source_target_pairs={{0,1},{1,2},{2,3},{3,4},{4,5},{5,6},{6,7},{8,9},{9,10},{10,11},{11... | collective-permute-start | bytes 52232 | tf_op jit(solution)/shard_map/ppermute | solution.py:22
  48.7 9.7 %collective-permute-start.10 = (f32[9,16,1]{2,1,0:T(8,128)S(1)}, f32[9,16,1]{2,1,0:T(8,128)S(1)}, u32[]{:S(2)}, u32[]{:S(2)}) collective-permute-start(f32[9,16,1]{2,1,0:T(8,128)S(1)} %get-tuple-element.80), channel_id=1, source_target_pairs={{0,8},{8,16},{16,24},{24,32},{32,40},{40,48},{48,56},{56,64},{64,7... | collective-permute-start | bytes 1736 | tf_op jit(solution)/shard_map/ppermute | solution.py:22
  50.6 19.4 %copy-start.4 = (f32[9,16,32]{2,1,0:T(8,128)S(1)}, f32[9,16,32]{2,1,0:T(8,128)}, u32[]{:S(2)}) copy-start(f32[9,16,32]{2,1,0:T(8,128)} %param.15) | copy-start | bytes 55300
  50.7 39.7 %copy-start.2 = (f32[16,32,128]{2,1,0:T(8,128)S(1)}, f32[16,32,128]{2,1,0:T(8,128)}, u32[]{:S(2)}) copy-start(f32[16,32,128]{2,1,0:T(8,128)} %param.9) | copy-start | bytes 786436
  50.7 9.1 %collective-permute-start.11 = (f32[9,16,1]{2,1,0:T(8,128)S(1)}, f32[9,16,1]{2,1,0:T(8,128)S(1)}, u32[]{:S(2)}, u32[]{:S(2)}) collective-permute-start(f32[9,16,1]{2,1,0:T(8,128)S(1)} %get-tuple-element.81), channel_id=1, source_target_pairs={{8,0},{16,8},{24,16},{32,24},{40,32},{48,40},{56,48},{64,56},{72,6... | collective-permute-start | bytes 1736 | tf_op jit(solution)/shard_map/ppermute | solution.py:23
  59.9 9.4 %collective-permute-start.12 = (f32[9,1,34]{2,1,0:T(1,128)S(1)}, f32[9,1,34]{2,1,0:T(1,128)S(1)}, u32[]{:S(2)}, u32[]{:S(2)}) collective-permute-start(f32[9,1,34]{2,1,0:T(1,128)S(1)} %get-tuple-element.78), channel_id=1, source_target_pairs={{1,0},{2,1},{3,2},{4,3},{5,4},{6,5},{7,6},{9,8},{10,9},{11,10},{12... | collective-permute-start | bytes 3680 | tf_op jit(solution)/shard_map/ppermute | solution.py:23
  61.8 8.2 %collective-permute-start.13 = (f32[9,1,34]{2,1,0:T(1,128)S(1)}, f32[9,1,34]{2,1,0:T(1,128)S(1)}, u32[]{:S(2)}, u32[]{:S(2)}) collective-permute-start(f32[9,1,34]{2,1,0:T(1,128)S(1)} %get-tuple-element.79), channel_id=1, source_target_pairs={{0,1},{1,2},{2,3},{3,4},{4,5},{5,6},{6,7},{8,9},{9,10},{10,11},{11... | collective-permute-start | bytes 3680 | tf_op jit(solution)/shard_map/ppermute | solution.py:22
  70.2 10.2 %collective-permute-start.14 = (f32[16,1]{1,0:T(8,128)S(1)}, f32[16,1]{1,0:T(8,128)S(1)}, u32[]{:S(2)}, u32[]{:S(2)}) collective-permute-start(f32[16,1]{1,0:T(8,128)S(1)} %get-tuple-element.102), channel_id=1, source_target_pairs={{0,8},{8,16},{16,24},{24,32},{32,40},{40,48},{48,56},{56,64},{64,7... | collective-permute-start | bytes 200 | tf_op jit(solution)/shard_map/ppermute | solution.py:22
  72.1 9.0 %collective-permute-start.15 = (f32[16,1]{1,0:T(8,128)S(1)}, f32[16,1]{1,0:T(8,128)S(1)}, u32[]{:S(2)}, u32[]{:S(2)}) collective-permute-start(f32[16,1]{1,0:T(8,128)S(1)} %get-tuple-element.103), channel_id=1, source_target_pairs={{8,0},{16,8},{24,16},{32,24},{40,32},{48,40},{56,48},{64,56},{72,6... | collective-permute-start | bytes 200 | tf_op jit(solution)/shard_map/ppermute | solution.py:23
  81.3 9.1 %collective-permute-start.16 = (f32[1,34]{1,0:T(1,128)S(1)}, f32[1,34]{1,0:T(1,128)S(1)}, u32[]{:S(2)}, u32[]{:S(2)}) collective-permute-start(f32[1,34]{1,0:T(1,128)S(1)} %get-tuple-element.96), channel_id=1, source_target_pairs={{0,1},{1,2},{2,3},{3,4},{4,5},{5,6},{6,7},{8,9},{9,10},{10,11},{11... | collective-permute-start | bytes 416 | tf_op jit(solution)/shard_map/ppermute | solution.py:22
  88.4 7.0 %collective-permute-start.17 = (f32[1,34]{1,0:T(1,128)S(1)}, f32[1,34]{1,0:T(1,128)S(1)}, u32[]{:S(2)}, u32[]{:S(2)}) collective-permute-start(f32[1,34]{1,0:T(1,128)S(1)} %get-tuple-element.97), channel_id=1, source_target_pairs={{1,0},{2,1},{3,2},{4,3},{5,4},{6,5},{7,6},{9,8},{10,9},{11,10},{12... | collective-permute-start | bytes 416 | tf_op jit(solution)/shard_map/ppermute | solution.py:23
  95.6 10.1 %collective-permute-start.18 = (f32[16,1]{1,0:T(8,128)S(1)}, f32[16,1]{1,0:T(8,128)S(1)}, u32[]{:S(2)}, u32[]{:S(2)}) collective-permute-start(f32[16,1]{1,0:T(8,128)S(1)} %get-tuple-element.100), channel_id=1, source_target_pairs={{0,8},{8,16},{16,24},{24,32},{32,40},{40,48},{48,56},{56,64},{64,7... | collective-permute-start | bytes 200 | tf_op jit(solution)/shard_map/ppermute | solution.py:22
  97.5 8.9 %collective-permute-start.19 = (f32[16,1]{1,0:T(8,128)S(1)}, f32[16,1]{1,0:T(8,128)S(1)}, u32[]{:S(2)}, u32[]{:S(2)}) collective-permute-start(f32[16,1]{1,0:T(8,128)S(1)} %get-tuple-element.101), channel_id=1, source_target_pairs={{8,0},{16,8},{24,16},{32,24},{40,32},{48,40},{56,48},{64,56},{72,6... | collective-permute-start | bytes 200 | tf_op jit(solution)/shard_map/ppermute | solution.py:23
  106.5 6.7 %collective-permute-start.20 = (f32[1,34]{1,0:T(1,128)S(1)}, f32[1,34]{1,0:T(1,128)S(1)}, u32[]{:S(2)}, u32[]{:S(2)}) collective-permute-start(f32[1,34]{1,0:T(1,128)S(1)} %get-tuple-element.92), channel_id=1, source_target_pairs={{0,1},{1,2},{2,3},{3,4},{4,5},{5,6},{6,7},{8,9},{9,10},{10,11},{11... | collective-permute-start | bytes 416 | tf_op jit(solution)/shard_map/ppermute | solution.py:22
  109.4 7.0 %collective-permute-start.21 = (f32[1,34]{1,0:T(1,128)S(1)}, f32[1,34]{1,0:T(1,128)S(1)}, u32[]{:S(2)}, u32[]{:S(2)}) collective-permute-start(f32[1,34]{1,0:T(1,128)S(1)} %get-tuple-element.93), channel_id=1, source_target_pairs={{1,0},{2,1},{3,2},{4,3},{5,4},{6,5},{7,6},{9,8},{10,9},{11,10},{12... | collective-permute-start | bytes 416 | tf_op jit(solution)/shard_map/ppermute | solution.py:23
  111.3 40.2 %collective-permute-start.29 = (f32[16,1,128]{2,1,0:T(1,128)S(1)}, f32[16,1,128]{2,1,0:T(1,128)S(1)}, u32[]{:S(2)}, u32[]{:S(2)}) collective-permute-start(f32[16,1,128]{2,1,0:T(1,128)S(1)} %get-tuple-element.70), channel_id=1, source_target_pairs={{0,8},{8,16},{16,24},{24,32},{32,40},{40,48},{48,56},{56,64},{64,7... | collective-permute-start | bytes 24584 | tf_op jit(solution)/shard_map/ppermute | solution.py:22
  116.6 10.1 %collective-permute-start.22 = (f32[16,1]{1,0:T(8,128)S(1)}, f32[16,1]{1,0:T(8,128)S(1)}, u32[]{:S(2)}, u32[]{:S(2)}) collective-permute-start(f32[16,1]{1,0:T(8,128)S(1)} %get-tuple-element.98), channel_id=1, source_target_pairs={{0,8},{8,16},{16,24},{24,32},{32,40},{40,48},{48,56},{56,64},{64,7... | collective-permute-start | bytes 200 | tf_op jit(solution)/shard_map/ppermute | solution.py:22
  118.5 8.9 %collective-permute-start.23 = (f32[16,1]{1,0:T(8,128)S(1)}, f32[16,1]{1,0:T(8,128)S(1)}, u32[]{:S(2)}, u32[]{:S(2)}) collective-permute-start(f32[16,1]{1,0:T(8,128)S(1)} %get-tuple-element.99), channel_id=1, source_target_pairs={{8,0},{16,8},{24,16},{32,24},{40,32},{48,40},{56,48},{64,56},{72,6... | collective-permute-start | bytes 200 | tf_op jit(solution)/shard_map/ppermute | solution.py:23
  127.5 13.6 %collective-permute-start.24 = (f32[1,34]{1,0:T(1,128)S(1)}, f32[1,34]{1,0:T(1,128)S(1)}, u32[]{:S(2)}, u32[]{:S(2)}) collective-permute-start(f32[1,34]{1,0:T(1,128)S(1)} %get-tuple-element.88), channel_id=1, source_target_pairs={{0,1},{1,2},{2,3},{3,4},{4,5},{5,6},{6,7},{8,9},{9,10},{10,11},{11... | collective-permute-start | bytes 416 | tf_op jit(solution)/shard_map/ppermute | solution.py:22
  131.0 10.1 %collective-permute-start.25 = (f32[1,34]{1,0:T(1,128)S(1)}, f32[1,34]{1,0:T(1,128)S(1)}, u32[]{:S(2)}, u32[]{:S(2)}) collective-permute-start(f32[1,34]{1,0:T(1,128)S(1)} %get-tuple-element.89), channel_id=1, source_target_pairs={{1,0},{2,1},{3,2},{4,3},{5,4},{6,5},{7,6},{9,8},{10,9},{11,10},{12... | collective-permute-start | bytes 416 | tf_op jit(solution)/shard_map/ppermute | solution.py:23
  132.9 18.5 %collective-permute-start.30 = (f32[16,1,128]{2,1,0:T(1,128)S(1)}, f32[16,1,128]{2,1,0:T(1,128)S(1)}, u32[]{:S(2)}, u32[]{:S(2)}) collective-permute-start(f32[16,1,128]{2,1,0:T(1,128)S(1)} %get-tuple-element.71), channel_id=1, source_target_pairs={{8,0},{16,8},{24,16},{32,24},{40,32},{48,40},{56,48},{64,56},{72,6... | collective-permute-start | bytes 24584 | tf_op jit(solution)/shard_map/ppermute | solution.py:23
  141.9 27.1 %copy-start.1 = (f32[16,32,128]{2,1,0:T(8,128)}, f32[16,32,128]{2,1,0:T(8,128)S(1)}, u32[]{:S(2)}) copy-start(f32[16,32,128]{2,1,0:T(8,128)S(1)} %fusion.5) | copy-start | bytes 786436
  141.9 18.1 %collective-permute-start.26 = (f32[16,1,128]{2,1,0:T(1,128)S(1)}, f32[16,1,128]{2,1,0:T(1,128)S(1)}, u32[]{:S(2)}, u32[]{:S(2)}) collective-permute-start(f32[16,1,128]{2,1,0:T(1,128)S(1)} %get-tuple-element.68), channel_id=1, source_target_pairs={{0,8},{8,16},{16,24},{24,32},{32,40},{40,48},{48,56},{56,64},{64,7... | collective-permute-start | bytes 24584 | tf_op jit(solution)/shard_map/ppermute | solution.py:22
  143.9 16.2 %collective-permute-start.27 = (f32[16,1,128]{2,1,0:T(1,128)S(1)}, f32[16,1,128]{2,1,0:T(1,128)S(1)}, u32[]{:S(2)}, u32[]{:S(2)}) collective-permute-start(f32[16,1,128]{2,1,0:T(1,128)S(1)} %get-tuple-element.69), channel_id=1, source_target_pairs={{8,0},{16,8},{24,16},{32,24},{40,32},{48,40},{56,48},{64,56},{72,6... | collective-permute-start | bytes 24584 | tf_op jit(solution)/shard_map/ppermute | solution.py:23
  151.5 16.3 %collective-permute-start.31 = (f32[1,34,128]{2,1,0:T(8,128)S(1)}, f32[1,34,128]{2,1,0:T(8,128)S(1)}, u32[]{:S(2)}, u32[]{:S(2)}) collective-permute-start(f32[1,34,128]{2,1,0:T(8,128)S(1)} %get-tuple-element.63), channel_id=1, source_target_pairs={{1,0},{2,1},{3,2},{4,3},{5,4},{6,5},{7,6},{9,8},{10,9},{11,10},{12... | collective-permute-start | bytes 52232 | tf_op jit(solution)/shard_map/ppermute | solution.py:23
  153.4 14.3 %collective-permute-start.33 = (f32[1,34,128]{2,1,0:T(8,128)S(1)}, f32[1,34,128]{2,1,0:T(8,128)S(1)}, u32[]{:S(2)}, u32[]{:S(2)}) collective-permute-start(f32[1,34,128]{2,1,0:T(8,128)S(1)} %get-tuple-element.62), channel_id=1, source_target_pairs={{0,1},{1,2},{2,3},{3,4},{4,5},{5,6},{6,7},{8,9},{9,10},{10,11},{11... | collective-permute-start | bytes 52232 | tf_op jit(solution)/shard_map/ppermute | solution.py:22
  160.1 8.1 %collective-permute-start.28 = (f32[1,34,128]{2,1,0:T(8,128)S(1)}, f32[1,34,128]{2,1,0:T(8,128)S(1)}, u32[]{:S(2)}, u32[]{:S(2)}) collective-permute-start(f32[1,34,128]{2,1,0:T(8,128)S(1)} %get-tuple-element.61), channel_id=1, source_target_pairs={{1,0},{2,1},{3,2},{4,3},{5,4},{6,5},{7,6},{9,8},{10,9},{11,10},{12... | collective-permute-start | bytes 52232 | tf_op jit(solution)/shard_map/ppermute | solution.py:23
  162.0 6.6 %collective-permute-start.32 = (f32[1,34,128]{2,1,0:T(8,128)S(1)}, f32[1,34,128]{2,1,0:T(8,128)S(1)}, u32[]{:S(2)}, u32[]{:S(2)}) collective-permute-start(f32[1,34,128]{2,1,0:T(8,128)S(1)} %get-tuple-element.60), channel_id=1, source_target_pairs={{0,1},{1,2},{2,3},{3,4},{4,5},{5,6},{6,7},{8,9},{9,10},{10,11},{11... | collective-permute-start | bytes 52232 | tf_op jit(solution)/shard_map/ppermute | solution.py:22
  168.1 1.0 copy-start.6
where the time goes:
time: 172 us; the launch traced here: 171 us
  starting transfers between devices  148 us (86%)
  waiting for transfers between devices  13.6 us (8%)
  other arithmetic  5.59 us (3%)
  local copies, waits for them, and re-layouts  2.9 us (2%)
    ppermute x17, starting transfers between devices, padded_2(): after = lax.ppermute(leading, axis, down)  81.5 us
    ppermute x17, starting transfers between devices, padded_2(): before = lax.ppermute(last, axis, up)  66 us
    ppermute x17, waiting for transfers between devices, padded_2(): after = lax.ppermute(leading, axis, down)  11.8 us
  transfers between devices with their start and end apart: 34, of which 9 were waited for; matrix products, arithmetic and copies ran while one was open for 2% of the time, Pallas kernels for 0%

commit v1 on v0

v1 whole, which is shorter than its diff:
```python
import jax
import jax.numpy as jnp
from jax import lax
from jax.experimental import pallas as pl
from jax.experimental.pallas import tpu as pltpu
from jax.sharding import PartitionSpec as P

SWEEPS = 3
OFFSETS = [(o // 3 - 1, o % 3 - 1) for o in range(9)]
OMEGA = 0.6667
DT = 0.01

NX, NY, L, K = 16, 32, 128, 4
TOP, WEST, TALL = 8, 4, 32
EDGE = 5
FIELDS = 2 + K
SUP, MAT, ACC = 0, K, K + 9
SMALL = K + 10
N_P, N_K, N_S, N_B, N_C = 0, 32, 64, 96, 224
N_SMALL = 288
N_ROWS = N_SMALL + 8 * 5
W_SAT = FIELDS * TALL
W_SMALL = W_SAT + NX
W_ROWS = W_SMALL + TALL


def roll(a, shift, axis):
    shift %= a.shape[axis]
    return pltpu.roll(a, shift, axis) if shift else a


def iota(shape, axis):
    return lax.broadcasted_iota(jnp.int32, shape, axis)


def trans_of(here, there):
    return 2.0 * here * there / (here + there)


def fraction(sat):
    rest = 1.0 - sat
    square = sat * sat
    return square / (square + 0.5 * (rest * rest))


def lane_sum(a):
    return jnp.sum(a, axis=-1, keepdims=True)


def bin_pieces(sup, pieces):
    total = None
    for dy in (-1, 0, 1):
        column = None
        for dx in (-1, 0, 1):
            code = float((dx + 1) * 3 + dy + 1)
            part = None
            for k in range(K):
                term = jnp.where(sup[k] == code, pieces[k], 0.0)
                part = term if part is None else part + term
            part = roll(part, dx, 0)
            column = part if column is None else column + part
        column = roll(column, dy, 1)
        total = column if total is None else total + column
    return total


def turned(scratch, value):
    scratch[...] = jnp.zeros((L, L), jnp.float32)
    scratch[WEST : WEST + NY, :] = value
    return scratch[...].T


def residual_kernel(
    p, sat, src, perm, basis, support, matrix, out_even, out_odd, small, bs, place, square
):
    even = lax.axis_index("narrow") % 2 == 0
    lanes = iota((NY, L), 1)
    rows = iota((NY, L), 0)
    cells = NX * NY
    div = [None] * NX
    last_x = None
    for x in range(NX):
        at = slice(x * NY, (x + 1) * NY)
        here = p[at, :]
        kx, ky, kz = (perm[c * cells + x * NY : c * cells + (x + 1) * NY, :] for c in range(3))
        fy = trans_of(ky, roll(ky, -1, 0)) * (here - roll(here, -1, 0))
        fy = jnp.where(rows < NY - 1, fy, 0.0)
        fz = trans_of(kz, roll(kz, -1, 1)) * (here - roll(here, -1, 1))
        fz = jnp.where(lanes < L - 1, fz, 0.0)
        total = (fy - roll(fy, 1, 0)) + (fz - roll(fz, 1, 1))
        if x < NX - 1:
            fx = trans_of(kx, perm[(x + 1) * NY : (x + 2) * NY, :]) * (here - p[(x + 1) * NY : (x + 2) * NY, :])
            total = total + fx
        if last_x is not None:
            total = total - last_x
        last_x = fx
        div[x] = total
    pieces = jnp.zeros((NY, L), jnp.float32)
    for x in range(NX):
        at = slice(x * NY * K, (x + 1) * NY * K)
        bs[at, :] = basis[at, :].astype(jnp.float32)
        res = src[x * NY : (x + 1) * NY, :] - div[x]
        for k in range(K):
            b = bs[pl.ds(x * NY * K + k, NY, stride=K), :]
            pieces = jnp.where(lanes == k * TALL + TOP + x, lane_sum(b * res), pieces)
    flipped = turned(square, pieces)
    place[...] = jnp.zeros((TALL, L), jnp.float32)
    stack = []
    for i in range(K + 9):
        if i < MAT:
            value = support[pl.ds(i, NX, stride=K), :].astype(jnp.float32)
        else:
            value = matrix[(i - MAT) * NX : (i - MAT + 1) * NX, :]
        place[TOP : TOP + NX, 0:NY] = value
        stack.append(roll(place[...], WEST, 1))
    acc = bin_pieces(stack[:K], [flipped[k * TALL : (k + 1) * TALL, :] for k in range(K)])
    stack.append(acc)
    for i in range(SMALL):
        small[i * TALL : (i + 1) * TALL, :] = stack[i]
    for out, takes_last in ((out_even, even), (out_odd, jnp.logical_not(even))):
        edge = jnp.where(takes_last, NX - 1, 0)
        row = pl.multiple_of(edge * NY, NY)
        out[N_P : N_P + NY, :] = p[pl.ds(row, NY), :]
        out[N_K : N_K + NY, :] = perm[pl.ds(row, NY), :]
        out[N_S : N_S + NY, :] = sat[pl.ds(row, NY), :]
        for k in range(K):
            out[N_B + k * NY : N_B + (k + 1) * NY, :] = bs[pl.ds(row * K + k, NY, stride=K), :]
        start = jnp.where(takes_last, NX - EDGE, 0) * NY
        for c, col in enumerate((0, NY - 1)):
            fields = [
                p[pl.ds(start + col, EDGE, stride=NY), :],
                perm[pl.ds(start + (cells + col), EDGE, stride=NY), :],
            ] + [bs[pl.ds((start + col) * K + k, EDGE, stride=NY * K), :] for k in range(K)]
            for f, value in enumerate(fields):
                to = N_C + (f * 2 + c) * EDGE
                out[to : to + EDGE, :] = value
        window = [jnp.where(takes_last, s[16:24, :], s[8:16, :]) for s in stack]
        window.append(jnp.where(takes_last, acc[24:32, :], acc[0:8, :]))
        for i in range(5):
            a, b, c = window[3 * i : 3 * i + 3]
            out[N_SMALL + 8 * i : N_SMALL + 8 * i + 8, :] = a + roll(b, 40, 1) + roll(c, 80, 1)


def narrow_kernel(
    gathered, odd, p, sat, perm, bs, small, out_even, out_odd, small_out, square
):
    even = lax.axis_index("narrow") % 2 == 0
    wide_even = lax.axis_index("wide") % 2 == 0
    mate = jnp.where(even, 1, 0)
    cells = NX * NY
    lanes = iota((NY, L), 1)

    def before(lo, n):
        return jnp.where(even, odd[lo : lo + n, :], gathered[mate, lo : lo + n, :])

    def after(lo, n):
        return jnp.where(even, gathered[mate, lo : lo + n, :], odd[lo : lo + n, :])

    in_slot = iota((8, L), 1) < 40

    def windows(get):
        out = []
        for i in range(5):
            block = get(N_SMALL + 8 * i, 8)
            out += [jnp.where(in_slot, roll(block, -40 * j, 1), 0.0) for j in range(3)]
        return out

    top, bottom = windows(before), windows(after)
    none = jnp.zeros((8, L), jnp.float32)
    stack = []
    for i in range(SMALL):
        own = small[i * TALL : (i + 1) * TALL, :]
        if i < ACC:
            own = own[8:24, :]
            stack.append(jnp.concatenate([top[i], own, bottom[i]], axis=0))
        else:
            stack.append(own + jnp.concatenate([top[i], top[i + 1], bottom[i + 1], bottom[i]], axis=0))
    pieces = jnp.zeros((NY, L), jnp.float32)
    for x, other_x, get in ((0, -1, before), (NX - 1, NX, after)):
        at = x * NY
        flux = trans_of(perm[at : at + NY, :], get(N_K, NY)) * (p[at : at + NY, :] - get(N_P, NY))
        for k in range(K):
            mine = lane_sum(bs[pl.ds(at * K + k, NY, stride=K), :] * -flux)
            pieces = jnp.where(lanes == k * TALL + TOP + x, mine, pieces)
            other = lane_sum(get(N_B + k * NY, NY) * flux)
            pieces = jnp.where(lanes == k * TALL + TOP + other_x, other, pieces)
    flipped = turned(square, pieces)
    stack[ACC] = stack[ACC] + bin_pieces(
        stack[:K], [flipped[k * TALL : (k + 1) * TALL, :] for k in range(K)]
    )
    for i in range(SMALL):
        small_out[i * TALL : (i + 1) * TALL, :] = stack[i]
    slot = iota((TALL, L), 1) // 8
    first = jnp.zeros((TALL, L), jnp.float32)
    last = jnp.zeros((TALL, L), jnp.float32)
    for i in range(SMALL):
        first = jnp.where(slot == i, roll(stack[i], 8 * i, 1), first)
        last = jnp.where(slot == i, roll(stack[i], 8 * i - 32, 1), last)
    blank = jnp.zeros((8, L), jnp.float32)
    for out, takes_last in ((out_even, wide_even), (out_odd, jnp.logical_not(wide_even))):
        col = jnp.where(takes_last, NY - 1, 0)
        fields = [
            p[pl.ds(col, NX, stride=NY), :],
            perm[pl.ds(cells + col, NX, stride=NY), :],
        ] + [bs[pl.ds(col * K + k, NX, stride=NY * K), :] for k in range(K)]
        for f, value in enumerate(fields):
            base = f * TALL
            lo = N_C + f * 2 * EDGE
            out[base : base + 8, :] = blank
            out[base + 24 : base + 32, :] = blank
            out[base + 3 : base + 8, :] = jnp.where(takes_last, before(lo + EDGE, EDGE), before(lo, EDGE))
            out[base + 8 : base + 24, :] = value
            out[base + 24 : base + 29, :] = jnp.where(takes_last, after(lo + EDGE, EDGE), after(lo, EDGE))
        out[W_SAT : W_SAT + NX, :] = sat[pl.ds(col, NX, stride=NY), :]
        out[W_SMALL : W_SMALL + TALL, :] = jnp.where(takes_last, last, first)


def final_kernel(
    in_even, in_odd, sent_even, sent_odd, gathered, odd, small, p, sat, perm, pore, bs, new, new_sat, square
):
    even = lax.axis_index("narrow") % 2 == 0
    wide_even = lax.axis_index("wide") % 2 == 0
    mate = jnp.where(even, 1, 0)
    cells = NX * NY

    def before(lo, n):
        return jnp.where(even, odd[lo : lo + n, :], gathered[mate, lo : lo + n, :])

    def after(lo, n):
        return jnp.where(even, gathered[mate, lo : lo + n, :], odd[lo : lo + n, :])

    def left(lo, n):
        return jnp.where(wide_even, in_odd[lo : lo + n, :], in_even[lo : lo + n, :])

    def right(lo, n):
        return jnp.where(wide_even, in_even[lo : lo + n, :], in_odd[lo : lo + n, :])

    def first(lo, n):
        return jnp.where(wide_even, sent_odd[lo : lo + n, :], sent_even[lo : lo + n, :])

    def last(lo, n):
        return jnp.where(wide_even, sent_even[lo : lo + n, :], sent_odd[lo : lo + n, :])

    lane = iota((TALL, L), 1)
    from_left, from_right = left(W_SMALL, TALL), right(W_SMALL, TALL)
    stack = []
    for i in range(SMALL):
        own = small[i * TALL : (i + 1) * TALL, :]
        own = own + jnp.where(lane < 8, roll(from_left, -8 * i, 1), 0.0)
        own = own + jnp.where(lane // 8 == 4, roll(from_right, 32 - 8 * i, 1), 0.0)
        stack.append(own)
    sup, mat = stack[:K], stack[MAT : MAT + 9]
    pieces = [jnp.zeros((TALL, L), jnp.float32)] * K
    for mine, other, y, other_y in ((first, left, 0, -1), (last, right, NY - 1, NY)):
        k_here, k_there = mine(TALL, TALL), other(TALL, TALL)
        total = k_here + k_there
        flux = (2.0 * k_here * k_there / jnp.where(total > 0, total, 1.0)) * (mine(0, TALL) - other(0, TALL))
        for k in range(K):
            lo = (2 + k) * TALL
            here = lane_sum(mine(lo, TALL) * -flux)
            there = lane_sum(other(lo, TALL) * flux)
            pieces[k] = jnp.where(lane == WEST + y, here, pieces[k])
            pieces[k] = jnp.where(lane == WEST + other_y, there, pieces[k])
    res = stack[ACC] + bin_pieces(sup, pieces)
    diag = mat[4]
    scale = jnp.where(diag > 0, OMEGA / jnp.where(diag > 0, diag, 1.0), 0.0)

    def moved(coarse):
        sides = {dy: roll(coarse, -dy, 1) for dy in (-1, 0, 1)}
        return [roll(sides[dy], -dx, 0) for dx, dy in OFFSETS]

    coarse = scale * res
    for _ in range(SWEEPS - 1):
        rest = res
        for o, value in enumerate(moved(coarse)):
            rest = rest - mat[o] * value
        coarse = coarse + scale * rest
    shifts = moved(coarse)
    picked = []
    for k in range(K):
        total = jnp.zeros((TALL, L), jnp.float32)
        for o in range(9):
            total = jnp.where(sup[k] == float(o), shifts[o], total)
        picked.append(total)
    for k in range(K):
        square[k * TALL : (k + 1) * TALL, :] = roll(picked[k], -WEST, 1)
    weights = square[...].T[0:NY, :]

    def weight(k, x):
        at = k * TALL + TOP + x
        return weights[:, at : at + 1]

    for x in range(NX):
        at = slice(x * NY, (x + 1) * NY)
        total = p[at, :]
        for k in range(K):
            total = total + bs[pl.ds(x * NY * K + k, NY, stride=K), :] * weight(k, x)
        new[at, :] = total
    ends = []
    for get, x in ((before, -1), (after, NX)):
        total = get(N_P, NY)
        for k in range(K):
            total = total + get(N_B + k * NY, NY) * weight(k, x)
        ends.append(total)
    sides = []
    for get, y in ((left, -1), (right, NY)):
        total = get(TOP, NX)
        for k in range(K):
            column = picked[k][TOP : TOP + NX, WEST + y : WEST + y + 1]
            total = total + get((2 + k) * TALL + TOP, NX) * column
        sides.append(total)

    def carried(trans, here, there, f_here, f_there):
        flux = trans * (here - there)
        return flux * jnp.where(flux > 0, f_here, f_there)

    west_k, east_k = left(TALL + TOP, NX), right(TALL + TOP, NX)
    west_f, east_f = fraction(left(W_SAT, NX)), fraction(right(W_SAT, NX))
    first_k = perm[pl.ds(cells, NX, stride=NY), :]
    west_flow = carried(
        trans_of(west_k, first_k),
        sides[0],
        new[pl.ds(0, NX, stride=NY), :],
        west_f,
        fraction(sat[pl.ds(0, NX, stride=NY), :]),
    )
    rows = iota((NY, L), 0)
    lanes = iota((NY, L), 1)
    kx_prev = before(N_K, NY)
    p_here, f_here, kx = new[0:NY, :], fraction(sat[0:NY, :]), perm[0:NY, :]
    flow_in = carried(trans_of(kx_prev, kx), ends[0], p_here, fraction(before(N_S, NY)), f_here)
    for x in range(NX):
        at = slice(x * NY, (x + 1) * NY)
        if x < NX - 1:
            nxt = slice((x + 1) * NY, (x + 2) * NY)
            p_next, f_next, kx_next = new[nxt, :], fraction(sat[nxt, :]), perm[nxt, :]
        else:
            p_next, f_next, kx_next = ends[1], fraction(after(N_S, NY)), after(N_K, NY)
        flow_out = carried(trans_of(kx, kx_next), p_here, p_next, f_here, f_next)
        total = flow_out - flow_in
        flow_in = flow_out
        ky = perm[cells + x * NY : cells + (x + 1) * NY, :]
        end = rows == NY - 1
        beside = lambda a, e: jnp.where(end, e[x : x + 1, :], roll(a, -1, 0))
        fy = carried(
            trans_of(ky, beside(ky, east_k)), p_here, beside(p_here, sides[1]), f_here, beside(f_here, east_f)
        )
        total = total + (fy - jnp.where(rows == 0, west_flow[x : x + 1, :], roll(fy, 1, 0)))
        kz = perm[2 * cells + x * NY : 2 * cells + (x + 1) * NY, :]
        fz = carried(
            trans_of(kz, roll(kz, -1, 1)), p_here, roll(p_here, -1, 1), f_here, roll(f_here, -1, 1)
        )
        fz = jnp.where(lanes < L - 1, fz, 0.0)
        total = total + (fz - roll(fz, 1, 1))
        new_sat[at, :] = sat[at, :] - DT * total / pore[at, :]
        p_here, f_here, kx = p_next, f_next, kx_next


def call(kernel, out_rows, scratch, flops, *args):
    shapes = [jax.ShapeDtypeStruct((r, L), jnp.float32) for r in out_rows]
    size = sum(a.size * a.dtype.itemsize for a in args) + sum(4 * L * r for r in out_rows)
    return pl.pallas_call(
        kernel,
        out_shape=shapes,
        in_specs=[pl.BlockSpec(memory_space=pltpu.VMEM)] * len(args),
        out_specs=[pl.BlockSpec(memory_space=pltpu.VMEM)] * len(shapes),
        scratch_shapes=[pltpu.VMEM((r, L), jnp.float32) for r in scratch],
        compiler_params=pltpu.CompilerParams(vmem_limit_bytes=32 * 1024 * 1024),
        cost_estimate=pl.CostEstimate(flops=flops, bytes_accessed=size, transcendentals=0),
    )(*args)


def swaps(n, start):
    pairs = [(i, i + 1) for i in range(start, n - 1, 2)]
    return pairs + [(j, i) for i, j in pairs]


def on_device(pressure, saturation, source, perm, pore_volume, basis, support, matrix):
    p, sat, src, k, pore = (
        a.reshape(-1, L) for a in (pressure, saturation, source, perm, pore_volume)
    )
    basis = basis.reshape(-1, L)
    support = support.transpose(0, 2, 1).reshape(NX * K, NY)
    matrix = matrix.reshape(9 * NX, NY)
    n_narrow, n_wide = lax.axis_size("narrow"), lax.axis_size("wide")
    out_even, out_odd, small, bs = call(
        residual_kernel, [N_ROWS, N_ROWS, SMALL * TALL, NX * NY * K], [TALL, L], 10**7,
        p, sat, src, k, basis, support, matrix,
    )
    odd = lax.ppermute(out_odd, "narrow", swaps(n_narrow, 1))
    gathered = lax.all_gather(
        out_even, "narrow", axis_index_groups=[[i, i + 1] for i in range(0, n_narrow, 2)]
    )
    sent_even, sent_odd, small = call(
        narrow_kernel, [W_ROWS, W_ROWS, SMALL * TALL], [L], 10**6,
        gathered, odd, p, sat, k, bs, small,
    )
    in_odd = lax.ppermute(sent_odd, "wide", swaps(n_wide, 1))
    in_even = lax.ppermute(sent_even, "wide", swaps(n_wide, 0))
    new, new_sat = call(
        final_kernel, [NX * NY, NX * NY], [L], 10**7,
        in_even, in_odd, sent_even, sent_odd, gathered, odd, small, p, sat, k, pore, bs,
    )
    return new.reshape(pressure.shape), new_sat.reshape(pressure.shape)


def solution(mesh):
    return jax.shard_map(
        on_device,
        mesh=mesh,
        in_specs=(
            P("narrow", "wide", None),
            P("narrow", "wide", None),
            P("narrow", "wide", None),
            P(None, "narrow", "wide", None),
            P("narrow", "wide", None),
            P("narrow", "wide", None, None),
            P("narrow", "wide", None),
            P(None, "narrow", "wide"),
        ),
        out_specs=(P("narrow", "wide", None), P("narrow", "wide", None)),
        check_vma=False,
    )
```

time: 172 us -> 37.9 us (0.22)
  starting transfers between devices: 148 us -> 15.3 us
  waiting for transfers between devices: 13.6 us -> 7.47 us
  other arithmetic: 5.59 us -> 0 us
  Pallas kernels: 0 us -> 5.31 us
  local copies, waits for them, and re-layouts: 2.9 us -> 6.66 us
  blocking collectives: 0 us -> 2.05 us
    ppermute x34 -> x3, starting transfers between devices: 148 us -> 15.3 us  [the longest x1 7.58 us: on_device(): odd = lax.ppermute(out_odd, 'narrow', swaps(n_narrow, 1))]
    unnamed x16 -> x18, local copies, waits for them, and re-layouts: 0.12 us -> 6.66 us
    ppermute x34 -> x3, waiting for transfers between devices: 13.6 us -> 7.47 us  [the longest x1 5.48 us: on_device(): in_odd = lax.ppermute(sent_odd, 'wide', swaps(n_wide, 1))]
    pallas_call x0 -> x3, Pallas kernels: none -> 5.31 us  [call(): pl.pallas_call(kernel, out_shape=shapes, in_specs=[pl.BlockSpec(memory_sp...]
    all_gather x0 -> x1, blocking collectives: none -> 2.05 us  [on_device(): lax.all_gather(out_even, 'narrow', axis_index_groups=[[i, i + 1] for i in...]
    sub x1 -> x0, other arithmetic: 1.95 us -> none  [on_device(): new_saturation = saturation - DT * total / pore_volume]
  transfers between devices with their start and end apart: 34 -> 3, of which waited for: 9 -> 2; matrix products, arithmetic and copies ran while one was open for 2% -> 0% of each run, Pallas kernels for 0% -> 0%
where the time goes in v1:
time: 37.9 us; the launch traced here: 37.4 us
  starting transfers between devices  15.3 us (40%)
  waiting for transfers between devices  7.47 us (20%)
  local copies, waits for them, and re-layouts  6.66 us (18%)
  Pallas kernels  5.31 us (14%)
  blocking collectives  2.05 us (5%)
  between operations  0.69 us (2%)
    ppermute x1, starting transfers between devices, on_device(): odd = lax.ppermute(out_odd, 'narrow', swaps(n_narrow, 1))  7.58 us
    unnamed x18, local copies, waits for them, and re-layouts  6.66 us
    ppermute x1, waiting for transfers between devices, on_device(): in_odd = lax.ppermute(sent_odd, 'wide', swaps(n_wide, 1))  5.48 us
    pallas_call x3, Pallas kernels, call(): pl.pallas_call(kernel, out_shape=shapes, in_specs=[pl.BlockSpec(memory_sp...  5.31 us
    ppermute x1, starting transfers between devices, on_device(): in_odd = lax.ppermute(sent_odd, 'wide', swaps(n_wide, 1))  4.56 us
    ppermute x1, starting transfers between devices, on_device(): in_even = lax.ppermute(sent_even, 'wide', swaps(n_wide, 0))  3.12 us
    all_gather x1, blocking collectives, on_device(): lax.all_gather(out_even, 'narrow', axis_index_groups=[[i, i + 1] for i in...  2.05 us
    ppermute x1, waiting for transfers between devices, on_device(): odd = lax.ppermute(out_odd, 'narrow', swaps(n_narrow, 1))  1.99 us
  transfers between devices with their start and end apart: 3, of which 2 were waited for; matrix products, arithmetic and copies ran while one was open for 0% of the time, Pallas kernels for 0%

profile of v1, /device:TPU:161, one launch (start us, length us, event | category | flops | bytes accessed | tf_op | source)
XLA Modules:
  0.0 37.4 jit_solution(6947239467966292617)
XLA Ops:
  0.6 0.0 copy-start
  0.6 1.1 %copy-done = f32[3,16,32,128]{3,2,1,0:T(8,128)S(1)} copy-done((f32[3,16,32,128]{3,2,1,0:T(8,128)S(1)}, f32[3,16,32,128]{3,2,1,0:T(8,128)}, u32[]{:S(2)}) %copy-start) | copy-done | bytes 786456
  1.8 0.0 copy-start.2
  1.8 0.9 %copy-done.2 = f32[16,32,128]{2,1,0:T(8,128)S(1)} copy-done((f32[16,32,128]{2,1,0:T(8,128)S(1)}, f32[16,32,128]{2,1,0:T(8,128)}, u32[]{:S(2)}) %copy-start.2) | copy-done | bytes 262168
  2.7 0.0 copy-start.3
  2.7 0.9 %copy-done.3 = f32[16,32,128]{2,1,0:T(8,128)S(1)} copy-done((f32[16,32,128]{2,1,0:T(8,128)S(1)}, f32[16,32,128]{2,1,0:T(8,128)}, u32[]{:S(2)}) %copy-start.3) | copy-done | bytes 262168
  3.7 0.0 copy-start.4
  3.7 1.0 %copy-done.4 = bf16[16,32,4,128]{3,2,1,0:T(4,128)(2,1)S(1)} copy-done((bf16[16,32,4,128]{3,2,1,0:T(4,128)(2,1)S(1)}, bf16[16,32,4,128]{3,2,1,0:T(4,128)(2,1)}, u32[]{:S(2)}) %copy-start.4) | copy-done | bytes 524312
  4.7 0.0 copy-start.5
  4.7 0.9 %copy-done.5 = f32[16,32,128]{2,1,0:T(8,128)S(1)} copy-done((f32[16,32,128]{2,1,0:T(8,128)S(1)}, f32[16,32,128]{2,1,0:T(8,128)}, u32[]{:S(2)}) %copy-start.5) | copy-done | bytes 262168
  5.7 0.0 copy-start.7
  5.7 0.9 %copy-done.7 = f32[9,16,32]{2,1,0:T(8,128)S(1)} copy-done((f32[9,16,32]{2,1,0:T(8,128)S(1)}, f32[9,16,32]{2,1,0:T(8,128)}, u32[]{:S(2)}) %copy-start.7) | copy-done | bytes 18456
  6.5 0.0 copy-start.8
  6.5 0.8 %copy-done.8 = s32[16,32,4]{1,2,0:T(4,128)S(1)} copy-done((s32[16,32,4]{1,2,0:T(4,128)S(1)}, s32[16,32,4]{1,2,0:T(4,128)}, u32[]{:S(2)}) %copy-start.8) | copy-done | bytes 8216
  7.3 0.0 copy-start.1
  7.3 1.6 %shard_map.95 = (f32[328,128]{1,0:T(8,128)S(1)}, f32[328,128]{1,0:T(8,128)S(1)}, f32[448,128]{1,0:T(8,128)S(1)}, f32[2048,128]{1,0:T(8,128)S(1)}) custom-call(f32[512,128]{1,0:T(8,128)S(1)} %bitcast.18, f32[512,128]{1,0:T(8,128)S(1)} %bitcast.21, f32[512,128]{1,0:T(8,128)S(1)} %bitcast.25, f32[1536,128]{1,0:T(8,128)S(1)} %bitcast.13, ...), custom_call_target="tpu_custom_call" | custom-call | flops 10000000 | bytes 3737600 | tf_op jit(solution)/shard_map/pallas_call | solution.py:362
  8.9 7.6 %collective-permute-start = (f32[328,128]{1,0:T(8,128)S(1)}, f32[328,128]{1,0:T(8,128)S(1)}, u32[]{:S(2)}, u32[]{:S(2)}) collective-permute-start(f32[328,128]{1,0:T(8,128)S(1)} %get-tuple-element.12), channel_id=1, source_target_pairs={{1,2},{3,4},{5,6},{2,1},{4,3},{6,5},{9,10},{11,12},{13,14},{10,9},... | collective-permute-start | bytes 503816 | tf_op jit(solution)/shard_map/ppermute | solution.py:390
  16.5 2.0 %all-gather = f32[656,128]{1,0:T(8,128)S(1)} all-gather(f32[328,128]{1,0:T(8,128)S(1)} %get-tuple-element.11), channel_id=2, replica_groups={{0,1},{2,3},{4,5},{6,7},{8,9},{10,11},{12,13},{14,15},{16,17},{18,19},{..., dimensions={0}, use_global_device_ids=true | all-gather | bytes 503808 | tf_op jit(solution)/shard_map/all_gather | solution.py:391
  18.6 2.0 %collective-permute-done.odd = f32[328,128]{1,0:T(8,128)S(1)} collective-permute-done((f32[328,128]{1,0:T(8,128)S(1)}, f32[328,128]{1,0:T(8,128)S(1)}, u32[]{:S(2)}, u32[]{:S(2)}) %collective-permute-start) | collective-permute-done | bytes 167968 | tf_op jit(solution)/shard_map/ppermute | solution.py:390
  20.6 0.0 copy-done.1
  20.6 0.0 copy-start.6
  20.6 0.5 %shard_map.96 = (f32[240,128]{1,0:T(8,128)S(1)}, f32[240,128]{1,0:T(8,128)S(1)}, f32[448,128]{1,0:T(8,128)S(1)}) custom-call(f32[2,328,128]{2,1,0:T(8,128)S(1)} %bitcast.16, f32[328,128]{1,0:T(8,128)S(1)} %collective-permute-done.odd, f32[512,128]{1,0:T(8,128)S(1)} %bitcast.19, f32[512,128]{1,0:T(8,128)S(1)} %bitcast.22, f32[1536,128]{1,0:T(8,128)S(1)} %bitcast.14, ...), custom_call_target="tpu_custom_call" | custom-call | flops 1000000 | bytes 3567616 | tf_op jit(solution)/shard_map/pallas_call | solution.py:362
  21.1 3.1 %collective-permute-start.1 = (f32[240,128]{1,0:T(8,128)S(1)}, f32[240,128]{1,0:T(8,128)S(1)}, u32[]{:S(2)}, u32[]{:S(2)}) collective-permute-start(f32[240,128]{1,0:T(8,128)S(1)} %get-tuple-element.15.sent_even), channel_id=1, source_target_pairs={{0,8},{16,24},{32,40},{48,56},{64,72},{80,88},{96,104},{112,120},{... | collective-permute-start | bytes 368648 | tf_op jit(solution)/shard_map/ppermute | solution.py:399
  24.2 4.6 %collective-permute-start.2 = (f32[240,128]{1,0:T(8,128)S(1)}, f32[240,128]{1,0:T(8,128)S(1)}, u32[]{:S(2)}, u32[]{:S(2)}) collective-permute-start(f32[240,128]{1,0:T(8,128)S(1)} %get-tuple-element.16.sent_odd), channel_id=1, source_target_pairs={{8,16},{24,32},{40,48},{56,64},{72,80},{88,96},{104,112},{120,128}... | collective-permute-start | bytes 368648 | tf_op jit(solution)/shard_map/ppermute | solution.py:398
  28.8 0.0 collective-permute-done.1.in_even
  28.8 5.5 %collective-permute-done.2.in_odd = f32[240,128]{1,0:T(8,128)S(1)} collective-permute-done((f32[240,128]{1,0:T(8,128)S(1)}, f32[240,128]{1,0:T(8,128)S(1)}, u32[]{:S(2)}, u32[]{:S(2)}) %collective-permute-start.2) | collective-permute-done | bytes 122912 | tf_op jit(solution)/shard_map/ppermute | solution.py:398
  34.3 0.0 copy-done.6
  34.3 3.1 %shard_map.97 = (f32[512,128]{1,0:T(8,128)}, f32[512,128]{1,0:T(8,128)}) custom-call(f32[240,128]{1,0:T(8,128)S(1)} %collective-permute-done.1.in_even, f32[240,128]{1,0:T(8,128)S(1)} %collective-permute-done.2.in_odd, f32[240,128]{1,0:T(8,128)S(1)} %get-tuple-element.15.sent_even, f32[240,128]{1,0:T(8,128)S(1)} %get-tuple-element.16.sent_odd, ...), custom_call_target="tpu_custom_call" | custom-call | flops 10000000 | bytes 4370432 | tf_op jit(solution)/shard_map/pallas_call | solution.py:362
Async XLA Ops:
  0.6 1.1 %copy-start = (f32[3,16,32,128]{3,2,1,0:T(8,128)S(1)}, f32[3,16,32,128]{3,2,1,0:T(8,128)}, u32[]{:S(2)}) copy-start(f32[3,16,32,128]{3,2,1,0:T(8,128)} %param.11) | copy-start | bytes 2359300
  1.8 0.9 %copy-start.2 = (f32[16,32,128]{2,1,0:T(8,128)S(1)}, f32[16,32,128]{2,1,0:T(8,128)}, u32[]{:S(2)}) copy-start(f32[16,32,128]{2,1,0:T(8,128)} %param.8) | copy-start | bytes 786436
  2.7 0.9 %copy-start.3 = (f32[16,32,128]{2,1,0:T(8,128)S(1)}, f32[16,32,128]{2,1,0:T(8,128)}, u32[]{:S(2)}) copy-start(f32[16,32,128]{2,1,0:T(8,128)} %param.9) | copy-start | bytes 786436
  3.7 1.0 %copy-start.4 = (bf16[16,32,4,128]{3,2,1,0:T(4,128)(2,1)S(1)}, bf16[16,32,4,128]{3,2,1,0:T(4,128)(2,1)}, u32[]{:S(2)}) copy-start(bf16[16,32,4,128]{3,2,1,0:T(4,128)(2,1)} %param.13) | copy-start | bytes 1572868
  4.7 0.9 %copy-start.5 = (f32[16,32,128]{2,1,0:T(8,128)S(1)}, f32[16,32,128]{2,1,0:T(8,128)}, u32[]{:S(2)}) copy-start(f32[16,32,128]{2,1,0:T(8,128)} %param.10) | copy-start | bytes 786436
  5.7 0.9 %copy-start.7 = (f32[9,16,32]{2,1,0:T(8,128)S(1)}, f32[9,16,32]{2,1,0:T(8,128)}, u32[]{:S(2)}) copy-start(f32[9,16,32]{2,1,0:T(8,128)} %param.15) | copy-start | bytes 55300
  6.5 0.8 %copy-start.8 = (s32[16,32,4]{1,2,0:T(4,128)S(1)}, s32[16,32,4]{1,2,0:T(4,128)}, u32[]{:S(2)}) copy-start(s32[16,32,4]{1,2,0:T(4,128)} %param.14) | copy-start | bytes 24580
  7.3 13.3 %copy-start.1 = (f32[3,16,32,128]{3,2,1,0:T(8,128)S(1)}, f32[3,16,32,128]{3,2,1,0:T(8,128)}, u32[]{:S(2)}) copy-start(f32[3,16,32,128]{3,2,1,0:T(8,128)} %param.11) | copy-start | bytes 2359300
  8.9 11.6 %collective-permute-start = (f32[328,128]{1,0:T(8,128)S(1)}, f32[328,128]{1,0:T(8,128)S(1)}, u32[]{:S(2)}, u32[]{:S(2)}) collective-permute-start(f32[328,128]{1,0:T(8,128)S(1)} %get-tuple-element.12), channel_id=1, source_target_pairs={{1,2},{3,4},{5,6},{2,1},{4,3},{6,5},{9,10},{11,12},{13,14},{10,9},... | collective-permute-start | bytes 503816 | tf_op jit(solution)/shard_map/ppermute | solution.py:390
  20.6 13.7 %copy-start.6 = (f32[16,32,128]{2,1,0:T(8,128)S(1)}, f32[16,32,128]{2,1,0:T(8,128)}, u32[]{:S(2)}) copy-start(f32[16,32,128]{2,1,0:T(8,128)} %param.12) | copy-start | bytes 786436
  21.1 7.7 %collective-permute-start.1 = (f32[240,128]{1,0:T(8,128)S(1)}, f32[240,128]{1,0:T(8,128)S(1)}, u32[]{:S(2)}, u32[]{:S(2)}) collective-permute-start(f32[240,128]{1,0:T(8,128)S(1)} %get-tuple-element.15.sent_even), channel_id=1, source_target_pairs={{0,8},{16,24},{32,40},{48,56},{64,72},{80,88},{96,104},{112,120},{... | collective-permute-start | bytes 368648 | tf_op jit(solution)/shard_map/ppermute | solution.py:399
  24.2 10.1 %collective-permute-start.2 = (f32[240,128]{1,0:T(8,128)S(1)}, f32[240,128]{1,0:T(8,128)S(1)}, u32[]{:S(2)}, u32[]{:S(2)}) collective-permute-start(f32[240,128]{1,0:T(8,128)S(1)} %get-tuple-element.16.sent_odd), channel_id=1, source_target_pairs={{8,16},{24,32},{40,48},{56,64},{72,80},{88,96},{104,112},{120,128}... | collective-permute-start | bytes 368648 | tf_op jit(solution)/shard_map/ppermute | solution.py:398

commit v2 on v1

--- a/solution.py
+++ b/solution.py
@@ -70,40 +70,96 @@
     return scratch[...].T
 
 
-def residual_kernel(
-    p, sat, src, perm, basis, support, matrix, out_even, out_odd, small, bs, place, square
+def rows_residual(p, perm, src, trans, lo, hi, base):
+    rows, lanes = iota((NY, L), 0), iota((NY, L), 1)
+
+    def face(x):
+        a, b = slice(x * NY, (x + 1) * NY), slice((x + 1) * NY, (x + 2) * NY)
+        value = trans_of(perm[0, a, :], perm[0, b, :])
+        if x >= lo:
+            trans[0, (x - base) * NY : (x - base + 1) * NY, :] = value
+        return value * (p[a, :] - p[b, :])
+
+    result = []
+    last = face(lo - 1) if lo > 0 else None
+    for x in range(lo, hi):
+        at = slice(x * NY, (x + 1) * NY)
+        here, ky, kz = p[at, :], perm[1, at, :], perm[2, at, :]
+        ty = jnp.where(rows < NY - 1, trans_of(ky, roll(ky, -1, 0)), 0.0)
+        tz = jnp.where(lanes < L - 1, trans_of(kz, roll(kz, -1, 1)), 0.0)
+        to = slice((x - base) * NY, (x - base + 1) * NY)
+        trans[1, to, :] = ty
+        trans[2, to, :] = tz
+        fy = ty * (here - roll(here, -1, 0))
+        fz = tz * (here - roll(here, -1, 1))
+        total = (fy - roll(fy, 1, 0)) + (fz - roll(fz, 1, 1))
+        if last is not None:
+            total = total - last
+        last = None
+        if x < NX - 1:
+            last = face(x)
+            total = total + last
+        result.append(src[to, :] - total)
+    return result
+
+
+def add_pieces(pieces, residuals, lo, bs, base):
+    lanes = iota((NY, L), 1)
+    for i, res in enumerate(residuals):
+        x = lo + i
+        for k in range(K):
+            b = bs[pl.ds((x - base) * NY * K + k, NY, stride=K), :]
+            pieces = jnp.where(lanes == k * TALL + TOP + x, lane_sum(b * res), pieces)
+    return pieces
+
+
+def split_pieces(square, pieces):
+    flipped = turned(square, pieces)
+    return [flipped[k * TALL : (k + 1) * TALL, :] for k in range(K)]
+
+
+LIMIT1 = 24
+LOW, HIGH = EDGE, NX - EDGE
+
+
+def copies_of(sems, pairs):
+    out = [pltpu.make_async_copy(src, dst, sems.at[i]) for i, (src, dst) in enumerate(pairs)]
+    for copy in out:
+        copy.start()
+    return out
+
+
+def edge_kernel(
+    p_in, perm_in, src_in, basis_in, support_in, matrix_in, sat_in,
+    out_even, out_odd, small, p, perm, sat, bs, trans,
+    src, basis, support, matrix, place, square, sems,
 ):
     even = lax.axis_index("narrow") % 2 == 0
-    lanes = iota((NY, L), 1)
-    rows = iota((NY, L), 0)
-    cells = NX * NY
-    div = [None] * NX
-    last_x = None
-    for x in range(NX):
-        at = slice(x * NY, (x + 1) * NY)
-        here = p[at, :]
-        kx, ky, kz = (perm[c * cells + x * NY : c * cells + (x + 1) * NY, :] for c in range(3))
-        fy = trans_of(ky, roll(ky, -1, 0)) * (here - roll(here, -1, 0))
-        fy = jnp.where(rows < NY - 1, fy, 0.0)
-        fz = trans_of(kz, roll(kz, -1, 1)) * (here - roll(here, -1, 1))
-        fz = jnp.where(lanes < L - 1, fz, 0.0)
-        total = (fy - roll(fy, 1, 0)) + (fz - roll(fz, 1, 1))
-        if x < NX - 1:
-            fx = trans_of(kx, perm[(x + 1) * NY : (x + 2) * NY, :]) * (here - p[(x + 1) * NY : (x + 2) * NY, :])
-            total = total + fx
-        if last_x is not None:
-            total = total - last_x
-        last_x = fx
-        div[x] = total
+    top, bottom, middle = (
+        pl.ds(0, (LOW + 1) * NY),
+        pl.ds((HIGH - 1) * NY, (LOW + 1) * NY),
+        pl.ds((LOW + 1) * NY, (HIGH - LOW - 2) * NY),
+    )
+    pairs = []
+    for part, first in ((top, 0), (bottom, HIGH)):
+        own, fine = pl.ds(first * NY, EDGE * NY), pl.ds(first * NY * K, EDGE * NY * K)
+        pairs += [(p_in.at[part], p.at[part]), (perm_in.at[:, part], perm.at[:, part])]
+        pairs += [(src_in.at[own], src.at[own]), (basis_in.at[fine], basis.at[fine])]
+    pairs += [(support_in, support), (matrix_in, matrix), (sat_in, sat)]
+    pairs += [(p_in.at[middle], p.at[middle]), (perm_in.at[:, middle], perm.at[:, middle])]
+    copies = copies_of(sems, pairs)
     pieces = jnp.zeros((NY, L), jnp.float32)
-    for x in range(NX):
-        at = slice(x * NY * K, (x + 1) * NY * K)
-        bs[at, :] = basis[at, :].astype(jnp.float32)
-        res = src[x * NY : (x + 1) * NY, :] - div[x]
-        for k in range(K):
-            b = bs[pl.ds(x * NY * K + k, NY, stride=K), :]
-            pieces = jnp.where(lanes == k * TALL + TOP + x, lane_sum(b * res), pieces)
-    flipped = turned(square, pieces)
+    for i, first in enumerate((0, HIGH)):
+        for copy in copies[4 * i : 4 * i + 3]:
+            copy.wait()
+        residuals = rows_residual(p, perm, src, trans, first, first + EDGE, 0)
+        copies[4 * i + 3].wait()
+        fine = slice(first * NY * K, (first + EDGE) * NY * K)
+        bs[fine, :] = basis[fine, :].astype(jnp.float32)
+        pieces = add_pieces(pieces, residuals, first, bs, 0)
+    pieces = split_pieces(square, pieces)
+    copies[8].wait()
+    copies[9].wait()
     place[...] = jnp.zeros((TALL, L), jnp.float32)
     stack = []
     for i in range(K + 9):
@@ -113,15 +169,16 @@
             value = matrix[(i - MAT) * NX : (i - MAT + 1) * NX, :]
         place[TOP : TOP + NX, 0:NY] = value
         stack.append(roll(place[...], WEST, 1))
-    acc = bin_pieces(stack[:K], [flipped[k * TALL : (k + 1) * TALL, :] for k in range(K)])
+    acc = bin_pieces(stack[:K], pieces)
     stack.append(acc)
     for i in range(SMALL):
         small[i * TALL : (i + 1) * TALL, :] = stack[i]
+    copies[10].wait()
     for out, takes_last in ((out_even, even), (out_odd, jnp.logical_not(even))):
         edge = jnp.where(takes_last, NX - 1, 0)
         row = pl.multiple_of(edge * NY, NY)
         out[N_P : N_P + NY, :] = p[pl.ds(row, NY), :]
-        out[N_K : N_K + NY, :] = perm[pl.ds(row, NY), :]
+        out[N_K : N_K + NY, :] = perm[0, pl.ds(row, NY), :]
         out[N_S : N_S + NY, :] = sat[pl.ds(row, NY), :]
         for k in range(K):
             out[N_B + k * NY : N_B + (k + 1) * NY, :] = bs[pl.ds(row * K + k, NY, stride=K), :]
@@ -129,7 +186,7 @@
         for c, col in enumerate((0, NY - 1)):
             fields = [
                 p[pl.ds(start + col, EDGE, stride=NY), :],
-                perm[pl.ds(start + (cells + col), EDGE, stride=NY), :],
+                perm[1, pl.ds(start + col, EDGE, stride=NY), :],
             ] + [bs[pl.ds((start + col) * K + k, EDGE, stride=NY * K), :] for k in range(K)]
             for f, value in enumerate(fields):
                 to = N_C + (f * 2 + c) * EDGE
@@ -139,15 +196,35 @@
         for i in range(5):
             a, b, c = window[3 * i : 3 * i + 3]
             out[N_SMALL + 8 * i : N_SMALL + 8 * i + 8, :] = a + roll(b, 40, 1) + roll(c, 80, 1)
+    copies[11].wait()
+    copies[12].wait()
+
+
+def middle_kernel(
+    src_in, basis_in, pore_in, p, perm, sat, small,
+    bs, trans, acc, frac, rate,
+    src, basis, pore, square, sems,
+):
+    own, fine = pl.ds(LOW * NY, (HIGH - LOW) * NY), pl.ds(LOW * NY * K, (HIGH - LOW) * NY * K)
+    copies = copies_of(sems, [(src_in.at[own], src), (basis_in.at[fine], basis), (pore_in, pore)])
+    frac[...] = fraction(sat[...])
+    copies[0].wait()
+    residuals = rows_residual(p, perm, src, trans, LOW, HIGH, LOW)
+    copies[1].wait()
+    bs[...] = basis[...].astype(jnp.float32)
+    pieces = add_pieces(jnp.zeros((NY, L), jnp.float32), residuals, LOW, bs, LOW)
+    sup = [small[k * TALL : (k + 1) * TALL, :] for k in range(K)]
+    acc[...] = bin_pieces(sup, split_pieces(square, pieces))
+    copies[2].wait()
+    rate[...] = DT / pore[...]
 
 
 def narrow_kernel(
-    gathered, odd, p, sat, perm, bs, small, out_even, out_odd, small_out, square
+    gathered, odd, p, sat, perm, bs, bs_middle, small, acc_middle, out_odd, out_even, small_out, square
 ):
     even = lax.axis_index("narrow") % 2 == 0
     wide_even = lax.axis_index("wide") % 2 == 0
     mate = jnp.where(even, 1, 0)
-    cells = NX * NY
     lanes = iota((NY, L), 1)
 
     def before(lo, n):
@@ -178,16 +255,13 @@
     pieces = jnp.zeros((NY, L), jnp.float32)
     for x, other_x, get in ((0, -1, before), (NX - 1, NX, after)):
         at = x * NY
-        flux = trans_of(perm[at : at + NY, :], get(N_K, NY)) * (p[at : at + NY, :] - get(N_P, NY))
+        flux = trans_of(perm[0, at : at + NY, :], get(N_K, NY)) * (p[at : at + NY, :] - get(N_P, NY))
         for k in range(K):
             mine = lane_sum(bs[pl.ds(at * K + k, NY, stride=K), :] * -flux)
             pieces = jnp.where(lanes == k * TALL + TOP + x, mine, pieces)
             other = lane_sum(get(N_B + k * NY, NY) * flux)
             pieces = jnp.where(lanes == k * TALL + TOP + other_x, other, pieces)
-    flipped = turned(square, pieces)
-    stack[ACC] = stack[ACC] + bin_pieces(
-        stack[:K], [flipped[k * TALL : (k + 1) * TALL, :] for k in range(K)]
-    )
+    stack[ACC] = stack[ACC] + acc_middle[...] + bin_pieces(stack[:K], split_pieces(square, pieces))
     for i in range(SMALL):
         small_out[i * TALL : (i + 1) * TALL, :] = stack[i]
     slot = iota((TALL, L), 1) // 8
@@ -199,29 +273,35 @@
     blank = jnp.zeros((8, L), jnp.float32)
     for out, takes_last in ((out_even, wide_even), (out_odd, jnp.logical_not(wide_even))):
         col = jnp.where(takes_last, NY - 1, 0)
-        fields = [
-            p[pl.ds(col, NX, stride=NY), :],
-            perm[pl.ds(cells + col, NX, stride=NY), :],
-        ] + [bs[pl.ds(col * K + k, NX, stride=NY * K), :] for k in range(K)]
-        for f, value in enumerate(fields):
+        for f in range(FIELDS):
             base = f * TALL
             lo = N_C + f * 2 * EDGE
             out[base : base + 8, :] = blank
             out[base + 24 : base + 32, :] = blank
             out[base + 3 : base + 8, :] = jnp.where(takes_last, before(lo + EDGE, EDGE), before(lo, EDGE))
-            out[base + 8 : base + 24, :] = value
+            if f < 2:
+                field = p[pl.ds(col, NX, stride=NY), :] if f == 0 else perm[1, pl.ds(col, NX, stride=NY), :]
+                out[base + TOP : base + TOP + NX, :] = field
+            else:
+                at = col * K + f - 2
+                for ref, x, start, n in (
+                    (bs, 0, 0, LOW), (bs_middle, LOW, 0, HIGH - LOW), (bs, HIGH, HIGH, NX - HIGH)
+                ):
+                    column = ref[pl.ds(start * NY * K + at, n, stride=NY * K), :]
+                    out[base + TOP + x : base + TOP + x + n, :] = column
             out[base + 24 : base + 29, :] = jnp.where(takes_last, after(lo + EDGE, EDGE), after(lo, EDGE))
         out[W_SAT : W_SAT + NX, :] = sat[pl.ds(col, NX, stride=NY), :]
         out[W_SMALL : W_SMALL + TALL, :] = jnp.where(takes_last, last, first)
 
 
 def final_kernel(
-    in_even, in_odd, sent_even, sent_odd, gathered, odd, small, p, sat, perm, pore, bs, new, new_sat, square
+    in_odd, in_even, sent_odd, sent_even, gathered, odd, small, p, sat, perm, bs, trans, bs_middle, trans_middle, frac, rate,
+    new_out, new_sat_out,
+    new, new_sat, square, sems,
 ):
     even = lax.axis_index("narrow") % 2 == 0
     wide_even = lax.axis_index("wide") % 2 == 0
     mate = jnp.where(even, 1, 0)
-    cells = NX * NY
 
     def before(lo, n):
         return jnp.where(even, odd[lo : lo + n, :], gathered[mate, lo : lo + n, :])
@@ -293,9 +373,11 @@
     for x in range(NX):
         at = slice(x * NY, (x + 1) * NY)
         total = p[at, :]
-        for k in range(K):
-            total = total + bs[pl.ds(x * NY * K + k, NY, stride=K), :] * weight(k, x)
+        ref, base = (bs_middle, LOW) if LOW <= x < HIGH else (bs, 0)
+        for k in range(K):
+            total = total + ref[pl.ds((x - base) * NY * K + k, NY, stride=K), :] * weight(k, x)
         new[at, :] = total
+    copies = copies_of(sems, [(new, new_out)])
     ends = []
     for get, x in ((before, -1), (after, NX)):
         total = get(N_P, NY)
@@ -310,64 +392,81 @@
             total = total + get((2 + k) * TALL + TOP, NX) * column
         sides.append(total)
 
-    def carried(trans, here, there, f_here, f_there):
-        flux = trans * (here - there)
+    def carried(value, here, there, f_here, f_there):
+        flux = value * (here - there)
         return flux * jnp.where(flux > 0, f_here, f_there)
 
-    west_k, east_k = left(TALL + TOP, NX), right(TALL + TOP, NX)
     west_f, east_f = fraction(left(W_SAT, NX)), fraction(right(W_SAT, NX))
-    first_k = perm[pl.ds(cells, NX, stride=NY), :]
+    east_t = trans_of(perm[1, pl.ds(NY - 1, NX, stride=NY), :], right(TALL + TOP, NX))
     west_flow = carried(
-        trans_of(west_k, first_k),
+        trans_of(perm[1, pl.ds(0, NX, stride=NY), :], left(TALL + TOP, NX)),
         sides[0],
         new[pl.ds(0, NX, stride=NY), :],
         west_f,
-        fraction(sat[pl.ds(0, NX, stride=NY), :]),
+        frac[pl.ds(0, NX, stride=NY), :],
     )
     rows = iota((NY, L), 0)
-    lanes = iota((NY, L), 1)
-    kx_prev = before(N_K, NY)
-    p_here, f_here, kx = new[0:NY, :], fraction(sat[0:NY, :]), perm[0:NY, :]
-    flow_in = carried(trans_of(kx_prev, kx), ends[0], p_here, fraction(before(N_S, NY)), f_here)
+    end = rows == NY - 1
+    p_here, f_here = new[0:NY, :], frac[0:NY, :]
+    flow_in = carried(
+        trans_of(before(N_K, NY), perm[0, 0:NY, :]), ends[0], p_here, fraction(before(N_S, NY)), f_here
+    )
     for x in range(NX):
         at = slice(x * NY, (x + 1) * NY)
+        ref, base = (trans_middle, LOW) if LOW <= x < HIGH else (trans, 0)
+        tx, ty, tz = (ref[c, (x - base) * NY : (x - base + 1) * NY, :] for c in range(3))
         if x < NX - 1:
             nxt = slice((x + 1) * NY, (x + 2) * NY)
-            p_next, f_next, kx_next = new[nxt, :], fraction(sat[nxt, :]), perm[nxt, :]
+            p_next, f_next = new[nxt, :], frac[nxt, :]
         else:
-            p_next, f_next, kx_next = ends[1], fraction(after(N_S, NY)), after(N_K, NY)
-        flow_out = carried(trans_of(kx, kx_next), p_here, p_next, f_here, f_next)
+            p_next, f_next = ends[1], fraction(after(N_S, NY))
+            tx = trans_of(perm[0, at, :], after(N_K, NY))
+        flow_out = carried(tx, p_here, p_next, f_here, f_next)
         total = flow_out - flow_in
         flow_in = flow_out
-        ky = perm[cells + x * NY : cells + (x + 1) * NY, :]
-        end = rows == NY - 1
         beside = lambda a, e: jnp.where(end, e[x : x + 1, :], roll(a, -1, 0))
         fy = carried(
-            trans_of(ky, beside(ky, east_k)), p_here, beside(p_here, sides[1]), f_here, beside(f_here, east_f)
+            jnp.where(end, east_t[x : x + 1, :], ty),
+            p_here,
+            beside(p_here, sides[1]),
+            f_here,
+            beside(f_here, east_f),
         )
         total = total + (fy - jnp.where(rows == 0, west_flow[x : x + 1, :], roll(fy, 1, 0)))
-        kz = perm[2 * cells + x * NY : 2 * cells + (x + 1) * NY, :]
-        fz = carried(
-            trans_of(kz, roll(kz, -1, 1)), p_here, roll(p_here, -1, 1), f_here, roll(f_here, -1, 1)
-        )
-        fz = jnp.where(lanes < L - 1, fz, 0.0)
+        fz = carried(tz, p_here, roll(p_here, -1, 1), f_here, roll(f_here, -1, 1))
         total = total + (fz - roll(fz, 1, 1))
-        new_sat[at, :] = sat[at, :] - DT * total / pore[at, :]
-        p_here, f_here, kx = p_next, f_next, kx_next
-
-
-def call(kernel, out_rows, scratch, flops, *args):
-    shapes = [jax.ShapeDtypeStruct((r, L), jnp.float32) for r in out_rows]
-    size = sum(a.size * a.dtype.itemsize for a in args) + sum(4 * L * r for r in out_rows)
+        new_sat[at, :] = sat[at, :] - rate[at, :] * total
+        p_here, f_here = p_next, f_next
+        if x % 4 == 3:
+            part = pl.ds((x - 3) * NY, 4 * NY)
+            copy = pltpu.make_async_copy(new_sat.at[part], new_sat_out.at[part], sems.at[1 + x // 4])
+            copy.start()
+            copies.append(copy)
+    for copy in copies:
+        copy.wait()
+
+
+VMEM = pl.BlockSpec(memory_space=pltpu.VMEM)
+HBM = pl.BlockSpec(memory_space=pltpu.HBM)
+
+
+def call(kernel, outs, scratch, flops, args, far=0, out_spec=VMEM, limit=24):
+    args = [pltpu.with_memory_space_constraint(a, pltpu.HBM) for a in args[:far]] + args[far:]
+    shapes = [jax.ShapeDtypeStruct(shape, jnp.float32) for shape in outs]
+    size = sum(a.size * a.dtype.itemsize for a in args) + sum(4 * a.size for a in shapes)
     return pl.pallas_call(
         kernel,
         out_shape=shapes,
-        in_specs=[pl.BlockSpec(memory_space=pltpu.VMEM)] * len(args),
-        out_specs=[pl.BlockSpec(memory_space=pltpu.VMEM)] * len(shapes),
-        scratch_shapes=[pltpu.VMEM((r, L), jnp.float32) for r in scratch],
-        compiler_params=pltpu.CompilerParams(vmem_limit_bytes=32 * 1024 * 1024),
+        in_specs=[HBM] * far + [VMEM] * (len(args) - far),
+        out_specs=[out_spec] * len(shapes),
+        scratch_shapes=scratch,
+        compiler_params=pltpu.CompilerParams(vmem_limit_bytes=limit * 1024 * 1024),
         cost_estimate=pl.CostEstimate(flops=flops, bytes_accessed=size, transcendentals=0),
     )(*args)
+
+
+def space(*shape, dtype=jnp.float32):
+    return pltpu.VMEM(shape, dtype)
 
 
 def swaps(n, start):
@@ -375,31 +474,63 @@
     return pairs + [(j, i) for i, j in pairs]
 
 
-def on_device(pressure, saturation, source, perm, pore_volume, basis, support, matrix):
-    p, sat, src, k, pore = (
-        a.reshape(-1, L) for a in (pressure, saturation, source, perm, pore_volume)
-    )
-    basis = basis.reshape(-1, L)
+def on_device(pressure, saturation, source, permeability, pore_volume, basis, support, matrix):
+    p_in, sat_in, src_in, pore_in = (
+        a.reshape(-1, L) for a in (pressure, saturation, source, pore_volume)
+    )
+    perm_in = permeability.reshape(3, -1, L)
+    basis_in = basis.reshape(-1, L)
     support = support.transpose(0, 2, 1).reshape(NX * K, NY)
     matrix = matrix.reshape(9 * NX, NY)
     n_narrow, n_wide = lax.axis_size("narrow"), lax.axis_size("wide")
-    out_even, out_odd, small, bs = call(
-        residual_kernel, [N_ROWS, N_ROWS, SMALL * TALL, NX * NY * K], [TALL, L], 10**7,
-        p, sat, src, k, basis, support, matrix,
+    cells, fine, middle = NX * NY, NX * NY * K, (HIGH - LOW) * NY
+    out_even, out_odd, small, p, perm, sat, bs, trans = call(
+        edge_kernel,
+        [(N_ROWS, L), (N_ROWS, L), (SMALL * TALL, L), (cells, L), (3, cells, L), (cells, L), (fine, L), (3, cells, L)],
+        [
+            space(cells, L), space(fine, L, dtype=jnp.bfloat16), space(NX * K, NY, dtype=jnp.int32), space(9 * NX, NY),
+            space(TALL, L), space(L, L), pltpu.SemaphoreType.DMA((13,)),
+        ],
+        10**7,
+        [p_in, perm_in, src_in, basis_in, support, matrix, sat_in],
+        far=7,
+        limit=LIMIT1,
     )
     odd = lax.ppermute(out_odd, "narrow", swaps(n_narrow, 1))
     gathered = lax.all_gather(
         out_even, "narrow", axis_index_groups=[[i, i + 1] for i in range(0, n_narrow, 2)]
     )
-    sent_even, sent_odd, small = call(
-        narrow_kernel, [W_ROWS, W_ROWS, SMALL * TALL], [L], 10**6,
-        gathered, odd, p, sat, k, bs, small,
+    bs_middle, trans_middle, acc, frac, rate = call(
+        middle_kernel,
+        [(middle * K, L), (3, middle, L), (TALL, L), (cells, L), (cells, L)],
+        [
+            space(middle, L), space(middle * K, L, dtype=jnp.bfloat16), space(cells, L),
+            space(L, L), pltpu.SemaphoreType.DMA((3,)),
+        ],
+        10**7,
+        [src_in, basis_in, pore_in, p, perm, sat, small],
+        far=3,
+        limit=24,
+    )
+    sent_odd, sent_even, small = call(
+        narrow_kernel,
+        [(W_ROWS, L), (W_ROWS, L), (SMALL * TALL, L)],
+        [space(L, L)],
+        10**6,
+        [gathered, odd, p, sat, perm, bs, bs_middle, small, acc],
     )
     in_odd = lax.ppermute(sent_odd, "wide", swaps(n_wide, 1))
     in_even = lax.ppermute(sent_even, "wide", swaps(n_wide, 0))
     new, new_sat = call(
-        final_kernel, [NX * NY, NX * NY], [L], 10**7,
-        in_even, in_odd, sent_even, sent_odd, gathered, odd, small, p, sat, k, pore, bs,
+        final_kernel,
+        [(cells, L), (cells, L)],
+        [space(cells, L), space(cells, L), space(L, L), pltpu.SemaphoreType.DMA((5,))],
+        10**7,
+        [
+            in_odd, in_even, sent_odd, sent_even, gathered, odd, small, p, sat, perm, bs, trans,
+            bs_middle, trans_middle, frac, rate,
+        ],
+        out_spec=HBM,
     )
     return new.reshape(pressure.shape), new_sat.reshape(pressure.shape)
 

time: 37.9 us -> 31.2 us (0.82)
  the two profiles are of different devices: /device:TPU:161 before, /device:TPU:184 now
where the time goes in v2:
time: 31.2 us; the launch traced here: 31 us
  starting transfers between devices  10.2 us (33%)
  Pallas kernels  7.2 us (23%)
  blocking collectives  7.17 us (23%)
  waiting for transfers between devices  5.75 us (18%)
  between operations  0.67 us (2%)
    pallas_call x4, Pallas kernels, call(): pl.pallas_call(kernel, out_shape=shapes, in_specs=[HBM] * far + [VMEM] *...  7.2 us
    all_gather x1, blocking collectives, on_device(): lax.all_gather(out_even, 'narrow', axis_index_groups=[[i, i + 1] for i in...  7.17 us
    ppermute x1, starting transfers between devices, on_device(): in_odd = lax.ppermute(sent_odd, 'wide', swaps(n_wide, 1))  6.36 us
    ppermute x1, waiting for transfers between devices, on_device(): in_even = lax.ppermute(sent_even, 'wide', swaps(n_wide, 0))  3.12 us
    ppermute x1, waiting for transfers between devices, on_device(): in_odd = lax.ppermute(sent_odd, 'wide', swaps(n_wide, 1))  2.63 us
    ppermute x1, starting transfers between devices, on_device(): in_even = lax.ppermute(sent_even, 'wide', swaps(n_wide, 0))  1.92 us
    ppermute x1, starting transfers between devices, on_device(): odd = lax.ppermute(out_odd, 'narrow', swaps(n_narrow, 1))  1.92 us
  transfers between devices with their start and end apart: 3, of which 2 were waited for; matrix products, arithmetic and copies ran while one was open for 0% of the time, Pallas kernels for 5%

profile of v2, /device:TPU:184, one launch (start us, length us, event | category | flops | bytes accessed | tf_op | source)
XLA Modules:
  0.0 31.0 jit_solution(14613478070296089997)
XLA Ops:
  0.6 2.3 %shard_map.95 = (f32[328,128]{1,0:T(8,128)S(1)}, f32[328,128]{1,0:T(8,128)S(1)}, f32[448,128]{1,0:T(8,128)S(1)}, f32[512,128]{1,0:T(8,128)S(1)}, f32[3,512,128]{...) custom-call(f32[512,128]{1,0:T(8,128)} %bitcast.20, ...), custom_call_target="tpu_custom_call" | custom-call | flops 10000000 | bytes 5834752 | tf_op jit(solution)/shard_map/pallas_call | solution.py:457
  2.9 1.9 %collective-permute-start = (f32[328,128]{1,0:T(8,128)S(1)}, f32[328,128]{1,0:T(8,128)S(1)}, u32[]{:S(2)}, u32[]{:S(2)}) collective-permute-start(f32[328,128]{1,0:T(8,128)S(1)} %get-tuple-element.21), channel_id=1, source_target_pairs={{1,2},{3,4},{5,6},{2,1},{4,3},{6,5},{9,10},{11,12},{13,14},{10,9},... | collective-permute-start | bytes 503816 | tf_op jit(solution)/shard_map/ppermute | solution.py:499
  4.8 1.6 %shard_map.96 = (f32[768,128]{1,0:T(8,128)S(1)}, f32[3,192,128]{2,1,0:T(8,128)S(1)}, f32[32,128]{1,0:T(8,128)S(1)}, f32[512,128]{1,0:T(8,128)S(1)}, f32[512,128]{1,0:T(8,128)S(1)}) custom-call(f32[512,128]{1,0:T(8,128)} %bitcast.18, bf16[2048,128]{1,0:T(8,128)(2,1)} %bitcast.16, f32[512,128]{1,0:T(8,128)} %bitcast.22, f32[512,128]{1,0:T(8,128)S(1)} %get-tuple-element.22.p, ...), custom_call_target="tpu_custom_call" | custom-call | flops 10000000 | bytes 3817472 | tf_op jit(solution)/shard_map/pallas_call | solution.py:457
  6.4 7.2 %all-gather = f32[656,128]{1,0:T(8,128)S(1)} all-gather(f32[328,128]{1,0:T(8,128)S(1)} %get-tuple-element.20), channel_id=2, replica_groups={{0,1},{2,3},{4,5},{6,7},{8,9},{10,11},{12,13},{14,15},{16,17},{18,19},{..., dimensions={0}, use_global_device_ids=true | all-gather | bytes 503808 | tf_op jit(solution)/shard_map/all_gather | solution.py:500
  13.6 0.0 collective-permute-done.odd
  13.6 0.5 %shard_map.97 = (f32[240,128]{1,0:T(8,128)S(1)}, f32[240,128]{1,0:T(8,128)S(1)}, f32[448,128]{1,0:T(8,128)S(1)}) custom-call(f32[2,328,128]{2,1,0:T(8,128)S(1)} %bitcast.13, f32[328,128]{1,0:T(8,128)S(1)} %collective-permute-done.odd, f32[512,128]{1,0:T(8,128)S(1)} %get-tuple-element.22.p, f32[512,128]{1,0:T(8,128)S(1)} %get-tuple-element.23.sat, ...), custom_call_target="tpu_custom_call" | custom-call | flops 1000000 | bytes 3977216 | tf_op jit(solution)/shard_map/pallas_call | solution.py:457
  14.1 6.4 %collective-permute-start.1 = (f32[240,128]{1,0:T(8,128)S(1)}, f32[240,128]{1,0:T(8,128)S(1)}, u32[]{:S(2)}, u32[]{:S(2)}) collective-permute-start(f32[240,128]{1,0:T(8,128)S(1)} %get-tuple-element.29.sent_odd), channel_id=1, source_target_pairs={{8,16},{24,32},{40,48},{56,64},{72,80},{88,96},{104,112},{120,128}... | collective-permute-start | bytes 368648 | tf_op jit(solution)/shard_map/ppermute | solution.py:522
  20.5 1.9 %collective-permute-start.2 = (f32[240,128]{1,0:T(8,128)S(1)}, f32[240,128]{1,0:T(8,128)S(1)}, u32[]{:S(2)}, u32[]{:S(2)}) collective-permute-start(f32[240,128]{1,0:T(8,128)S(1)} %get-tuple-element.30.sent_even), channel_id=1, source_target_pairs={{0,8},{16,24},{32,40},{48,56},{64,72},{80,88},{96,104},{112,120},{... | collective-permute-start | bytes 368648 | tf_op jit(solution)/shard_map/ppermute | solution.py:523
  22.4 2.6 %collective-permute-done.1.in_odd = f32[240,128]{1,0:T(8,128)S(1)} collective-permute-done((f32[240,128]{1,0:T(8,128)S(1)}, f32[240,128]{1,0:T(8,128)S(1)}, u32[]{:S(2)}, u32[]{:S(2)}) %collective-permute-start.1) | collective-permute-done | bytes 122912 | tf_op jit(solution)/shard_map/ppermute | solution.py:522
  25.0 3.1 %collective-permute-done.2.in_even = f32[240,128]{1,0:T(8,128)S(1)} collective-permute-done((f32[240,128]{1,0:T(8,128)S(1)}, f32[240,128]{1,0:T(8,128)S(1)}, u32[]{:S(2)}, u32[]{:S(2)}) %collective-permute-start.2) | collective-permute-done | bytes 122912 | tf_op jit(solution)/shard_map/ppermute | solution.py:523
  28.1 2.9 %shard_map.98 = (f32[512,128]{1,0:T(8,128)}, f32[512,128]{1,0:T(8,128)}) custom-call(f32[240,128]{1,0:T(8,128)S(1)} %collective-permute-done.1.in_odd, f32[240,128]{1,0:T(8,128)S(1)} %collective-permute-done.2.in_even, f32[240,128]{1,0:T(8,128)S(1)} %get-tuple-element.29.sent_odd, f32[240,128]{1,0:T(8,128)S(1)} %get-tuple-element.30.sent_even, ...), custom_call_target="tpu_custom_call" | custom-call | flops 10000000 | bytes 6107136 | tf_op jit(solution)/shard_map/pallas_call | solution.py:457
Async XLA Ops:
  2.9 10.7 %collective-permute-start = (f32[328,128]{1,0:T(8,128)S(1)}, f32[328,128]{1,0:T(8,128)S(1)}, u32[]{:S(2)}, u32[]{:S(2)}) collective-permute-start(f32[328,128]{1,0:T(8,128)S(1)} %get-tuple-element.21), channel_id=1, source_target_pairs={{1,2},{3,4},{5,6},{2,1},{4,3},{6,5},{9,10},{11,12},{13,14},{10,9},... | collective-permute-start | bytes 503816 | tf_op jit(solution)/shard_map/ppermute | solution.py:499
  14.1 10.9 %collective-permute-start.1 = (f32[240,128]{1,0:T(8,128)S(1)}, f32[240,128]{1,0:T(8,128)S(1)}, u32[]{:S(2)}, u32[]{:S(2)}) collective-permute-start(f32[240,128]{1,0:T(8,128)S(1)} %get-tuple-element.29.sent_odd), channel_id=1, source_target_pairs={{8,16},{24,32},{40,48},{56,64},{72,80},{88,96},{104,112},{120,128}... | collective-permute-start | bytes 368648 | tf_op jit(solution)/shard_map/ppermute | solution.py:522
  20.5 7.7 %collective-permute-start.2 = (f32[240,128]{1,0:T(8,128)S(1)}, f32[240,128]{1,0:T(8,128)S(1)}, u32[]{:S(2)}, u32[]{:S(2)}) collective-permute-start(f32[240,128]{1,0:T(8,128)S(1)} %get-tuple-element.30.sent_even), channel_id=1, source_target_pairs={{0,8},{16,24},{32,40},{48,56},{64,72},{80,88},{96,104},{112,120},{... | collective-permute-start | bytes 368648 | tf_op jit(solution)/shard_map/ppermute | solution.py:523

commit v3 on v2

--- a/solution.py
+++ b/solution.py
@@ -309,11 +309,18 @@
     def after(lo, n):
         return jnp.where(even, gathered[mate, lo : lo + n, :], odd[lo : lo + n, :])
 
+    place = lax.axis_index("wide")
+    inside = jnp.logical_and(place > 0, place < lax.axis_size("wide") - 1)
+    odd_mate = jnp.where(wide_even, 0, 1)
+
+    def odd_side(lo, n):
+        return jnp.where(inside, in_odd[odd_mate, lo : lo + n, :], 0.0)
+
     def left(lo, n):
-        return jnp.where(wide_even, in_odd[lo : lo + n, :], in_even[lo : lo + n, :])
+        return jnp.where(wide_even, odd_side(lo, n), in_even[lo : lo + n, :])
 
     def right(lo, n):
-        return jnp.where(wide_even, in_even[lo : lo + n, :], in_odd[lo : lo + n, :])
+        return jnp.where(wide_even, in_even[lo : lo + n, :], odd_side(lo, n))
 
     def first(lo, n):
         return jnp.where(wide_even, sent_odd[lo : lo + n, :], sent_even[lo : lo + n, :])
@@ -519,8 +526,10 @@
         10**6,
         [gathered, odd, p, sat, perm, bs, bs_middle, small, acc],
     )
-    in_odd = lax.ppermute(sent_odd, "wide", swaps(n_wide, 1))
     in_even = lax.ppermute(sent_even, "wide", swaps(n_wide, 0))
+    in_odd = lax.all_gather(
+        sent_odd, "wide", axis_index_groups=[[i, (i + 1) % n_wide] for i in range(1, n_wide, 2)]
+    )
     new, new_sat = call(
         final_kernel,
         [(cells, L), (cells, L)],

time: 31.2 us -> 31.2 us (level)
  the two profiles are of different devices: /device:TPU:184 before, /device:TPU:160 now
where the time goes in v3:
time: 31.2 us; the launch traced here: 31 us
  blocking collectives  17.8 us (57%)
  Pallas kernels  7.19 us (23%)
  starting transfers between devices  5.32 us (17%)
  between operations  0.67 us (2%)
    all_gather x1, blocking collectives, on_device(): lax.all_gather(sent_odd, 'wide', axis_index_groups=[[i, (i + 1) % n_wide]...  10.6 us
    pallas_call x4, Pallas kernels, call(): pl.pallas_call(kernel, out_shape=shapes, in_specs=[HBM] * far + [VMEM] *...  7.19 us
    all_gather x1, blocking collectives, on_device(): lax.all_gather(out_even, 'narrow', axis_index_groups=[[i, i + 1] for i in...  7.17 us
    ppermute x1, starting transfers between devices, on_device(): in_even = lax.ppermute(sent_even, 'wide', swaps(n_wide, 0))  3.4 us
    ppermute x1, starting transfers between devices, on_device(): odd = lax.ppermute(out_odd, 'narrow', swaps(n_narrow, 1))  1.92 us
  transfers between devices with their start and end apart: 2, of which 0 were waited for; matrix products, arithmetic and copies ran while one was open for 0% of the time, Pallas kernels for 5%

profile of v3, /device:TPU:160, one launch (start us, length us, event | category | flops | bytes accessed | tf_op | source)
XLA Modules:
  0.0 31.0 jit_solution(5542042543659788717)
XLA Ops:
  0.6 2.3 %shard_map.95 = (f32[328,128]{1,0:T(8,128)S(1)}, f32[328,128]{1,0:T(8,128)S(1)}, f32[448,128]{1,0:T(8,128)S(1)}, f32[512,128]{1,0:T(8,128)S(1)}, f32[3,512,128]{...) custom-call(f32[512,128]{1,0:T(8,128)} %bitcast.22, ...), custom_call_target="tpu_custom_call" | custom-call | flops 10000000 | bytes 5834752 | tf_op jit(solution)/shard_map/pallas_call | solution.py:464
  2.9 1.9 %collective-permute-start = (f32[328,128]{1,0:T(8,128)S(1)}, f32[328,128]{1,0:T(8,128)S(1)}, u32[]{:S(2)}, u32[]{:S(2)}) collective-permute-start(f32[328,128]{1,0:T(8,128)S(1)} %get-tuple-element.21), channel_id=1, source_target_pairs={{1,2},{3,4},{5,6},{2,1},{4,3},{6,5},{9,10},{11,12},{13,14},{10,9},... | collective-permute-start | bytes 503816 | tf_op jit(solution)/shard_map/ppermute | solution.py:506
  4.8 1.5 %shard_map.96 = (f32[768,128]{1,0:T(8,128)S(1)}, f32[3,192,128]{2,1,0:T(8,128)S(1)}, f32[32,128]{1,0:T(8,128)S(1)}, f32[512,128]{1,0:T(8,128)S(1)}, f32[512,128]{1,0:T(8,128)S(1)}) custom-call(f32[512,128]{1,0:T(8,128)} %bitcast.20, bf16[2048,128]{1,0:T(8,128)(2,1)} %bitcast.18, f32[512,128]{1,0:T(8,128)} %bitcast.24, f32[512,128]{1,0:T(8,128)S(1)} %get-tuple-element.22.p, ...), custom_call_target="tpu_custom_call" | custom-call | flops 10000000 | bytes 3817472 | tf_op jit(solution)/shard_map/pallas_call | solution.py:464
  6.4 7.2 %all-gather = f32[656,128]{1,0:T(8,128)S(1)} all-gather(f32[328,128]{1,0:T(8,128)S(1)} %get-tuple-element.20), channel_id=2, replica_groups={{0,1},{2,3},{4,5},{6,7},{8,9},{10,11},{12,13},{14,15},{16,17},{18,19},{..., dimensions={0}, use_global_device_ids=true | all-gather | bytes 503808 | tf_op jit(solution)/shard_map/all_gather | solution.py:507
  13.6 0.0 collective-permute-done.odd
  13.6 0.5 %shard_map.97 = (f32[240,128]{1,0:T(8,128)S(1)}, f32[240,128]{1,0:T(8,128)S(1)}, f32[448,128]{1,0:T(8,128)S(1)}) custom-call(f32[2,328,128]{2,1,0:T(8,128)S(1)} %bitcast.14, f32[328,128]{1,0:T(8,128)S(1)} %collective-permute-done.odd, f32[512,128]{1,0:T(8,128)S(1)} %get-tuple-element.22.p, f32[512,128]{1,0:T(8,128)S(1)} %get-tuple-element.23.sat, ...), custom_call_target="tpu_custom_call" | custom-call | flops 1000000 | bytes 3977216 | tf_op jit(solution)/shard_map/pallas_call | solution.py:464
  14.1 3.4 %collective-permute-start.1 = (f32[240,128]{1,0:T(8,128)S(1)}, f32[240,128]{1,0:T(8,128)S(1)}, u32[]{:S(2)}, u32[]{:S(2)}) collective-permute-start(f32[240,128]{1,0:T(8,128)S(1)} %get-tuple-element.30.sent_even), channel_id=1, source_target_pairs={{0,8},{16,24},{32,40},{48,56},{64,72},{80,88},{96,104},{112,120},{... | collective-permute-start | bytes 368648 | tf_op jit(solution)/shard_map/ppermute | solution.py:529
  17.5 10.6 %all-gather.1 = f32[480,128]{1,0:T(8,128)S(1)} all-gather(f32[240,128]{1,0:T(8,128)S(1)} %get-tuple-element.29.sent_odd), channel_id=3, replica_groups={{8,16},{24,32},{40,48},{56,64},{72,80},{88,96},{104,112},{120,128},{136..., dimensions={0}, use_global_device_ids=true | all-gather | bytes 368640 | tf_op jit(solution)/shard_map/all_gather | solution.py:530
  28.1 0.0 collective-permute-done.1.in_even
  28.1 2.9 %shard_map.98 = (f32[512,128]{1,0:T(8,128)}, f32[512,128]{1,0:T(8,128)}) custom-call(f32[2,240,128]{2,1,0:T(8,128)S(1)} %bitcast.16, f32[240,128]{1,0:T(8,128)S(1)} %collective-permute-done.1.in_even, f32[240,128]{1,0:T(8,128)S(1)} %get-tuple-element.29.sent_odd, f32[240,128]{1,0:T(8,128)S(1)} %get-tuple-element.30.sent_even, f32[2,328,128]{2,1,0:T(8,128)S(1)} %bitcast.15, ...), custom_call_target="tpu_custom_call" | custom-call | flops 10000000 | bytes 6230016 | tf_op jit(solution)/shard_map/pallas_call | solution.py:464
Async XLA Ops:
  2.9 10.7 %collective-permute-start = (f32[328,128]{1,0:T(8,128)S(1)}, f32[328,128]{1,0:T(8,128)S(1)}, u32[]{:S(2)}, u32[]{:S(2)}) collective-permute-start(f32[328,128]{1,0:T(8,128)S(1)} %get-tuple-element.21), channel_id=1, source_target_pairs={{1,2},{3,4},{5,6},{2,1},{4,3},{6,5},{9,10},{11,12},{13,14},{10,9},... | collective-permute-start | bytes 503816 | tf_op jit(solution)/shard_map/ppermute | solution.py:506
  14.1 14.1 %collective-permute-start.1 = (f32[240,128]{1,0:T(8,128)S(1)}, f32[240,128]{1,0:T(8,128)S(1)}, u32[]{:S(2)}, u32[]{:S(2)}) collective-permute-start(f32[240,128]{1,0:T(8,128)S(1)} %get-tuple-element.30.sent_even), channel_id=1, source_target_pairs={{0,8},{16,24},{32,40},{48,56},{64,72},{80,88},{96,104},{112,120},{... | collective-permute-start | bytes 368648 | tf_op jit(solution)/shard_map/ppermute | solution.py:529

commit v4 on v2

--- a/solution.py
+++ b/solution.py
@@ -19,9 +19,12 @@
 N_P, N_K, N_S, N_B, N_C = 0, 32, 64, 96, 224
 N_SMALL = 288
 N_ROWS = N_SMALL + 8 * 5
-W_SAT = FIELDS * TALL
-W_SMALL = W_SAT + NX
-W_ROWS = W_SMALL + TALL
+COLUMN = NX + 2 * EDGE
+MARGIN = TOP - EDGE
+W_SAT = 0
+W_FIELD = NX
+W_SMALL = W_FIELD + FIELDS * COLUMN
+W_ROWS = W_SMALL + COLUMN + 10
 
 
 def roll(a, shift, axis):
@@ -45,6 +48,11 @@
 
 def lane_sum(a):
     return jnp.sum(a, axis=-1, keepdims=True)
+
+
+def halves(a):
+    high = a.astype(jnp.bfloat16)
+    return high, (a - high.astype(jnp.float32)).astype(jnp.bfloat16)
 
 
 def bin_pieces(sup, pieces):
@@ -74,22 +82,20 @@
     rows, lanes = iota((NY, L), 0), iota((NY, L), 1)
 
     def face(x):
-        a, b = slice(x * NY, (x + 1) * NY), slice((x + 1) * NY, (x + 2) * NY)
+        a, b = slice((x - base) * NY, (x - base + 1) * NY), slice((x - base + 1) * NY, (x - base + 2) * NY)
         value = trans_of(perm[0, a, :], perm[0, b, :])
-        if x >= lo:
-            trans[0, (x - base) * NY : (x - base + 1) * NY, :] = value
+        trans[0, a, :] = value
         return value * (p[a, :] - p[b, :])
 
     result = []
     last = face(lo - 1) if lo > 0 else None
     for x in range(lo, hi):
-        at = slice(x * NY, (x + 1) * NY)
+        at = slice((x - base) * NY, (x - base + 1) * NY)
         here, ky, kz = p[at, :], perm[1, at, :], perm[2, at, :]
         ty = jnp.where(rows < NY - 1, trans_of(ky, roll(ky, -1, 0)), 0.0)
         tz = jnp.where(lanes < L - 1, trans_of(kz, roll(kz, -1, 1)), 0.0)
-        to = slice((x - base) * NY, (x - base + 1) * NY)
-        trans[1, to, :] = ty
-        trans[2, to, :] = tz
+        trans[1, at, :] = ty
+        trans[2, at, :] = tz
         fy = ty * (here - roll(here, -1, 0))
         fz = tz * (here - roll(here, -1, 1))
         total = (fy - roll(fy, 1, 0)) + (fz - roll(fz, 1, 1))
@@ -99,16 +105,17 @@
         if x < NX - 1:
             last = face(x)
             total = total + last
-        result.append(src[to, :] - total)
+        result.append(src[at, :] - total)
     return result
 
 
-def add_pieces(pieces, residuals, lo, bs, base):
+def add_pieces(pieces, residuals, lo, mixed, bs, base):
     lanes = iota((NY, L), 1)
     for i, res in enumerate(residuals):
         x = lo + i
         for k in range(K):
-            b = bs[pl.ds((x - base) * NY * K + k, NY, stride=K), :]
+            b = mixed[pl.ds((x - base) * NY * K + k, NY, stride=K), :]
+            bs[k, (x - base) * NY : (x - base + 1) * NY, :] = b
             pieces = jnp.where(lanes == k * TALL + TOP + x, lane_sum(b * res), pieces)
     return pieces
 
@@ -118,7 +125,6 @@
     return [flipped[k * TALL : (k + 1) * TALL, :] for k in range(K)]
 
 
-LIMIT1 = 24
 LOW, HIGH = EDGE, NX - EDGE
 
 
@@ -131,22 +137,21 @@
 
 def edge_kernel(
     p_in, perm_in, src_in, basis_in, support_in, matrix_in, sat_in,
-    out_even, out_odd, small, p, perm, sat, bs, trans,
-    src, basis, support, matrix, place, square, sems,
+    out_even, out_odd, small, p, perm, bs, trans, basis,
+    src, mixed, support, matrix, place, square, sems,
 ):
     even = lax.axis_index("narrow") % 2 == 0
-    top, bottom, middle = (
-        pl.ds(0, (LOW + 1) * NY),
-        pl.ds((HIGH - 1) * NY, (LOW + 1) * NY),
-        pl.ds((LOW + 1) * NY, (HIGH - LOW - 2) * NY),
-    )
+    rows_even = pl.ds(pl.multiple_of(jnp.where(even, NX - 1, 0) * NY, NY), NY)
+    rows_odd = pl.ds(pl.multiple_of(jnp.where(even, 0, NX - 1) * NY, NY), NY)
     pairs = []
-    for part, first in ((top, 0), (bottom, HIGH)):
+    for near, first in ((0, 0), (HIGH - 1, HIGH)):
+        part = pl.ds(near * NY, (EDGE + 1) * NY)
         own, fine = pl.ds(first * NY, EDGE * NY), pl.ds(first * NY * K, EDGE * NY * K)
         pairs += [(p_in.at[part], p.at[part]), (perm_in.at[:, part], perm.at[:, part])]
         pairs += [(src_in.at[own], src.at[own]), (basis_in.at[fine], basis.at[fine])]
-    pairs += [(support_in, support), (matrix_in, matrix), (sat_in, sat)]
-    pairs += [(p_in.at[middle], p.at[middle]), (perm_in.at[:, middle], perm.at[:, middle])]
+    pairs += [(support_in, support), (matrix_in, matrix)]
+    pairs += [(sat_in.at[rows_even], out_even.at[pl.ds(N_S, NY)])]
+    pairs += [(sat_in.at[rows_odd], out_odd.at[pl.ds(N_S, NY)])]
     copies = copies_of(sems, pairs)
     pieces = jnp.zeros((NY, L), jnp.float32)
     for i, first in enumerate((0, HIGH)):
@@ -155,8 +160,8 @@
         residuals = rows_residual(p, perm, src, trans, first, first + EDGE, 0)
         copies[4 * i + 3].wait()
         fine = slice(first * NY * K, (first + EDGE) * NY * K)
-        bs[fine, :] = basis[fine, :].astype(jnp.float32)
-        pieces = add_pieces(pieces, residuals, first, bs, 0)
+        mixed[fine, :] = basis[fine, :].astype(jnp.float32)
+        pieces = add_pieces(pieces, residuals, first, mixed, bs, 0)
     pieces = split_pieces(square, pieces)
     copies[8].wait()
     copies[9].wait()
@@ -173,21 +178,19 @@
     stack.append(acc)
     for i in range(SMALL):
         small[i * TALL : (i + 1) * TALL, :] = stack[i]
-    copies[10].wait()
     for out, takes_last in ((out_even, even), (out_odd, jnp.logical_not(even))):
         edge = jnp.where(takes_last, NX - 1, 0)
         row = pl.multiple_of(edge * NY, NY)
         out[N_P : N_P + NY, :] = p[pl.ds(row, NY), :]
         out[N_K : N_K + NY, :] = perm[0, pl.ds(row, NY), :]
-        out[N_S : N_S + NY, :] = sat[pl.ds(row, NY), :]
         for k in range(K):
-            out[N_B + k * NY : N_B + (k + 1) * NY, :] = bs[pl.ds(row * K + k, NY, stride=K), :]
+            out[N_B + k * NY : N_B + (k + 1) * NY, :] = bs[k, pl.ds(row, NY), :]
         start = jnp.where(takes_last, NX - EDGE, 0) * NY
         for c, col in enumerate((0, NY - 1)):
             fields = [
                 p[pl.ds(start + col, EDGE, stride=NY), :],
                 perm[1, pl.ds(start + col, EDGE, stride=NY), :],
-            ] + [bs[pl.ds((start + col) * K + k, EDGE, stride=NY * K), :] for k in range(K)]
+            ] + [bs[k, pl.ds(start + col, EDGE, stride=NY), :] for k in range(K)]
             for f, value in enumerate(fields):
                 to = N_C + (f * 2 + c) * EDGE
                 out[to : to + EDGE, :] = value
@@ -196,31 +199,41 @@
         for i in range(5):
             a, b, c = window[3 * i : 3 * i + 3]
             out[N_SMALL + 8 * i : N_SMALL + 8 * i + 8, :] = a + roll(b, 40, 1) + roll(c, 80, 1)
+    copies[10].wait()
     copies[11].wait()
-    copies[12].wait()
 
 
 def middle_kernel(
-    src_in, basis_in, pore_in, p, perm, sat, small,
-    bs, trans, acc, frac, rate,
-    src, basis, pore, square, sems,
+    p_in, perm_in, src_in, basis_in, sat_in, pore_in, small,
+    p, perm, bs, trans, acc, sat, frac, rate, basis,
+    src, mixed, pore, square, sems,
 ):
+    near = pl.ds((LOW - 1) * NY, (HIGH - LOW + 2) * NY)
     own, fine = pl.ds(LOW * NY, (HIGH - LOW) * NY), pl.ds(LOW * NY * K, (HIGH - LOW) * NY * K)
-    copies = copies_of(sems, [(src_in.at[own], src), (basis_in.at[fine], basis), (pore_in, pore)])
-    frac[...] = fraction(sat[...])
-    copies[0].wait()
-    residuals = rows_residual(p, perm, src, trans, LOW, HIGH, LOW)
-    copies[1].wait()
-    bs[...] = basis[...].astype(jnp.float32)
-    pieces = add_pieces(jnp.zeros((NY, L), jnp.float32), residuals, LOW, bs, LOW)
+    inner = pl.ds(NY, (HIGH - LOW) * NY)
+    copies = copies_of(
+        sems,
+        [
+            (p_in.at[near], p), (perm_in.at[:, near], perm), (src_in.at[own], src.at[inner]),
+            (basis_in.at[fine], basis), (sat_in, sat), (pore_in, pore),
+        ],
+    )
+    for copy in copies[:3]:
+        copy.wait()
+    residuals = rows_residual(p, perm, src, trans, LOW, HIGH, LOW - 1)
+    copies[3].wait()
+    mixed[...] = basis[...].astype(jnp.float32)
+    pieces = add_pieces(jnp.zeros((NY, L), jnp.float32), residuals, LOW, mixed, bs, LOW)
     sup = [small[k * TALL : (k + 1) * TALL, :] for k in range(K)]
     acc[...] = bin_pieces(sup, split_pieces(square, pieces))
-    copies[2].wait()
+    copies[4].wait()
+    frac[...] = fraction(sat[...])
+    copies[5].wait()
     rate[...] = DT / pore[...]
 
 
 def narrow_kernel(
-    gathered, odd, p, sat, perm, bs, bs_middle, small, acc_middle, out_odd, out_even, small_out, square
+    gathered, odd, p, perm, bs, p_middle, perm_middle, bs_middle, sat, small, acc_middle, out_odd, out_even, small_out, square
 ):
     even = lax.axis_index("narrow") % 2 == 0
     wide_even = lax.axis_index("wide") % 2 == 0
@@ -257,7 +270,7 @@
         at = x * NY
         flux = trans_of(perm[0, at : at + NY, :], get(N_K, NY)) * (p[at : at + NY, :] - get(N_P, NY))
         for k in range(K):
-            mine = lane_sum(bs[pl.ds(at * K + k, NY, stride=K), :] * -flux)
+            mine = lane_sum(bs[k, at : at + NY, :] * -flux)
             pieces = jnp.where(lanes == k * TALL + TOP + x, mine, pieces)
             other = lane_sum(get(N_B + k * NY, NY) * flux)
             pieces = jnp.where(lanes == k * TALL + TOP + other_x, other, pieces)
@@ -270,32 +283,33 @@
     for i in range(SMALL):
         first = jnp.where(slot == i, roll(stack[i], 8 * i, 1), first)
         last = jnp.where(slot == i, roll(stack[i], 8 * i - 32, 1), last)
-    blank = jnp.zeros((8, L), jnp.float32)
     for out, takes_last in ((out_even, wide_even), (out_odd, jnp.logical_not(wide_even))):
         col = jnp.where(takes_last, NY - 1, 0)
         for f in range(FIELDS):
-            base = f * TALL
+            base = W_FIELD + f * COLUMN
             lo = N_C + f * 2 * EDGE
-            out[base : base + 8, :] = blank
-            out[base + 24 : base + 32, :] = blank
-            out[base + 3 : base + 8, :] = jnp.where(takes_last, before(lo + EDGE, EDGE), before(lo, EDGE))
-            if f < 2:
-                field = p[pl.ds(col, NX, stride=NY), :] if f == 0 else perm[1, pl.ds(col, NX, stride=NY), :]
-                out[base + TOP : base + TOP + NX, :] = field
-            else:
-                at = col * K + f - 2
-                for ref, x, start, n in (
-                    (bs, 0, 0, LOW), (bs_middle, LOW, 0, HIGH - LOW), (bs, HIGH, HIGH, NX - HIGH)
-                ):
-                    column = ref[pl.ds(start * NY * K + at, n, stride=NY * K), :]
-                    out[base + TOP + x : base + TOP + x + n, :] = column
-            out[base + 24 : base + 29, :] = jnp.where(takes_last, after(lo + EDGE, EDGE), after(lo, EDGE))
+            out[base : base + EDGE, :] = jnp.where(takes_last, before(lo + EDGE, EDGE), before(lo, EDGE))
+            base += EDGE
+            for middle, x, n in ((False, 0, LOW), (True, LOW, HIGH - LOW), (False, HIGH, NX - HIGH)):
+                rows = pl.ds((x - LOW) * NY + col if middle else x * NY + col, n, stride=NY)
+                after_first = pl.ds((x - LOW + 1) * NY + col if middle else x * NY + col, n, stride=NY)
+                if f == 0:
+                    column = (p_middle if middle else p)[after_first, :]
+                elif f == 1:
+                    column = (perm_middle if middle else perm)[1, after_first, :]
+                else:
+                    column = (bs_middle if middle else bs)[f - 2, rows, :]
+                out[base + x : base + x + n, :] = column
+            base += NX
+            out[base : base + EDGE, :] = jnp.where(takes_last, after(lo + EDGE, EDGE), after(lo, EDGE))
         out[W_SAT : W_SAT + NX, :] = sat[pl.ds(col, NX, stride=NY), :]
-        out[W_SMALL : W_SMALL + TALL, :] = jnp.where(takes_last, last, first)
+        out[W_SMALL : W_SMALL + COLUMN, :] = jnp.where(takes_last, last, first)[MARGIN : MARGIN + COLUMN, :]
+        out[W_SMALL + COLUMN : W_ROWS, :] = jnp.zeros((W_ROWS - W_SMALL - COLUMN, L), jnp.float32)
 
 
 def final_kernel(
-    in_odd, in_even, sent_odd, sent_even, gathered, odd, small, p, sat, perm, bs, trans, bs_middle, trans_middle, frac, rate,
+    in_odd, in_even, sent_odd, sent_even, gathered, odd, small, p, perm, basis, trans,
+    p_middle, basis_middle, trans_middle, sat, frac, rate,
     new_out, new_sat_out,
     new, new_sat, square, sems,
 ):
@@ -322,7 +336,16 @@
         return jnp.where(wide_even, sent_even[lo : lo + n, :], sent_odd[lo : lo + n, :])
 
     lane = iota((TALL, L), 1)
-    from_left, from_right = left(W_SMALL, TALL), right(W_SMALL, TALL)
+    row = iota((TALL, L), 0)
+    sent = jnp.logical_and(row >= MARGIN, row < MARGIN + COLUMN)
+
+    def column_of(get, f):
+        return get(W_FIELD + f * COLUMN - MARGIN, TALL)
+
+    def own_rows(get, f):
+        return get(W_FIELD + f * COLUMN + EDGE, NX)
+
+    from_left, from_right = (jnp.where(sent, column_of(get, FIELDS), 0.0) for get in (left, right))
     stack = []
     for i in range(SMALL):
         own = small[i * TALL : (i + 1) * TALL, :]
@@ -332,13 +355,14 @@
     sup, mat = stack[:K], stack[MAT : MAT + 9]
     pieces = [jnp.zeros((TALL, L), jnp.float32)] * K
     for mine, other, y, other_y in ((first, left, 0, -1), (last, right, NY - 1, NY)):
-        k_here, k_there = mine(TALL, TALL), other(TALL, TALL)
+        k_here, k_there = column_of(mine, 1), column_of(other, 1)
         total = k_here + k_there
-        flux = (2.0 * k_here * k_there / jnp.where(total > 0, total, 1.0)) * (mine(0, TALL) - other(0, TALL))
+        flux = (2.0 * k_here * k_there / jnp.where(total > 0, total, 1.0)) * (
+            column_of(mine, 0) - column_of(other, 0)
+        )
         for k in range(K):
-            lo = (2 + k) * TALL
-            here = lane_sum(mine(lo, TALL) * -flux)
-            there = lane_sum(other(lo, TALL) * flux)
+            here = lane_sum(column_of(mine, 2 + k) * -flux)
+            there = lane_sum(column_of(other, 2 + k) * flux)
             pieces[k] = jnp.where(lane == WEST + y, here, pieces[k])
             pieces[k] = jnp.where(lane == WEST + other_y, there, pieces[k])
     res = stack[ACC] + bin_pieces(sup, pieces)
@@ -362,34 +386,46 @@
         for o in range(9):
             total = jnp.where(sup[k] == float(o), shifts[o], total)
         picked.append(total)
+    spread = jnp.zeros((TALL, L), jnp.float32)
     for k in range(K):
-        square[k * TALL : (k + 1) * TALL, :] = roll(picked[k], -WEST, 1)
-    weights = square[...].T[0:NY, :]
-
-    def weight(k, x):
-        at = k * TALL + TOP + x
-        return weights[:, at : at + 1]
-
+        spread = jnp.where(lane // NY == k, roll(picked[k], k * NY - WEST, 1), spread)
+    spread = jnp.concatenate(halves(spread), axis=0)
+    source = iota((L, L), 0)
+    reorder = iota((L, L), 1) == (source % NY) * K + source // NY
+    square[0 : 2 * TALL, :] = jnp.dot(
+        spread, reorder.astype(jnp.bfloat16), preferred_element_type=jnp.float32
+    )
+    square[2 * TALL :, :] = spread.astype(jnp.float32)
+    rows, lanes = iota((NY, L), 0), iota((NY, L), 1)
+
+    def prolonged(values, start, x, mine):
+        parts = []
+        for at in (start, start + TALL):
+            parts.append(jnp.where(mine, square[at + TOP + x : at + TOP + x + 1, :], 0.0))
+        weights = jnp.concatenate(parts, axis=0).astype(jnp.bfloat16)
+        both = jnp.dot(weights, values, preferred_element_type=jnp.float32)
+        return both[:NY, :] + both[NY:, :]
+
+    own = lanes // K == rows
     for x in range(NX):
         at = slice(x * NY, (x + 1) * NY)
-        total = p[at, :]
-        ref, base = (bs_middle, LOW) if LOW <= x < HIGH else (bs, 0)
-        for k in range(K):
-            total = total + ref[pl.ds((x - base) * NY * K + k, NY, stride=K), :] * weight(k, x)
-        new[at, :] = total
+        inner = LOW <= x < HIGH
+        before_x = p_middle[(x - LOW + 1) * NY : (x - LOW + 2) * NY, :] if inner else p[at, :]
+        ref, base = (basis_middle, LOW) if inner else (basis, 0)
+        values = ref[(x - base) * NY * K : (x - base + 1) * NY * K, :]
+        new[at, :] = before_x + prolonged(values, 0, x, own)
     copies = copies_of(sems, [(new, new_out)])
     ends = []
+    own = lanes % NY == rows
     for get, x in ((before, -1), (after, NX)):
-        total = get(N_P, NY)
-        for k in range(K):
-            total = total + get(N_B + k * NY, NY) * weight(k, x)
-        ends.append(total)
+        values = get(N_B, K * NY).astype(jnp.bfloat16)
+        ends.append(get(N_P, NY) + prolonged(values, 2 * TALL, x, own))
     sides = []
     for get, y in ((left, -1), (right, NY)):
-        total = get(TOP, NX)
+        total = own_rows(get, 0)
         for k in range(K):
             column = picked[k][TOP : TOP + NX, WEST + y : WEST + y + 1]
-            total = total + get((2 + k) * TALL + TOP, NX) * column
+            total = total + own_rows(get, 2 + k) * column
         sides.append(total)
 
     def carried(value, here, there, f_here, f_there):
@@ -397,15 +433,14 @@
         return flux * jnp.where(flux > 0, f_here, f_there)
 
     west_f, east_f = fraction(left(W_SAT, NX)), fraction(right(W_SAT, NX))
-    east_t = trans_of(perm[1, pl.ds(NY - 1, NX, stride=NY), :], right(TALL + TOP, NX))
+    east_t = trans_of(own_rows(last, 1), own_rows(right, 1))
     west_flow = carried(
-        trans_of(perm[1, pl.ds(0, NX, stride=NY), :], left(TALL + TOP, NX)),
+        trans_of(own_rows(first, 1), own_rows(left, 1)),
         sides[0],
         new[pl.ds(0, NX, stride=NY), :],
         west_f,
         frac[pl.ds(0, NX, stride=NY), :],
     )
-    rows = iota((NY, L), 0)
     end = rows == NY - 1
     p_here, f_here = new[0:NY, :], frac[0:NY, :]
     flow_in = carried(
@@ -413,7 +448,7 @@
     )
     for x in range(NX):
         at = slice(x * NY, (x + 1) * NY)
-        ref, base = (trans_middle, LOW) if LOW <= x < HIGH else (trans, 0)
+        ref, base = (trans_middle, LOW - 1) if LOW <= x < HIGH else (trans, 0)
         tx, ty, tz = (ref[c, (x - base) * NY : (x - base + 1) * NY, :] for c in range(3))
         if x < NX - 1:
             nxt = slice((x + 1) * NY, (x + 2) * NY)
@@ -450,17 +485,17 @@
 HBM = pl.BlockSpec(memory_space=pltpu.HBM)
 
 
-def call(kernel, outs, scratch, flops, args, far=0, out_spec=VMEM, limit=24):
+def call(kernel, outs, scratch, flops, args, far=0, out_spec=VMEM):
     args = [pltpu.with_memory_space_constraint(a, pltpu.HBM) for a in args[:far]] + args[far:]
-    shapes = [jax.ShapeDtypeStruct(shape, jnp.float32) for shape in outs]
-    size = sum(a.size * a.dtype.itemsize for a in args) + sum(4 * a.size for a in shapes)
+    shapes = [jax.ShapeDtypeStruct(o[:-1], o[-1]) if isinstance(o[-1], type) else jax.ShapeDtypeStruct(o, jnp.float32) for o in outs]
+    size = sum(a.size * a.dtype.itemsize for a in [*args, *shapes])
     return pl.pallas_call(
         kernel,
         out_shape=shapes,
         in_specs=[HBM] * far + [VMEM] * (len(args) - far),
         out_specs=[out_spec] * len(shapes),
         scratch_shapes=scratch,
-        compiler_params=pltpu.CompilerParams(vmem_limit_bytes=limit * 1024 * 1024),
+        compiler_params=pltpu.CompilerParams(vmem_limit_bytes=24 * 1024 * 1024),
         cost_estimate=pl.CostEstimate(flops=flops, bytes_accessed=size, transcendentals=0),
     )(*args)
 
@@ -484,40 +519,43 @@
     matrix = matrix.reshape(9 * NX, NY)
     n_narrow, n_wide = lax.axis_size("narrow"), lax.axis_size("wide")
     cells, fine, middle = NX * NY, NX * NY * K, (HIGH - LOW) * NY
-    out_even, out_odd, small, p, perm, sat, bs, trans = call(
+    near = middle + 2 * NY
+    out_even, out_odd, small, p, perm, bs, trans, basis = call(
         edge_kernel,
-        [(N_ROWS, L), (N_ROWS, L), (SMALL * TALL, L), (cells, L), (3, cells, L), (cells, L), (fine, L), (3, cells, L)],
+        [(N_ROWS, L), (N_ROWS, L), (SMALL * TALL, L), (cells, L), (3, cells, L), (K, cells, L), (3, cells, L),
+         (fine, L, jnp.bfloat16)],
         [
-            space(cells, L), space(fine, L, dtype=jnp.bfloat16), space(NX * K, NY, dtype=jnp.int32), space(9 * NX, NY),
-            space(TALL, L), space(L, L), pltpu.SemaphoreType.DMA((13,)),
+            space(cells, L), space(fine, L), space(NX * K, NY, dtype=jnp.int32),
+            space(9 * NX, NY), space(TALL, L), space(L, L), pltpu.SemaphoreType.DMA((12,)),
         ],
         10**7,
         [p_in, perm_in, src_in, basis_in, support, matrix, sat_in],
         far=7,
-        limit=LIMIT1,
     )
     odd = lax.ppermute(out_odd, "narrow", swaps(n_narrow, 1))
     gathered = lax.all_gather(
         out_even, "narrow", axis_index_groups=[[i, i + 1] for i in range(0, n_narrow, 2)]
     )
-    bs_middle, trans_middle, acc, frac, rate = call(
+    p_middle, perm_middle, bs_middle, trans_middle, acc, sat, frac, rate, basis_middle = call(
         middle_kernel,
-        [(middle * K, L), (3, middle, L), (TALL, L), (cells, L), (cells, L)],
         [
-            space(middle, L), space(middle * K, L, dtype=jnp.bfloat16), space(cells, L),
-            space(L, L), pltpu.SemaphoreType.DMA((3,)),
+            (near, L), (3, near, L), (K, middle, L), (3, near, L), (TALL, L), (cells, L), (cells, L), (cells, L),
+            (middle * K, L, jnp.bfloat16),
+        ],
+        [
+            space(near, L), space(middle * K, L), space(cells, L),
+            space(L, L), pltpu.SemaphoreType.DMA((6,)),
         ],
         10**7,
-        [src_in, basis_in, pore_in, p, perm, sat, small],
-        far=3,
-        limit=24,
+        [p_in, perm_in, src_in, basis_in, sat_in, pore_in, small],
+        far=6,
     )
     sent_odd, sent_even, small = call(
         narrow_kernel,
         [(W_ROWS, L), (W_ROWS, L), (SMALL * TALL, L)],
         [space(L, L)],
         10**6,
-        [gathered, odd, p, sat, perm, bs, bs_middle, small, acc],
+        [gathered, odd, p, perm, bs, p_middle, perm_middle, bs_middle, sat, small, acc],
     )
     in_odd = lax.ppermute(sent_odd, "wide", swaps(n_wide, 1))
     in_even = lax.ppermute(sent_even, "wide", swaps(n_wide, 0))
@@ -527,8 +565,8 @@
         [space(cells, L), space(cells, L), space(L, L), pltpu.SemaphoreType.DMA((5,))],
         10**7,
         [
-            in_odd, in_even, sent_odd, sent_even, gathered, odd, small, p, sat, perm, bs, trans,
-            bs_middle, trans_middle, frac, rate,
+            in_odd, in_even, sent_odd, sent_even, gathered, odd, small, p, perm, basis, trans,
+            p_middle, basis_middle, trans_middle, sat, frac, rate,
         ],
         out_spec=HBM,
     )

time: 31.2 us -> 30.1 us (0.965)
  the two profiles are of different devices: /device:TPU:184 before, /device:TPU:176 now
where the time goes in v4:
time: 30.1 us; the launch traced here: 29.9 us
  starting transfers between devices  10.2 us (34%)
  blocking collectives  7.17 us (24%)
  Pallas kernels  6.8 us (23%)
  waiting for transfers between devices  5.07 us (17%)
  between operations  0.67 us (2%)
    all_gather x1, blocking collectives, on_device(): lax.all_gather(out_even, 'narrow', axis_index_groups=[[i, i + 1] for i in...  7.17 us
    pallas_call x4, Pallas kernels, call(): pl.pallas_call(kernel, out_shape=shapes, in_specs=[HBM] * far + [VMEM] *...  6.8 us
    ppermute x1, starting transfers between devices, on_device(): in_odd = lax.ppermute(sent_odd, 'wide', swaps(n_wide, 1))  6.36 us
    ppermute x1, waiting for transfers between devices, on_device(): in_even = lax.ppermute(sent_even, 'wide', swaps(n_wide, 0))  3.12 us
    ppermute x1, waiting for transfers between devices, on_device(): in_odd = lax.ppermute(sent_odd, 'wide', swaps(n_wide, 1))  1.95 us
    ppermute x1, starting transfers between devices, on_device(): odd = lax.ppermute(out_odd, 'narrow', swaps(n_narrow, 1))  1.92 us
    ppermute x1, starting transfers between devices, on_device(): in_even = lax.ppermute(sent_even, 'wide', swaps(n_wide, 0))  1.92 us
  transfers between devices with their start and end apart: 3, of which 2 were waited for; matrix products, arithmetic and copies ran while one was open for 0% of the time, Pallas kernels for 6%

profile of v4, /device:TPU:176, one launch (start us, length us, event | category | flops | bytes accessed | tf_op | source)
XLA Modules:
  0.0 29.9 jit_solution(13556132042747977785)
XLA Ops:
  0.6 2.3 %shard_map.95 = (f32[328,128]{1,0:T(8,128)S(1)}, f32[328,128]{1,0:T(8,128)S(1)}, f32[448,128]{1,0:T(8,128)S(1)}, f32[512,128]{1,0:T(8,128)S(1)}, f32[3,512,128]{...) custom-call(f32[512,128]{1,0:T(8,128)} %bitcast.19, ...), custom_call_target="tpu_custom_call" | custom-call | flops 10000000 | bytes 6096896 | tf_op jit(solution)/shard_map/pallas_call | solution.py:492
  3.0 1.9 %collective-permute-start = (f32[328,128]{1,0:T(8,128)S(1)}, f32[328,128]{1,0:T(8,128)S(1)}, u32[]{:S(2)}, u32[]{:S(2)}) collective-permute-start(f32[328,128]{1,0:T(8,128)S(1)} %get-tuple-element.25), channel_id=1, source_target_pairs={{1,2},{3,4},{5,6},{2,1},{4,3},{6,5},{9,10},{11,12},{13,14},{10,9},... | collective-permute-start | bytes 503816 | tf_op jit(solution)/shard_map/ppermute | solution.py:535
  4.9 1.9 %shard_map.96 = (f32[256,128]{1,0:T(8,128)S(1)}, f32[3,256,128]{2,1,0:T(8,128)S(1)}, f32[4,192,128]{2,1,0:T(8,128)S(1)}, f32[3,256,128]{2,1,0:T(8,128)S(1)}, f32...) custom-call(f32[512,128]{1,0:T(8,128)} %bitcast.20, ...), custom_call_target="tpu_custom_call" | custom-call | flops 10000000 | bytes 4898816 | tf_op jit(solution)/shard_map/pallas_call | solution.py:492
  6.8 7.2 %all-gather = f32[656,128]{1,0:T(8,128)S(1)} all-gather(f32[328,128]{1,0:T(8,128)S(1)} %get-tuple-element.24), channel_id=2, replica_groups={{0,1},{2,3},{4,5},{6,7},{8,9},{10,11},{12,13},{14,15},{16,17},{18,19},{..., dimensions={0}, use_global_device_ids=true | all-gather | bytes 503808 | tf_op jit(solution)/shard_map/all_gather | solution.py:536
  14.0 0.0 collective-permute-done.odd
  14.0 0.6 %shard_map.97 = (f32[208,128]{1,0:T(8,128)S(1)}, f32[208,128]{1,0:T(8,128)S(1)}, f32[448,128]{1,0:T(8,128)S(1)}) custom-call(f32[2,328,128]{2,1,0:T(8,128)S(1)} %bitcast.13, f32[328,128]{1,0:T(8,128)S(1)} %collective-permute-done.odd, f32[512,128]{1,0:T(8,128)S(1)} %get-tuple-element.26.p, f32[3,512,128]{2,1,0:T(8,128)S(1)} %get-tuple-element.27.perm, ...), custom_call_target="tpu_custom_call" | custom-call | flops 1000000 | bytes 4468736 | tf_op jit(solution)/shard_map/pallas_call | solution.py:492
  14.5 6.4 %collective-permute-start.1 = (f32[208,128]{1,0:T(8,128)S(1)}, f32[208,128]{1,0:T(8,128)S(1)}, u32[]{:S(2)}, u32[]{:S(2)}) collective-permute-start(f32[208,128]{1,0:T(8,128)S(1)} %get-tuple-element.35.sent_odd), channel_id=1, source_target_pairs={{8,16},{24,32},{40,48},{56,64},{72,80},{88,96},{104,112},{120,128}... | collective-permute-start | bytes 319496 | tf_op jit(solution)/shard_map/ppermute | solution.py:560
  20.9 1.9 %collective-permute-start.2 = (f32[208,128]{1,0:T(8,128)S(1)}, f32[208,128]{1,0:T(8,128)S(1)}, u32[]{:S(2)}, u32[]{:S(2)}) collective-permute-start(f32[208,128]{1,0:T(8,128)S(1)} %get-tuple-element.36.sent_even), channel_id=1, source_target_pairs={{0,8},{16,24},{32,40},{48,56},{64,72},{80,88},{96,104},{112,120},{... | collective-permute-start | bytes 319496 | tf_op jit(solution)/shard_map/ppermute | solution.py:561
  22.8 1.9 %collective-permute-done.1.in_odd = f32[208,128]{1,0:T(8,128)S(1)} collective-permute-done((f32[208,128]{1,0:T(8,128)S(1)}, f32[208,128]{1,0:T(8,128)S(1)}, u32[]{:S(2)}, u32[]{:S(2)}) %collective-permute-start.1) | collective-permute-done | bytes 106528 | tf_op jit(solution)/shard_map/ppermute | solution.py:560
  24.8 3.1 %collective-permute-done.2.in_even = f32[208,128]{1,0:T(8,128)S(1)} collective-permute-done((f32[208,128]{1,0:T(8,128)S(1)}, f32[208,128]{1,0:T(8,128)S(1)}, u32[]{:S(2)}, u32[]{:S(2)}) %collective-permute-start.2) | collective-permute-done | bytes 106528 | tf_op jit(solution)/shard_map/ppermute | solution.py:561
  27.9 2.0 %shard_map.98 = (f32[512,128]{1,0:T(8,128)}, f32[512,128]{1,0:T(8,128)}) custom-call(f32[208,128]{1,0:T(8,128)S(1)} %collective-permute-done.1.in_odd, f32[208,128]{1,0:T(8,128)S(1)} %collective-permute-done.2.in_even, f32[208,128]{1,0:T(8,128)S(1)} %get-tuple-element.35.sent_odd, f32[208,128]{1,0:T(8,128)S(1)} %get-tuple-element.36.sent_even, ...), custom_call_target="tpu_custom_call" | custom-call | flops 10000000 | bytes 5550080 | tf_op jit(solution)/shard_map/pallas_call | solution.py:492
Async XLA Ops:
  3.0 11.0 %collective-permute-start = (f32[328,128]{1,0:T(8,128)S(1)}, f32[328,128]{1,0:T(8,128)S(1)}, u32[]{:S(2)}, u32[]{:S(2)}) collective-permute-start(f32[328,128]{1,0:T(8,128)S(1)} %get-tuple-element.25), channel_id=1, source_target_pairs={{1,2},{3,4},{5,6},{2,1},{4,3},{6,5},{9,10},{11,12},{13,14},{10,9},... | collective-permute-start | bytes 503816 | tf_op jit(solution)/shard_map/ppermute | solution.py:535
  14.5 10.2 %collective-permute-start.1 = (f32[208,128]{1,0:T(8,128)S(1)}, f32[208,128]{1,0:T(8,128)S(1)}, u32[]{:S(2)}, u32[]{:S(2)}) collective-permute-start(f32[208,128]{1,0:T(8,128)S(1)} %get-tuple-element.35.sent_odd), channel_id=1, source_target_pairs={{8,16},{24,32},{40,48},{56,64},{72,80},{88,96},{104,112},{120,128}... | collective-permute-start | bytes 319496 | tf_op jit(solution)/shard_map/ppermute | solution.py:560
  20.9 7.0 %collective-permute-start.2 = (f32[208,128]{1,0:T(8,128)S(1)}, f32[208,128]{1,0:T(8,128)S(1)}, u32[]{:S(2)}, u32[]{:S(2)}) collective-permute-start(f32[208,128]{1,0:T(8,128)S(1)} %get-tuple-element.36.sent_even), channel_id=1, source_target_pairs={{0,8},{16,24},{32,40},{48,56},{64,72},{80,88},{96,104},{112,120},{... | collective-permute-start | bytes 319496 | tf_op jit(solution)/shard_map/ppermute | solution.py:561

commit v5 on v4

--- a/solution.py
+++ b/solution.py
@@ -323,11 +323,13 @@
     def after(lo, n):
         return jnp.where(even, gathered[mate, lo : lo + n, :], odd[lo : lo + n, :])
 
+    wide_mate = jnp.where(wide_even, 1, 0)
+
     def left(lo, n):
-        return jnp.where(wide_even, in_odd[lo : lo + n, :], in_even[lo : lo + n, :])
+        return jnp.where(wide_even, in_odd[lo : lo + n, :], in_even[wide_mate, lo : lo + n, :])
 
     def right(lo, n):
-        return jnp.where(wide_even, in_even[lo : lo + n, :], in_odd[lo : lo + n, :])
+        return jnp.where(wide_even, in_even[wide_mate, lo : lo + n, :], in_odd[lo : lo + n, :])
 
     def first(lo, n):
         return jnp.where(wide_even, sent_odd[lo : lo + n, :], sent_even[lo : lo + n, :])
@@ -558,7 +560,9 @@
         [gathered, odd, p, perm, bs, p_middle, perm_middle, bs_middle, sat, small, acc],
     )
     in_odd = lax.ppermute(sent_odd, "wide", swaps(n_wide, 1))
-    in_even = lax.ppermute(sent_even, "wide", swaps(n_wide, 0))
+    in_even = lax.all_gather(
+        sent_even, "wide", axis_index_groups=[[i, i + 1] for i in range(0, n_wide, 2)]
+    )
     new, new_sat = call(
         final_kernel,
         [(cells, L), (cells, L)],

time: 30.1 us -> 28.9 us (0.960)
  the two profiles are of different devices: /device:TPU:176 before, /device:TPU:184 now
where the time goes in v5:
time: 28.9 us; the launch traced here: 28.7 us
  blocking collectives  13 us (45%)
  starting transfers between devices  8.28 us (29%)
  Pallas kernels  6.79 us (23%)
  between operations  0.66 us (2%)
    all_gather x1, blocking collectives, on_device(): lax.all_gather(out_even, 'narrow', axis_index_groups=[[i, i + 1] for i in...  7.17 us
    pallas_call x4, Pallas kernels, call(): pl.pallas_call(kernel, out_shape=shapes, in_specs=[HBM] * far + [VMEM] *...  6.79 us
    ppermute x1, starting transfers between devices, on_device(): in_odd = lax.ppermute(sent_odd, 'wide', swaps(n_wide, 1))  6.36 us
    all_gather x1, blocking collectives, on_device(): lax.all_gather(sent_even, 'wide', axis_index_groups=[[i, i + 1] for i in...  5.79 us
    ppermute x1, starting transfers between devices, on_device(): odd = lax.ppermute(out_odd, 'narrow', swaps(n_narrow, 1))  1.92 us
  transfers between devices with their start and end apart: 2, of which 0 were waited for; matrix products, arithmetic and copies ran while one was open for 0% of the time, Pallas kernels for 7%

profile of v5, /device:TPU:184, one launch (start us, length us, event | category | flops | bytes accessed | tf_op | source)
XLA Modules:
  0.0 28.7 jit_solution(2397327602107225476)
XLA Ops:
  0.6 2.3 %shard_map.95 = (f32[328,128]{1,0:T(8,128)S(1)}, f32[328,128]{1,0:T(8,128)S(1)}, f32[448,128]{1,0:T(8,128)S(1)}, f32[512,128]{1,0:T(8,128)S(1)}, f32[3,512,128]{...) custom-call(f32[512,128]{1,0:T(8,128)} %bitcast.21, ...), custom_call_target="tpu_custom_call" | custom-call | flops 10000000 | bytes 6096896 | tf_op jit(solution)/shard_map/pallas_call | solution.py:494
  3.0 1.9 %collective-permute-start = (f32[328,128]{1,0:T(8,128)S(1)}, f32[328,128]{1,0:T(8,128)S(1)}, u32[]{:S(2)}, u32[]{:S(2)}) collective-permute-start(f32[328,128]{1,0:T(8,128)S(1)} %get-tuple-element.25), channel_id=1, source_target_pairs={{1,2},{3,4},{5,6},{2,1},{4,3},{6,5},{9,10},{11,12},{13,14},{10,9},... | collective-permute-start | bytes 503816 | tf_op jit(solution)/shard_map/ppermute | solution.py:537
  4.9 1.9 %shard_map.96 = (f32[256,128]{1,0:T(8,128)S(1)}, f32[3,256,128]{2,1,0:T(8,128)S(1)}, f32[4,192,128]{2,1,0:T(8,128)S(1)}, f32[3,256,128]{2,1,0:T(8,128)S(1)}, f32...) custom-call(f32[512,128]{1,0:T(8,128)} %bitcast.22, ...), custom_call_target="tpu_custom_call" | custom-call | flops 10000000 | bytes 4898816 | tf_op jit(solution)/shard_map/pallas_call | solution.py:494
  6.8 7.2 %all-gather = f32[656,128]{1,0:T(8,128)S(1)} all-gather(f32[328,128]{1,0:T(8,128)S(1)} %get-tuple-element.24), channel_id=2, replica_groups={{0,1},{2,3},{4,5},{6,7},{8,9},{10,11},{12,13},{14,15},{16,17},{18,19},{..., dimensions={0}, use_global_device_ids=true | all-gather | bytes 503808 | tf_op jit(solution)/shard_map/all_gather | solution.py:538
  14.0 0.0 collective-permute-done.odd
  14.0 0.6 %shard_map.97 = (f32[208,128]{1,0:T(8,128)S(1)}, f32[208,128]{1,0:T(8,128)S(1)}, f32[448,128]{1,0:T(8,128)S(1)}) custom-call(f32[2,328,128]{2,1,0:T(8,128)S(1)} %bitcast.14, f32[328,128]{1,0:T(8,128)S(1)} %collective-permute-done.odd, f32[512,128]{1,0:T(8,128)S(1)} %get-tuple-element.26.p, f32[3,512,128]{2,1,0:T(8,128)S(1)} %get-tuple-element.27.perm, ...), custom_call_target="tpu_custom_call" | custom-call | flops 1000000 | bytes 4468736 | tf_op jit(solution)/shard_map/pallas_call | solution.py:494
  14.5 6.4 %collective-permute-start.1 = (f32[208,128]{1,0:T(8,128)S(1)}, f32[208,128]{1,0:T(8,128)S(1)}, u32[]{:S(2)}, u32[]{:S(2)}) collective-permute-start(f32[208,128]{1,0:T(8,128)S(1)} %get-tuple-element.35.sent_odd), channel_id=1, source_target_pairs={{8,16},{24,32},{40,48},{56,64},{72,80},{88,96},{104,112},{120,128}... | collective-permute-start | bytes 319496 | tf_op jit(solution)/shard_map/ppermute | solution.py:562
  20.9 5.8 %all-gather.1 = f32[416,128]{1,0:T(8,128)S(1)} all-gather(f32[208,128]{1,0:T(8,128)S(1)} %get-tuple-element.36.sent_even), channel_id=3, replica_groups={{0,8},{16,24},{32,40},{48,56},{64,72},{80,88},{96,104},{112,120},{128,1..., dimensions={0}, use_global_device_ids=true | all-gather | bytes 319488 | tf_op jit(solution)/shard_map/all_gather | solution.py:563
  26.7 0.0 collective-permute-done.1.in_odd
  26.7 2.0 %shard_map.98 = (f32[512,128]{1,0:T(8,128)}, f32[512,128]{1,0:T(8,128)}) custom-call(f32[208,128]{1,0:T(8,128)S(1)} %collective-permute-done.1.in_odd, f32[2,208,128]{2,1,0:T(8,128)S(1)} %bitcast.16, f32[208,128]{1,0:T(8,128)S(1)} %get-tuple-element.35.sent_odd, f32[208,128]{1,0:T(8,128)S(1)} %get-tuple-element.36.sent_even, f32[2,328,128]{2,1,0:T(8,128)S(1)} %bitcast.15, ...), custom_call_target="tpu_custom_call" | custom-call | flops 10000000 | bytes 5656576 | tf_op jit(solution)/shard_map/pallas_call | solution.py:494
Async XLA Ops:
  3.0 11.0 %collective-permute-start = (f32[328,128]{1,0:T(8,128)S(1)}, f32[328,128]{1,0:T(8,128)S(1)}, u32[]{:S(2)}, u32[]{:S(2)}) collective-permute-start(f32[328,128]{1,0:T(8,128)S(1)} %get-tuple-element.25), channel_id=1, source_target_pairs={{1,2},{3,4},{5,6},{2,1},{4,3},{6,5},{9,10},{11,12},{13,14},{10,9},... | collective-permute-start | bytes 503816 | tf_op jit(solution)/shard_map/ppermute | solution.py:537
  14.5 12.2 %collective-permute-start.1 = (f32[208,128]{1,0:T(8,128)S(1)}, f32[208,128]{1,0:T(8,128)S(1)}, u32[]{:S(2)}, u32[]{:S(2)}) collective-permute-start(f32[208,128]{1,0:T(8,128)S(1)} %get-tuple-element.35.sent_odd), channel_id=1, source_target_pairs={{8,16},{24,32},{40,48},{56,64},{72,80},{88,96},{104,112},{120,128}... | collective-permute-start | bytes 319496 | tf_op jit(solution)/shard_map/ppermute | solution.py:562

commit v6 on v5

--- a/solution.py
+++ b/solution.py
@@ -125,6 +125,7 @@
     return [flipped[k * TALL : (k + 1) * TALL, :] for k in range(K)]
 
 
+CHUNKS = (4, 9, 13, NX - 1)
 LOW, HIGH = EDGE, NX - EDGE
 
 
@@ -143,41 +144,39 @@
     even = lax.axis_index("narrow") % 2 == 0
     rows_even = pl.ds(pl.multiple_of(jnp.where(even, NX - 1, 0) * NY, NY), NY)
     rows_odd = pl.ds(pl.multiple_of(jnp.where(even, 0, NX - 1) * NY, NY), NY)
-    pairs = []
+    pairs = [(support_in, support), (matrix_in, matrix)]
     for near, first in ((0, 0), (HIGH - 1, HIGH)):
         part = pl.ds(near * NY, (EDGE + 1) * NY)
         own, fine = pl.ds(first * NY, EDGE * NY), pl.ds(first * NY * K, EDGE * NY * K)
         pairs += [(p_in.at[part], p.at[part]), (perm_in.at[:, part], perm.at[:, part])]
         pairs += [(src_in.at[own], src.at[own]), (basis_in.at[fine], basis.at[fine])]
-    pairs += [(support_in, support), (matrix_in, matrix)]
     pairs += [(sat_in.at[rows_even], out_even.at[pl.ds(N_S, NY)])]
     pairs += [(sat_in.at[rows_odd], out_odd.at[pl.ds(N_S, NY)])]
     copies = copies_of(sems, pairs)
-    pieces = jnp.zeros((NY, L), jnp.float32)
-    for i, first in enumerate((0, HIGH)):
-        for copy in copies[4 * i : 4 * i + 3]:
-            copy.wait()
-        residuals = rows_residual(p, perm, src, trans, first, first + EDGE, 0)
-        copies[4 * i + 3].wait()
-        fine = slice(first * NY * K, (first + EDGE) * NY * K)
-        mixed[fine, :] = basis[fine, :].astype(jnp.float32)
-        pieces = add_pieces(pieces, residuals, first, mixed, bs, 0)
-    pieces = split_pieces(square, pieces)
-    copies[8].wait()
-    copies[9].wait()
+    copies[0].wait()
+    copies[1].wait()
     place[...] = jnp.zeros((TALL, L), jnp.float32)
-    stack = []
     for i in range(K + 9):
         if i < MAT:
             value = support[pl.ds(i, NX, stride=K), :].astype(jnp.float32)
         else:
             value = matrix[(i - MAT) * NX : (i - MAT + 1) * NX, :]
         place[TOP : TOP + NX, 0:NY] = value
-        stack.append(roll(place[...], WEST, 1))
+        small[i * TALL : (i + 1) * TALL, :] = roll(place[...], WEST, 1)
+    pieces = jnp.zeros((NY, L), jnp.float32)
+    for i, first in enumerate((0, HIGH)):
+        for copy in copies[4 * i + 2 : 4 * i + 5]:
+            copy.wait()
+        residuals = rows_residual(p, perm, src, trans, first, first + EDGE, 0)
+        copies[4 * i + 5].wait()
+        fine = slice(first * NY * K, (first + EDGE) * NY * K)
+        mixed[fine, :] = basis[fine, :].astype(jnp.float32)
+        pieces = add_pieces(pieces, residuals, first, mixed, bs, 0)
+    pieces = split_pieces(square, pieces)
+    stack = [small[i * TALL : (i + 1) * TALL, :] for i in range(ACC)]
     acc = bin_pieces(stack[:K], pieces)
     stack.append(acc)
-    for i in range(SMALL):
-        small[i * TALL : (i + 1) * TALL, :] = stack[i]
+    small[ACC * TALL : SMALL * TALL, :] = acc
     for out, takes_last in ((out_even, even), (out_odd, jnp.logical_not(even))):
         edge = jnp.where(takes_last, NX - 1, 0)
         row = pl.multiple_of(edge * NY, NY)
@@ -444,6 +443,7 @@
         frac[pl.ds(0, NX, stride=NY), :],
     )
     end = rows == NY - 1
+    done = 0
     p_here, f_here = new[0:NY, :], frac[0:NY, :]
     flow_in = carried(
         trans_of(before(N_K, NY), perm[0, 0:NY, :]), ends[0], p_here, fraction(before(N_S, NY)), f_here
@@ -474,11 +474,12 @@
         total = total + (fz - roll(fz, 1, 1))
         new_sat[at, :] = sat[at, :] - rate[at, :] * total
         p_here, f_here = p_next, f_next
-        if x % 4 == 3:
-            part = pl.ds((x - 3) * NY, 4 * NY)
-            copy = pltpu.make_async_copy(new_sat.at[part], new_sat_out.at[part], sems.at[1 + x // 4])
+        if x in CHUNKS:
+            part = pl.ds(done * NY, (x + 1 - done) * NY)
+            copy = pltpu.make_async_copy(new_sat.at[part], new_sat_out.at[part], sems.at[len(copies)])
             copy.start()
             copies.append(copy)
+            done = x + 1
     for copy in copies:
         copy.wait()
 

time: 28.9 us -> 28.8 us (level)
  no operation moved by 1% of the time
where the time goes in v6:
time: 28.8 us; the launch traced here: 28.6 us
  blocking collectives  13 us (45%)
  starting transfers between devices  8.28 us (29%)
  Pallas kernels  6.71 us (23%)
  between operations  0.66 us (2%)
    all_gather x1, blocking collectives, on_device(): lax.all_gather(out_even, 'narrow', axis_index_groups=[[i, i + 1] for i in...  7.17 us
    pallas_call x4, Pallas kernels, call(): pl.pallas_call(kernel, out_shape=shapes, in_specs=[HBM] * far + [VMEM] *...  6.71 us
    ppermute x1, starting transfers between devices, on_device(): in_odd = lax.ppermute(sent_odd, 'wide', swaps(n_wide, 1))  6.36 us
    all_gather x1, blocking collectives, on_device(): lax.all_gather(sent_even, 'wide', axis_index_groups=[[i, i + 1] for i in...  5.79 us
    ppermute x1, starting transfers between devices, on_device(): odd = lax.ppermute(out_odd, 'narrow', swaps(n_narrow, 1))  1.92 us
  transfers between devices with their start and end apart: 2, of which 0 were waited for; matrix products, arithmetic and copies ran while one was open for 0% of the time, Pallas kernels for 7%

profile of v6, /device:TPU:184, one launch (start us, length us, event | category | flops | bytes accessed | tf_op | source)
XLA Modules:
  0.0 28.6 jit_solution(7668131290123294251)
XLA Ops:
  0.6 2.3 %shard_map.95 = (f32[328,128]{1,0:T(8,128)S(1)}, f32[328,128]{1,0:T(8,128)S(1)}, f32[448,128]{1,0:T(8,128)S(1)}, f32[512,128]{1,0:T(8,128)S(1)}, f32[3,512,128]{...) custom-call(f32[512,128]{1,0:T(8,128)} %bitcast.21, ...), custom_call_target="tpu_custom_call" | custom-call | flops 10000000 | bytes 6096896 | tf_op jit(solution)/shard_map/pallas_call | solution.py:495
  2.9 1.9 %collective-permute-start = (f32[328,128]{1,0:T(8,128)S(1)}, f32[328,128]{1,0:T(8,128)S(1)}, u32[]{:S(2)}, u32[]{:S(2)}) collective-permute-start(f32[328,128]{1,0:T(8,128)S(1)} %get-tuple-element.25), channel_id=1, source_target_pairs={{1,2},{3,4},{5,6},{2,1},{4,3},{6,5},{9,10},{11,12},{13,14},{10,9},... | collective-permute-start | bytes 503816 | tf_op jit(solution)/shard_map/ppermute | solution.py:538
  4.8 1.9 %shard_map.96 = (f32[256,128]{1,0:T(8,128)S(1)}, f32[3,256,128]{2,1,0:T(8,128)S(1)}, f32[4,192,128]{2,1,0:T(8,128)S(1)}, f32[3,256,128]{2,1,0:T(8,128)S(1)}, f32...) custom-call(f32[512,128]{1,0:T(8,128)} %bitcast.22, ...), custom_call_target="tpu_custom_call" | custom-call | flops 10000000 | bytes 4898816 | tf_op jit(solution)/shard_map/pallas_call | solution.py:495
  6.7 7.2 %all-gather = f32[656,128]{1,0:T(8,128)S(1)} all-gather(f32[328,128]{1,0:T(8,128)S(1)} %get-tuple-element.24), channel_id=2, replica_groups={{0,1},{2,3},{4,5},{6,7},{8,9},{10,11},{12,13},{14,15},{16,17},{18,19},{..., dimensions={0}, use_global_device_ids=true | all-gather | bytes 503808 | tf_op jit(solution)/shard_map/all_gather | solution.py:539
  13.9 0.0 collective-permute-done.odd
  13.9 0.6 %shard_map.97 = (f32[208,128]{1,0:T(8,128)S(1)}, f32[208,128]{1,0:T(8,128)S(1)}, f32[448,128]{1,0:T(8,128)S(1)}) custom-call(f32[2,328,128]{2,1,0:T(8,128)S(1)} %bitcast.14, f32[328,128]{1,0:T(8,128)S(1)} %collective-permute-done.odd, f32[512,128]{1,0:T(8,128)S(1)} %get-tuple-element.26.p, f32[3,512,128]{2,1,0:T(8,128)S(1)} %get-tuple-element.27.perm, ...), custom_call_target="tpu_custom_call" | custom-call | flops 1000000 | bytes 4468736 | tf_op jit(solution)/shard_map/pallas_call | solution.py:495
  14.5 6.4 %collective-permute-start.1 = (f32[208,128]{1,0:T(8,128)S(1)}, f32[208,128]{1,0:T(8,128)S(1)}, u32[]{:S(2)}, u32[]{:S(2)}) collective-permute-start(f32[208,128]{1,0:T(8,128)S(1)} %get-tuple-element.35.sent_odd), channel_id=1, source_target_pairs={{8,16},{24,32},{40,48},{56,64},{72,80},{88,96},{104,112},{120,128}... | collective-permute-start | bytes 319496 | tf_op jit(solution)/shard_map/ppermute | solution.py:563
  20.8 5.8 %all-gather.1 = f32[416,128]{1,0:T(8,128)S(1)} all-gather(f32[208,128]{1,0:T(8,128)S(1)} %get-tuple-element.36.sent_even), channel_id=3, replica_groups={{0,8},{16,24},{32,40},{48,56},{64,72},{80,88},{96,104},{112,120},{128,1..., dimensions={0}, use_global_device_ids=true | all-gather | bytes 319488 | tf_op jit(solution)/shard_map/all_gather | solution.py:564
  26.6 0.0 collective-permute-done.1.in_odd
  26.6 2.0 %shard_map.98 = (f32[512,128]{1,0:T(8,128)}, f32[512,128]{1,0:T(8,128)}) custom-call(f32[208,128]{1,0:T(8,128)S(1)} %collective-permute-done.1.in_odd, f32[2,208,128]{2,1,0:T(8,128)S(1)} %bitcast.16, f32[208,128]{1,0:T(8,128)S(1)} %get-tuple-element.35.sent_odd, f32[208,128]{1,0:T(8,128)S(1)} %get-tuple-element.36.sent_even, f32[2,328,128]{2,1,0:T(8,128)S(1)} %bitcast.15, ...), custom_call_target="tpu_custom_call" | custom-call | flops 10000000 | bytes 5656576 | tf_op jit(solution)/shard_map/pallas_call | solution.py:495
Async XLA Ops:
  2.9 11.0 %collective-permute-start = (f32[328,128]{1,0:T(8,128)S(1)}, f32[328,128]{1,0:T(8,128)S(1)}, u32[]{:S(2)}, u32[]{:S(2)}) collective-permute-start(f32[328,128]{1,0:T(8,128)S(1)} %get-tuple-element.25), channel_id=1, source_target_pairs={{1,2},{3,4},{5,6},{2,1},{4,3},{6,5},{9,10},{11,12},{13,14},{10,9},... | collective-permute-start | bytes 503816 | tf_op jit(solution)/shard_map/ppermute | solution.py:538
  14.5 12.2 %collective-permute-start.1 = (f32[208,128]{1,0:T(8,128)S(1)}, f32[208,128]{1,0:T(8,128)S(1)}, u32[]{:S(2)}, u32[]{:S(2)}) collective-permute-start(f32[208,128]{1,0:T(8,128)S(1)} %get-tuple-element.35.sent_odd), channel_id=1, source_target_pairs={{8,16},{24,32},{40,48},{56,64},{72,80},{88,96},{104,112},{120,128}... | collective-permute-start | bytes 319496 | tf_op jit(solution)/shard_map/ppermute | solution.py:563

commit v7 on v6

--- a/solution.py
+++ b/solution.py
@@ -213,22 +213,22 @@
     copies = copies_of(
         sems,
         [
-            (p_in.at[near], p), (perm_in.at[:, near], perm), (src_in.at[own], src.at[inner]),
-            (basis_in.at[fine], basis), (sat_in, sat), (pore_in, pore),
+            (sat_in, sat), (pore_in, pore), (p_in.at[near], p), (perm_in.at[:, near], perm),
+            (src_in.at[own], src.at[inner]), (basis_in.at[fine], basis),
         ],
     )
-    for copy in copies[:3]:
+    copies[0].wait()
+    frac[...] = fraction(sat[...])
+    copies[1].wait()
+    rate[...] = DT / pore[...]
+    for copy in copies[2:5]:
         copy.wait()
     residuals = rows_residual(p, perm, src, trans, LOW, HIGH, LOW - 1)
-    copies[3].wait()
+    copies[5].wait()
     mixed[...] = basis[...].astype(jnp.float32)
     pieces = add_pieces(jnp.zeros((NY, L), jnp.float32), residuals, LOW, mixed, bs, LOW)
     sup = [small[k * TALL : (k + 1) * TALL, :] for k in range(K)]
     acc[...] = bin_pieces(sup, split_pieces(square, pieces))
-    copies[4].wait()
-    frac[...] = fraction(sat[...])
-    copies[5].wait()
-    rate[...] = DT / pore[...]
 
 
 def narrow_kernel(

time: 28.8 us -> 28.8 us (level)
  no operation moved by 1% of the time
where the time goes in v7:
time: 28.8 us; the launch traced here: 28.6 us
  blocking collectives  12.9 us (45%)
  starting transfers between devices  8.28 us (29%)
  Pallas kernels  6.73 us (23%)
  between operations  0.66 us (2%)
    all_gather x1, blocking collectives, on_device(): lax.all_gather(out_even, 'narrow', axis_index_groups=[[i, i + 1] for i in...  7.17 us
    pallas_call x4, Pallas kernels, call(): pl.pallas_call(kernel, out_shape=shapes, in_specs=[HBM] * far + [VMEM] *...  6.73 us
    ppermute x1, starting transfers between devices, on_device(): in_odd = lax.ppermute(sent_odd, 'wide', swaps(n_wide, 1))  6.36 us
    all_gather x1, blocking collectives, on_device(): lax.all_gather(sent_even, 'wide', axis_index_groups=[[i, i + 1] for i in...  5.78 us
    ppermute x1, starting transfers between devices, on_device(): odd = lax.ppermute(out_odd, 'narrow', swaps(n_narrow, 1))  1.92 us
  transfers between devices with their start and end apart: 2, of which 0 were waited for; matrix products, arithmetic and copies ran while one was open for 0% of the time, Pallas kernels for 7%

profile of v7, /device:TPU:184, one launch (start us, length us, event | category | flops | bytes accessed | tf_op | source)
XLA Modules:
  0.0 28.6 jit_solution(18303153234934989979)
XLA Ops:
  0.6 2.3 %shard_map.95 = (f32[328,128]{1,0:T(8,128)S(1)}, f32[328,128]{1,0:T(8,128)S(1)}, f32[448,128]{1,0:T(8,128)S(1)}, f32[512,128]{1,0:T(8,128)S(1)}, f32[3,512,128]{...) custom-call(f32[512,128]{1,0:T(8,128)} %bitcast.21, ...), custom_call_target="tpu_custom_call" | custom-call | flops 10000000 | bytes 6096896 | tf_op jit(solution)/shard_map/pallas_call | solution.py:495
  2.9 1.9 %collective-permute-start = (f32[328,128]{1,0:T(8,128)S(1)}, f32[328,128]{1,0:T(8,128)S(1)}, u32[]{:S(2)}, u32[]{:S(2)}) collective-permute-start(f32[328,128]{1,0:T(8,128)S(1)} %get-tuple-element.25), channel_id=1, source_target_pairs={{1,2},{3,4},{5,6},{2,1},{4,3},{6,5},{9,10},{11,12},{13,14},{10,9},... | collective-permute-start | bytes 503816 | tf_op jit(solution)/shard_map/ppermute | solution.py:538
  4.8 1.9 %shard_map.96 = (f32[256,128]{1,0:T(8,128)S(1)}, f32[3,256,128]{2,1,0:T(8,128)S(1)}, f32[4,192,128]{2,1,0:T(8,128)S(1)}, f32[3,256,128]{2,1,0:T(8,128)S(1)}, f32...) custom-call(f32[512,128]{1,0:T(8,128)} %bitcast.22, ...), custom_call_target="tpu_custom_call" | custom-call | flops 10000000 | bytes 4898816 | tf_op jit(solution)/shard_map/pallas_call | solution.py:495
  6.7 7.2 %all-gather = f32[656,128]{1,0:T(8,128)S(1)} all-gather(f32[328,128]{1,0:T(8,128)S(1)} %get-tuple-element.24), channel_id=2, replica_groups={{0,1},{2,3},{4,5},{6,7},{8,9},{10,11},{12,13},{14,15},{16,17},{18,19},{..., dimensions={0}, use_global_device_ids=true | all-gather | bytes 503808 | tf_op jit(solution)/shard_map/all_gather | solution.py:539
  13.9 0.0 collective-permute-done.odd
  13.9 0.6 %shard_map.97 = (f32[208,128]{1,0:T(8,128)S(1)}, f32[208,128]{1,0:T(8,128)S(1)}, f32[448,128]{1,0:T(8,128)S(1)}) custom-call(f32[2,328,128]{2,1,0:T(8,128)S(1)} %bitcast.14, f32[328,128]{1,0:T(8,128)S(1)} %collective-permute-done.odd, f32[512,128]{1,0:T(8,128)S(1)} %get-tuple-element.26.p, f32[3,512,128]{2,1,0:T(8,128)S(1)} %get-tuple-element.27.perm, ...), custom_call_target="tpu_custom_call" | custom-call | flops 1000000 | bytes 4468736 | tf_op jit(solution)/shard_map/pallas_call | solution.py:495
  14.5 6.4 %collective-permute-start.1 = (f32[208,128]{1,0:T(8,128)S(1)}, f32[208,128]{1,0:T(8,128)S(1)}, u32[]{:S(2)}, u32[]{:S(2)}) collective-permute-start(f32[208,128]{1,0:T(8,128)S(1)} %get-tuple-element.35.sent_odd), channel_id=1, source_target_pairs={{8,16},{24,32},{40,48},{56,64},{72,80},{88,96},{104,112},{120,128}... | collective-permute-start | bytes 319496 | tf_op jit(solution)/shard_map/ppermute | solution.py:563
  20.8 5.8 %all-gather.1 = f32[416,128]{1,0:T(8,128)S(1)} all-gather(f32[208,128]{1,0:T(8,128)S(1)} %get-tuple-element.36.sent_even), channel_id=3, replica_groups={{0,8},{16,24},{32,40},{48,56},{64,72},{80,88},{96,104},{112,120},{128,1..., dimensions={0}, use_global_device_ids=true | all-gather | bytes 319488 | tf_op jit(solution)/shard_map/all_gather | solution.py:564
  26.6 0.0 collective-permute-done.1.in_odd
  26.6 2.0 %shard_map.98 = (f32[512,128]{1,0:T(8,128)}, f32[512,128]{1,0:T(8,128)}) custom-call(f32[208,128]{1,0:T(8,128)S(1)} %collective-permute-done.1.in_odd, f32[2,208,128]{2,1,0:T(8,128)S(1)} %bitcast.16, f32[208,128]{1,0:T(8,128)S(1)} %get-tuple-element.35.sent_odd, f32[208,128]{1,0:T(8,128)S(1)} %get-tuple-element.36.sent_even, f32[2,328,128]{2,1,0:T(8,128)S(1)} %bitcast.15, ...), custom_call_target="tpu_custom_call" | custom-call | flops 10000000 | bytes 5656576 | tf_op jit(solution)/shard_map/pallas_call | solution.py:495
Async XLA Ops:
  2.9 11.0 %collective-permute-start = (f32[328,128]{1,0:T(8,128)S(1)}, f32[328,128]{1,0:T(8,128)S(1)}, u32[]{:S(2)}, u32[]{:S(2)}) collective-permute-start(f32[328,128]{1,0:T(8,128)S(1)} %get-tuple-element.25), channel_id=1, source_target_pairs={{1,2},{3,4},{5,6},{2,1},{4,3},{6,5},{9,10},{11,12},{13,14},{10,9},... | collective-permute-start | bytes 503816 | tf_op jit(solution)/shard_map/ppermute | solution.py:538
  14.5 12.1 %collective-permute-start.1 = (f32[208,128]{1,0:T(8,128)S(1)}, f32[208,128]{1,0:T(8,128)S(1)}, u32[]{:S(2)}, u32[]{:S(2)}) collective-permute-start(f32[208,128]{1,0:T(8,128)S(1)} %get-tuple-element.35.sent_odd), channel_id=1, source_target_pairs={{8,16},{24,32},{40,48},{56,64},{72,80},{88,96},{104,112},{120,128}... | collective-permute-start | bytes 319496 | tf_op jit(solution)/shard_map/ppermute | solution.py:563
